TPU v7x, 128 devices: a whole 4x4x4 slice. The times are simulated.
128 devices in a mesh: blk: 8 (over z, y_lo), grp: 16 (over y_hi, x, core).
Axes of the slice: x: 4, y: 4 (y_hi: 2, y_lo: 2; y = y_hi * 2 + y_lo), z: 4, core: 2. Of those that a mesh axis runs over, the one named last changes fastest.
Arguments:
- student: bfloat16 [16384, 1024], P(('blk', 'grp')), may hold values from -6 to 6
- teacher: bfloat16 [16384, 4096], P(('blk', 'grp')), may hold values from -6 to 6
Outputs:
- student_grad: float32 [16384, 1024], P(('blk', 'grp'))
All inputs are finite; a program needn't handle non-finite values.
Results may differ from a plain program's by a relative error of at most 0.0085.
Values may be sent and summed in bfloat16 or wider, within the bound.
No kernel may reach another device: no remote copies, remote signals or barrier semaphores. Data moves between devices by JAX's collectives and lax.ppermute only.
A program may use at most 192 MiB of HBM per device.

v0:
```python
import math

import jax
import jax.numpy as jnp
from jax import lax
from jax.sharding import PartitionSpec as P


def shifted(block, axis, distance):
    devices = range(lax.axis_size(axis))
    route = [((i - distance) % len(devices), i) for i in devices]
    return lax.ppermute(block, axis, route)


def unit_rows(values):
    wide = values.astype(jnp.float32)
    recip = 1.0 / jnp.sqrt(jnp.sum(wide * wide, axis=1, keepdims=True) + 1e-06)
    return (wide * recip, recip)


def residual_tile(block_s, block_t, visit_s, visit_t):
    scale_s = math.sqrt(block_s.shape[1])
    scale_t = math.sqrt(block_t.shape[1])
    gram_s = lax.dot_general(
        block_s, visit_s, (((1,), (1,)), ((), ())), preferred_element_type=jnp.float32
    )
    gram_t = lax.dot_general(
        block_t, visit_t, (((1,), (1,)), ((), ())), preferred_element_type=jnp.float32
    )
    squash_s = jnp.tanh(scale_s * gram_s)
    squash_t = jnp.tanh(scale_t * gram_t)
    return ((squash_s - squash_t) * scale_s * (1.0 - squash_s * squash_s)).astype(jnp.bfloat16)


def local(student, teacher):
    unit_f, recip = unit_rows(student)
    unit_s = unit_f.astype(jnp.bfloat16)
    teach_f, teach_r = unit_rows(teacher)
    unit_t = teach_f.astype(jnp.bfloat16)
    block_s, block_t = (
        lax.all_gather(unit_s, "grp", axis=0, tiled=True),
        lax.all_gather(unit_t, "grp", axis=0, tiled=True),
    )
    loop_len = lax.axis_size("blk")
    total = block_s.shape[0] * loop_len
    coef = 4.0 * unit_s.shape[1] / math.sqrt(total)
    accum = jnp.zeros((block_s.shape[0], unit_s.shape[1]), jnp.float32)
    visit_s, visit_t = (unit_s, unit_t)
    for step in range(loop_len):
        if step > 0:
            visit_s, visit_t = shifted((visit_s, visit_t), "blk", 1)
        resid = residual_tile(block_s, block_t, visit_s, visit_t)
        accum = accum + jnp.dot(resid, visit_s, preferred_element_type=jnp.float32)
    summed = lax.psum_scatter(accum, "grp", scatter_dimension=0, tiled=True)
    dunit = coef * summed
    inner = jnp.sum(dunit * unit_f, axis=1, keepdims=True)
    return recip * (dunit - inner * unit_f)


def solution(mesh):
    in_specs = (P(("blk", "grp"), None), P(("blk", "grp"), None))
    out_specs = P(("blk", "grp"), None)
    return jax.shard_map(local, mesh=mesh, in_specs=in_specs, out_specs=out_specs, check_vma=False)
```

profile of v0, /device:TPU:0, one launch (start us, length us, event | category | flops | bytes accessed | tf_op | source)
XLA Modules:
  0.0 539.5 jit_solution(13660138975250337897)
XLA Ops:
  6.5 0.0 all-gather.3.cloned.1.call-start
  6.5 1.1 fusion.79
  7.6 1.8 fusion.75
  9.4 0.0 all-gather.3.cloned.1.call-update
  9.4 0.0 all-gather.5.cloned.1.call-start
  9.5 1.5 fusion.55
  11.0 2.5 fusion.56
  13.5 0.0 all-gather.5.cloned.1.call-update
  13.5 0.0 reduce-scatter.2.cloned.1.call-start
  13.6 1.7 collective-permute-start.1
  15.3 29.7 %collective-permute-done.1 = bf16[128,4096]{1,0:T(8,128)(2,1)S(1)} collective-permute-done((bf16[128,4096]{1,0:T(8,128)(2,1)}, bf16[128,4096]{1,0:T(8,128)(2,1)S(1)}, u32[]{:S(2)}, u32[]{:S(2)}) %collective-permute-start.1) | collective-permute-done | bytes 1048608 | tf_op jit(solution)/shard_map/ppermute | solution.py:12
  45.0 0.0 collective-permute-start.3
  45.0 37.7 %collective-permute-done.3 = bf16[128,4096]{1,0:T(8,128)(2,1)S(1)} collective-permute-done((bf16[128,4096]{1,0:T(8,128)(2,1)S(1)}, bf16[128,4096]{1,0:T(8,128)(2,1)S(1)}, u32[]{:S(2)}, u32[]{:S(2)}) %collective-permute-start.3) | collective-permute-done | bytes 1048608 | tf_op jit(solution)/shard_map/ppermute | solution.py:12
  82.6 0.0 collective-permute-start.5
  82.6 37.8 %collective-permute-done.5 = bf16[128,4096]{1,0:T(8,128)(2,1)S(1)} collective-permute-done((bf16[128,4096]{1,0:T(8,128)(2,1)S(1)}, bf16[128,4096]{1,0:T(8,128)(2,1)S(1)}, u32[]{:S(2)}, u32[]{:S(2)}) %collective-permute-start.5) | collective-permute-done | bytes 1048608 | tf_op jit(solution)/shard_map/ppermute | solution.py:12
  120.5 0.0 collective-permute-start.7
  120.5 31.3 %collective-permute-done.7 = bf16[128,4096]{1,0:T(8,128)(2,1)S(1)} collective-permute-done((bf16[128,4096]{1,0:T(8,128)(2,1)S(1)}, bf16[128,4096]{1,0:T(8,128)(2,1)S(1)}, u32[]{:S(2)}, u32[]{:S(2)}) %collective-permute-start.7) | collective-permute-done | bytes 1048608 | tf_op jit(solution)/shard_map/ppermute | solution.py:12
  151.7 0.0 collective-permute-start.9
  151.7 0.0 collective-permute-start
  151.7 60.0 %collective-permute-done = bf16[128,1024]{1,0:T(8,128)(2,1)S(1)} collective-permute-done((bf16[128,1024]{1,0:T(8,128)(2,1)}, bf16[128,1024]{1,0:T(8,128)(2,1)S(1)}, u32[]{:S(2)}, u32[]{:S(2)}) %collective-permute-start) | collective-permute-done | bytes 262176 | tf_op jit(solution)/shard_map/ppermute | solution.py:12
  211.8 0.0 collective-permute-start.2
  211.8 12.5 %collective-permute-done.2 = bf16[128,1024]{1,0:T(8,128)(2,1)S(1)} collective-permute-done((bf16[128,1024]{1,0:T(8,128)(2,1)S(1)}, bf16[128,1024]{1,0:T(8,128)(2,1)S(1)}, u32[]{:S(2)}, u32[]{:S(2)}) %collective-permute-start.2) | collective-permute-done | bytes 262176 | tf_op jit(solution)/shard_map/ppermute | solution.py:12
  224.3 0.0 collective-permute-start.4
  224.3 0.0 collective-permute-done.9
  224.3 0.1 collective-permute-start.11
  224.4 11.3 %collective-permute-done.4 = bf16[128,1024]{1,0:T(8,128)(2,1)S(1)} collective-permute-done((bf16[128,1024]{1,0:T(8,128)(2,1)S(1)}, bf16[128,1024]{1,0:T(8,128)(2,1)S(1)}, u32[]{:S(2)}, u32[]{:S(2)}) %collective-permute-start.4) | collective-permute-done | bytes 262176 | tf_op jit(solution)/shard_map/ppermute | solution.py:12
  235.6 0.0 collective-permute-start.6
  235.6 21.9 %collective-permute-done.6 = bf16[128,1024]{1,0:T(8,128)(2,1)S(1)} collective-permute-done((bf16[128,1024]{1,0:T(8,128)(2,1)S(1)}, bf16[128,1024]{1,0:T(8,128)(2,1)S(1)}, u32[]{:S(2)}, u32[]{:S(2)}) %collective-permute-start.6) | collective-permute-done | bytes 262176 | tf_op jit(solution)/shard_map/ppermute | solution.py:12
  257.6 0.0 collective-permute-start.8
  257.6 9.3 %collective-permute-done.8 = bf16[128,1024]{1,0:T(8,128)(2,1)S(1)} collective-permute-done((bf16[128,1024]{1,0:T(8,128)(2,1)S(1)}, bf16[128,1024]{1,0:T(8,128)(2,1)S(1)}, u32[]{:S(2)}, u32[]{:S(2)}) %collective-permute-start.8) | collective-permute-done | bytes 262176 | tf_op jit(solution)/shard_map/ppermute | solution.py:12
  266.9 0.0 collective-permute-start.10
  266.9 11.4 %collective-permute-done.10 = bf16[128,1024]{1,0:T(8,128)(2,1)S(1)} collective-permute-done((bf16[128,1024]{1,0:T(8,128)(2,1)S(1)}, bf16[128,1024]{1,0:T(8,128)(2,1)S(1)}, u32[]{:S(2)}, u32[]{:S(2)}) %collective-permute-start.10) | collective-permute-done | bytes 262176 | tf_op jit(solution)/shard_map/ppermute | solution.py:12
  278.2 0.0 collective-permute-start.12
  278.3 0.0 collective-permute-done.11
  278.3 0.0 copy-done.12
  278.3 0.0 copy-done.13
  278.3 0.0 copy-done.14
  278.3 0.6 collective-permute-start.13
  278.9 0.0 all-gather.3.cloned.1.call-done
  278.9 4.6 fusion.1
  283.6 4.4 fusion.2
  288.0 0.0 copy-done
  288.0 2.3 fusion.3
  290.3 2.3 fusion.4
  292.6 1.3 fusion.5
  293.9 2.3 fusion.6
  296.2 0.0 copy-done.2
  296.2 1.3 fusion.7
  297.5 0.0 collective-permute-done.12
  297.5 2.2 fusion
  299.7 0.0 all-gather.5.cloned.1.call-done
  299.8 13.6 %fusion.50 = f32[2048,1024]{1,0:T(8,128)} fusion(bf16[128,1024]{1,0:T(8,128)(2,1)} %copy-done.9, f32[2048,128]{1,0:T(8,128)} %fusion.1, bf16[2048,4096]{1,0:T(8,128)(2,1)} %all-gather.5.cloned.1.call-done, bf16[128,4096]{1,0:T(8,128)(2,1)} %collective-permute-done.11), kind=kOutput, calls=%fused_computation.69 | convolution fusion | flops 2686189568 | bytes 27525120 | tf_op jit(solution)/shard_map/dot_general | solution.py:53
  313.3 13.5 %fusion.45 = f32[2048,1024]{1,0:T(8,128)} fusion(bf16[128,1024]{1,0:T(8,128)(2,1)} %copy-done.8, f32[2048,128]{1,0:T(8,128)} %fusion.2, bf16[2048,4096]{1,0:T(8,128)(2,1)} %all-gather.5.cloned.1.call-done, bf16[128,4096]{1,0:T(8,128)(2,1)} %copy-done.14), kind=kOutput, calls=%fused_computation.64 | convolution fusion | flops 2686189568 | bytes 27525120 | tf_op jit(solution)/shard_map/dot_general | solution.py:53
  326.8 13.4 %fusion.40 = f32[2048,1024]{1,0:T(8,128)} fusion(bf16[128,1024]{1,0:T(8,128)(2,1)} %copy-done.7, f32[2048,128]{1,0:T(8,128)} %fusion.3, bf16[2048,4096]{1,0:T(8,128)(2,1)} %all-gather.5.cloned.1.call-done, bf16[128,4096]{1,0:T(8,128)(2,1)} %copy-done.13), kind=kOutput, calls=%fused_computation.59 | convolution fusion | flops 2686189568 | bytes 27525120 | tf_op jit(solution)/shard_map/dot_general | solution.py:53
  340.3 13.6 %fusion.35 = f32[2048,1024]{1,0:T(8,128)} fusion(bf16[128,1024]{1,0:T(8,128)(2,1)} %copy-done.6, f32[2048,128]{1,0:T(8,128)} %fusion.4, bf16[2048,4096]{1,0:T(8,128)(2,1)} %all-gather.5.cloned.1.call-done, bf16[128,4096]{1,0:T(8,128)(2,1)} %copy-done.12), kind=kOutput, calls=%fused_computation.54 | convolution fusion | flops 2686189568 | bytes 27525120 | tf_op jit(solution)/shard_map/dot_general | solution.py:53
  353.9 13.3 %fusion.30 = f32[2048,1024]{1,0:T(8,128)} fusion(bf16[128,1024]{1,0:T(8,128)(2,1)} %copy-done.5, f32[2048,128]{1,0:T(8,128)S(1)} %fusion.5, bf16[2048,4096]{1,0:T(8,128)(2,1)} %all-gather.5.cloned.1.call-done, bf16[128,4096]{1,0:T(8,128)(2,1)} %copy-done.11), kind=kOutput, calls=%fused_computation.49 | convolution fusion | flops 2686189568 | bytes 27525120 | tf_op jit(solution)/shard_map/dot_general | solution.py:53
  367.1 13.5 %fusion.25 = f32[2048,1024]{1,0:T(8,128)} fusion(bf16[128,1024]{1,0:T(8,128)(2,1)} %copy-done.4, f32[2048,128]{1,0:T(8,128)} %fusion.6, bf16[2048,4096]{1,0:T(8,128)(2,1)} %all-gather.5.cloned.1.call-done, bf16[128,4096]{1,0:T(8,128)(2,1)} %copy-done.10), kind=kOutput, calls=%fused_computation.44 | convolution fusion | flops 2686189568 | bytes 27525120 | tf_op jit(solution)/shard_map/dot_general | solution.py:53
  380.6 13.2 %fusion.20 = f32[2048,1024]{1,0:T(8,128)} fusion(bf16[128,1024]{1,0:T(8,128)(2,1)S(1)} %copy-done.2, f32[2048,128]{1,0:T(8,128)S(1)} %fusion.7, bf16[2048,4096]{1,0:T(8,128)(2,1)} %all-gather.5.cloned.1.call-done, bf16[128,4096]{1,0:T(8,128)(2,1)S(1)} %copy-done.1), kind=kOutput, calls=%fused_computation.39 | convolution fusion | flops 2686189568 | bytes 27525120 | tf_op jit(solution)/shard_map/dot_general | solution.py:53
  393.9 0.0 collective-permute-done.13
  393.9 30.0 %add_add_fusion = f32[2048,1024]{1,0:T(8,128)} fusion(f32[2048,1024]{1,0:T(8,128)} %fusion.50, f32[2048,1024]{1,0:T(8,128)} %fusion.45, f32[2048,1024]{1,0:T(8,128)} %fusion.40, f32[2048,1024]{1,0:T(8,128)} %fusion.35, f32[2048,1024]{1,0:T(8,128)} %fusion.30, f32[2048,1024]{1,0:T(8,128)} %fusion.20, f32[2048,1024]{1,0:T(8,128)} %fusion.25, ...), kind=kOutput, calls=%fused_computation | convolution fusion | flops 2700869632 | bytes 86245376 | tf_op jit(solution)/shard_map/dot_general | solution.py:53
  423.9 0.0 reduce-scatter.2.cloned.1.call-update
  423.9 105.4 %reduce-scatter.2.cloned.1.call-done = f32[128,1024]{1,0:T(8,128)} async-done(((f32[2048,1024]{1,0:T(8,128)}), f32[128,1024]{1,0:T(8,128)}) %reduce-scatter.2.cloned.1.call-update) | async-done | bytes 524304 | tf_op jit(solution)/shard_map/reduce_scatter | solution.py:54
  529.3 1.3 fusion.76
  530.6 2.1 fusion.78
  (27 shorter events, 0.1 us)
Async XLA Ops:
  6.5 272.4 %all-gather.3.cloned.1.call-start = ((), (), s32[]{:S(2)}) async-start(), calls=%async_computation.1 | async-start | bytes 4456448 | tf_op jit(solution)/shard_map/all_gather | solution.py:41
  9.4 290.3 %all-gather.5.cloned.1.call-start = ((), (), s32[]{:S(2)}) async-start(), calls=%async_computation.2 | async-start | bytes 17825792 | tf_op jit(solution)/shard_map/all_gather | solution.py:42
  13.5 515.8 %reduce-scatter.2.cloned.1.call-start = ((), (), s32[]{:S(2)}) async-start(), calls=%async_computation.3 | async-start | bytes 8912896 | tf_op jit(solution)/shard_map/reduce_scatter | solution.py:54
  13.6 31.4 %collective-permute-start.1 = (bf16[128,4096]{1,0:T(8,128)(2,1)}, bf16[128,4096]{1,0:T(8,128)(2,1)S(1)}, u32[]{:S(2)}, u32[]{:S(2)}) collective-permute-start(bf16[128,4096]{1,0:T(8,128)(2,1)} %fusion.56), channel_id=1, source_target_pairs={{112,0},{0,16},{16,32},{32,48},{48,64},{64,80},{80,96},{96,112},{1... | collective-permute-start | bytes 3145736 | tf_op jit(solution)/shard_map/ppermute | solution.py:12
  44.9 233.3 %copy-start.10 = (bf16[128,4096]{1,0:T(8,128)(2,1)}, bf16[128,4096]{1,0:T(8,128)(2,1)S(1)}, u32[]{:S(2)}) copy-start(bf16[128,4096]{1,0:T(8,128)(2,1)S(1)} %collective-permute-done.1) | copy-start | bytes 3145732
  45.0 37.7 %collective-permute-start.3 = (bf16[128,4096]{1,0:T(8,128)(2,1)S(1)}, bf16[128,4096]{1,0:T(8,128)(2,1)S(1)}, u32[]{:S(2)}, u32[]{:S(2)}) collective-permute-start(bf16[128,4096]{1,0:T(8,128)(2,1)S(1)} %collective-permute-done.1), channel_id=1, source_target_pairs={{112,0},{0,16},{16,32},{32,48},{48,64},{64,80},{80,96},{96,112},{1... | collective-permute-start | bytes 3145736 | tf_op jit(solution)/shard_map/ppermute | solution.py:12
  82.6 195.6 %copy-start.11 = (bf16[128,4096]{1,0:T(8,128)(2,1)}, bf16[128,4096]{1,0:T(8,128)(2,1)S(1)}, u32[]{:S(2)}) copy-start(bf16[128,4096]{1,0:T(8,128)(2,1)S(1)} %collective-permute-done.3) | copy-start | bytes 3145732
  82.6 37.8 %collective-permute-start.5 = (bf16[128,4096]{1,0:T(8,128)(2,1)S(1)}, bf16[128,4096]{1,0:T(8,128)(2,1)S(1)}, u32[]{:S(2)}, u32[]{:S(2)}) collective-permute-start(bf16[128,4096]{1,0:T(8,128)(2,1)S(1)} %collective-permute-done.3), channel_id=1, source_target_pairs={{112,0},{0,16},{16,32},{32,48},{48,64},{64,80},{80,96},{96,112},{1... | collective-permute-start | bytes 3145736 | tf_op jit(solution)/shard_map/ppermute | solution.py:12
  120.5 157.8 %copy-start.12 = (bf16[128,4096]{1,0:T(8,128)(2,1)}, bf16[128,4096]{1,0:T(8,128)(2,1)S(1)}, u32[]{:S(2)}) copy-start(bf16[128,4096]{1,0:T(8,128)(2,1)S(1)} %collective-permute-done.5) | copy-start | bytes 3145732
  120.5 31.3 %collective-permute-start.7 = (bf16[128,4096]{1,0:T(8,128)(2,1)S(1)}, bf16[128,4096]{1,0:T(8,128)(2,1)S(1)}, u32[]{:S(2)}, u32[]{:S(2)}) collective-permute-start(bf16[128,4096]{1,0:T(8,128)(2,1)S(1)} %collective-permute-done.5), channel_id=1, source_target_pairs={{112,0},{0,16},{16,32},{32,48},{48,64},{64,80},{80,96},{96,112},{1... | collective-permute-start | bytes 3145736 | tf_op jit(solution)/shard_map/ppermute | solution.py:12
  151.7 126.5 %copy-start.13 = (bf16[128,4096]{1,0:T(8,128)(2,1)}, bf16[128,4096]{1,0:T(8,128)(2,1)S(1)}, u32[]{:S(2)}) copy-start(bf16[128,4096]{1,0:T(8,128)(2,1)S(1)} %collective-permute-done.7) | copy-start | bytes 3145732
  151.7 72.6 %collective-permute-start.9 = (bf16[128,4096]{1,0:T(8,128)(2,1)S(1)}, bf16[128,4096]{1,0:T(8,128)(2,1)S(1)}, u32[]{:S(2)}, u32[]{:S(2)}) collective-permute-start(bf16[128,4096]{1,0:T(8,128)(2,1)S(1)} %collective-permute-done.7), channel_id=1, source_target_pairs={{112,0},{0,16},{16,32},{32,48},{48,64},{64,80},{80,96},{96,112},{1... | collective-permute-start | bytes 3145736 | tf_op jit(solution)/shard_map/ppermute | solution.py:12
  151.7 60.0 %collective-permute-start = (bf16[128,1024]{1,0:T(8,128)(2,1)}, bf16[128,1024]{1,0:T(8,128)(2,1)S(1)}, u32[]{:S(2)}, u32[]{:S(2)}) collective-permute-start(bf16[128,1024]{1,0:T(8,128)(2,1)} %fusion.75), channel_id=1, source_target_pairs={{112,0},{0,16},{16,32},{32,48},{48,64},{64,80},{80,96},{96,112},{1... | collective-permute-start | bytes 786440 | tf_op jit(solution)/shard_map/ppermute | solution.py:12
  211.8 82.1 %copy-start.4 = (bf16[128,1024]{1,0:T(8,128)(2,1)}, bf16[128,1024]{1,0:T(8,128)(2,1)S(1)}, u32[]{:S(2)}) copy-start(bf16[128,1024]{1,0:T(8,128)(2,1)S(1)} %collective-permute-done) | copy-start | bytes 786436
  211.8 12.5 %collective-permute-start.2 = (bf16[128,1024]{1,0:T(8,128)(2,1)S(1)}, bf16[128,1024]{1,0:T(8,128)(2,1)S(1)}, u32[]{:S(2)}, u32[]{:S(2)}) collective-permute-start(bf16[128,1024]{1,0:T(8,128)(2,1)S(1)} %collective-permute-done), channel_id=1, source_target_pairs={{112,0},{0,16},{16,32},{32,48},{48,64},{64,80},{80,96},{96,112},{1... | collective-permute-start | bytes 786440 | tf_op jit(solution)/shard_map/ppermute | solution.py:12
  224.3 68.3 %copy-start.5 = (bf16[128,1024]{1,0:T(8,128)(2,1)}, bf16[128,1024]{1,0:T(8,128)(2,1)S(1)}, u32[]{:S(2)}) copy-start(bf16[128,1024]{1,0:T(8,128)(2,1)S(1)} %collective-permute-done.2) | copy-start | bytes 786436
  224.3 11.4 %collective-permute-start.4 = (bf16[128,1024]{1,0:T(8,128)(2,1)S(1)}, bf16[128,1024]{1,0:T(8,128)(2,1)S(1)}, u32[]{:S(2)}, u32[]{:S(2)}) collective-permute-start(bf16[128,1024]{1,0:T(8,128)(2,1)S(1)} %collective-permute-done.2), channel_id=1, source_target_pairs={{112,0},{0,16},{16,32},{32,48},{48,64},{64,80},{80,96},{96,112},{1... | collective-permute-start | bytes 786440 | tf_op jit(solution)/shard_map/ppermute | solution.py:12
  224.3 54.0 %copy-start.14 = (bf16[128,4096]{1,0:T(8,128)(2,1)}, bf16[128,4096]{1,0:T(8,128)(2,1)S(1)}, u32[]{:S(2)}) copy-start(bf16[128,4096]{1,0:T(8,128)(2,1)S(1)} %collective-permute-done.9) | copy-start | bytes 3145732
  224.3 54.0 %collective-permute-start.11 = (bf16[128,4096]{1,0:T(8,128)(2,1)S(1)}, bf16[128,4096]{1,0:T(8,128)(2,1)}, u32[]{:S(2)}, u32[]{:S(2)}) collective-permute-start(bf16[128,4096]{1,0:T(8,128)(2,1)S(1)} %collective-permute-done.9), channel_id=1, source_target_pairs={{112,0},{0,16},{16,32},{32,48},{48,64},{64,80},{80,96},{96,112},{1... | collective-permute-start | bytes 3145736 | tf_op jit(solution)/shard_map/ppermute | solution.py:12
  235.6 54.6 %copy-start.6 = (bf16[128,1024]{1,0:T(8,128)(2,1)}, bf16[128,1024]{1,0:T(8,128)(2,1)S(1)}, u32[]{:S(2)}) copy-start(bf16[128,1024]{1,0:T(8,128)(2,1)S(1)} %collective-permute-done.4) | copy-start | bytes 786436
  235.6 22.0 %collective-permute-start.6 = (bf16[128,1024]{1,0:T(8,128)(2,1)S(1)}, bf16[128,1024]{1,0:T(8,128)(2,1)S(1)}, u32[]{:S(2)}, u32[]{:S(2)}) collective-permute-start(bf16[128,1024]{1,0:T(8,128)(2,1)S(1)} %collective-permute-done.4), channel_id=1, source_target_pairs={{112,0},{0,16},{16,32},{32,48},{48,64},{64,80},{80,96},{96,112},{1... | collective-permute-start | bytes 786440 | tf_op jit(solution)/shard_map/ppermute | solution.py:12
  257.6 32.7 %copy-start.7 = (bf16[128,1024]{1,0:T(8,128)(2,1)}, bf16[128,1024]{1,0:T(8,128)(2,1)S(1)}, u32[]{:S(2)}) copy-start(bf16[128,1024]{1,0:T(8,128)(2,1)S(1)} %collective-permute-done.6) | copy-start | bytes 786436
  257.6 9.3 %collective-permute-start.8 = (bf16[128,1024]{1,0:T(8,128)(2,1)S(1)}, bf16[128,1024]{1,0:T(8,128)(2,1)S(1)}, u32[]{:S(2)}, u32[]{:S(2)}) collective-permute-start(bf16[128,1024]{1,0:T(8,128)(2,1)S(1)} %collective-permute-done.6), channel_id=1, source_target_pairs={{112,0},{0,16},{16,32},{32,48},{48,64},{64,80},{80,96},{96,112},{1... | collective-permute-start | bytes 786440 | tf_op jit(solution)/shard_map/ppermute | solution.py:12
  266.9 23.4 %copy-start.8 = (bf16[128,1024]{1,0:T(8,128)(2,1)}, bf16[128,1024]{1,0:T(8,128)(2,1)S(1)}, u32[]{:S(2)}) copy-start(bf16[128,1024]{1,0:T(8,128)(2,1)S(1)} %collective-permute-done.8) | copy-start | bytes 786436
  266.9 11.4 %collective-permute-start.10 = (bf16[128,1024]{1,0:T(8,128)(2,1)S(1)}, bf16[128,1024]{1,0:T(8,128)(2,1)S(1)}, u32[]{:S(2)}, u32[]{:S(2)}) collective-permute-start(bf16[128,1024]{1,0:T(8,128)(2,1)S(1)} %collective-permute-done.8), channel_id=1, source_target_pairs={{112,0},{0,16},{16,32},{32,48},{48,64},{64,80},{80,96},{96,112},{1... | collective-permute-start | bytes 786440 | tf_op jit(solution)/shard_map/ppermute | solution.py:12
  278.2 12.0 %copy-start.9 = (bf16[128,1024]{1,0:T(8,128)(2,1)}, bf16[128,1024]{1,0:T(8,128)(2,1)S(1)}, u32[]{:S(2)}) copy-start(bf16[128,1024]{1,0:T(8,128)(2,1)S(1)} %collective-permute-done.10) | copy-start | bytes 786436
  278.2 19.2 %collective-permute-start.12 = (bf16[128,1024]{1,0:T(8,128)(2,1)S(1)}, bf16[128,1024]{1,0:T(8,128)(2,1)}, u32[]{:S(2)}, u32[]{:S(2)}) collective-permute-start(bf16[128,1024]{1,0:T(8,128)(2,1)S(1)} %collective-permute-done.10), channel_id=1, source_target_pairs={{112,0},{0,16},{16,32},{32,48},{48,64},{64,80},{80,96},{96,112},{1... | collective-permute-start | bytes 786440 | tf_op jit(solution)/shard_map/ppermute | solution.py:12
  278.3 115.6 %collective-permute-start.13 = (bf16[128,4096]{1,0:T(8,128)(2,1)}, bf16[128,4096]{1,0:T(8,128)(2,1)}, u32[]{:S(2)}, u32[]{:S(2)}) collective-permute-start(bf16[128,4096]{1,0:T(8,128)(2,1)} %collective-permute-done.11), channel_id=1, source_target_pairs={{112,0},{0,16},{16,32},{32,48},{48,64},{64,80},{80,96},{96,112},{1... | collective-permute-start | bytes 3145736 | tf_op jit(solution)/shard_map/ppermute | solution.py:12
  278.9 9.1 %copy-start = (bf16[2048,1024]{1,0:T(8,128)(2,1)S(1)}, bf16[2048,1024]{1,0:T(8,128)(2,1)}, u32[]{:S(2)}) copy-start(bf16[2048,1024]{1,0:T(8,128)(2,1)} %all-gather.3.cloned.1.call-done) | copy-start | bytes 12582916
  292.6 3.6 copy-start.2
  367.1 13.5 %copy-start.1 = (bf16[128,4096]{1,0:T(8,128)(2,1)S(1)}, bf16[128,4096]{1,0:T(8,128)(2,1)}, u32[]{:S(2)}) copy-start(bf16[128,4096]{1,0:T(8,128)(2,1)} %fusion.56) | copy-start | bytes 3145732
  423.9 105.4 %copy-start.3 = (bf16[128,1024]{1,0:T(8,128)(2,1)S(1)}, bf16[128,1024]{1,0:T(8,128)(2,1)}, u32[]{:S(2)}) copy-start(bf16[128,1024]{1,0:T(8,128)(2,1)} %param.2) | copy-start | bytes 786436
Sparse Core Ops, SparseCore 0:
  9.8 71.6 all-gather.2
  83.9 154.7 all-gather.4
  424.0 105.2 reduce-scatter.1
where the time goes:
time: 545 us; the launch traced here: 539 us
  waiting for transfers between devices  368 us (68%)
  matrix products  145 us (27%)
  between operations  13.6 us (2%)
  other arithmetic  10.2 us (2%)
    ppermute x14, waiting for transfers between devices, shifted(): return lax.ppermute(block, axis, route)  263 us
    dot_general x8, matrix products, local(): accum = accum + jnp.dot(resid, visit_s, preferred_element_type=jnp.float32)  124 us
    reduce_scatter x1, waiting for transfers between devices, local(): summed = lax.psum_scatter(accum, 'grp', scatter_dimension=0, tiled=True)  105 us
    dot_general x8, matrix products, residual_tile(): lax.dot_general(block_s, visit_s, (((1,), (1,)), ((), ())), preferred_ele...  20.7 us
  transfers between devices with their start and end apart: 17, of which 11 were waited for; matrix products, arithmetic and copies ran while one was open for 22% of the time, Pallas kernels for 0%

commit v1 on v0

v1 whole, which is shorter than its diff:
```python
import functools
import itertools
import math

import jax
import jax.numpy as jnp
from jax import lax
from jax.experimental import pallas as pl
from jax.experimental.pallas import tpu as pltpu
from jax.sharding import PartitionSpec as P

ROWS = 128
DS, DT = 1024, 4096
WIDE = DS + DT
HALF = WIDE // 2
SCALE_S, SCALE_T = math.sqrt(DS), math.sqrt(DT)

LAYOUT_1 = ["000s", "000o", "001o", "003o", "030o", "300o", "300s", "010o", "010s"]
GROUPS_1 = [("000", [["000o"], ["001o"]]), ("300", [["000o", "001o", "003o", "030o"]]),
            ("010", [["000o", "001o", "003o", "030o", "300o"]])]
LAYOUT_2 = ["000s", "000o", "010o", "010s", "300o", "300s", "200o", "200s",
            "030o", "003o", "001o", "002o", "031o", "033o", "110o", "110s"]
GROUPS_2 = [("010", [["002o", "031o"]]), ("000", [["002o"], ["200o"]]), ("300", [["002o", "031o", "033o", "110o"]]),
            ("200", [["001o", "002o", "031o", "033o"]]), ("110", [["030o", "003o", "001o", "002o", "031o", "033o"]])]
LAYOUT_3 = ["032o", "032s", "010o", "300o", "110o", "200o", "210o", "210s", "030o", "031o"]
GROUPS_3 = [("032", [["010o", "300o", "110o", "200o", "210o"]]), ("210", [["030o", "031o"]])]


def offset(name):
    return tuple(int(t) for t in name[:3])


def fetch(block, distance, flip=False):
    dx, dy, dz = distance
    pairs = []
    for z, low, high, x, core in itertools.product(range(4), range(2), range(2), range(4), range(2)):
        y = (2 * high + low + dy) % 4
        source = ((((z + dz) % 4 * 2 + y % 2) * 2 + y // 2) * 4 + (x + dx) % 4) * 2 + (core ^ int(flip))
        target = (((z * 2 + low) * 2 + high) * 4 + x) * 2 + core
        pairs.append((source, target))
    return lax.ppermute(block, ("blk", "grp"), pairs)


def swap(block):
    return fetch(block, (0, 0, 0), True)


def give(block, name):
    return fetch(block, tuple(-t for t in offset(name)), name[3] == "s")


def unit_kernel(student, teacher, out):
    for source, first, width in ((student, 0, DS), (teacher, DS, DT)):
        wide = source[...].astype(jnp.float32)
        recip = 1.0 / jnp.sqrt(jnp.sum(wide * wide, axis=1, keepdims=True) + 1e-06)
        out[:, first : first + width] = (wide * recip).astype(jnp.bfloat16)


def unit_rows(student, teacher):
    return pl.pallas_call(
        unit_kernel,
        out_shape=jax.ShapeDtypeStruct((ROWS, WIDE), jnp.bfloat16),
        in_specs=[pl.BlockSpec(memory_space=pltpu.VMEM)] * 2,
        out_specs=pl.BlockSpec(memory_space=pltpu.VMEM),
        compiler_params=pltpu.CompilerParams(vmem_limit_bytes=16 << 20),
        name="unit_rows",
    )(student, teacher)


def involution(one, two):
    return all((2 * (s - t)) % 4 == 0 for s, t in zip(offset(one), offset(two)))


def phase_kernel(layout, groups, pieces, starts, adds, outs, *refs):
    at = {name: i * ROWS for i, name in enumerate(layout)}
    refs = list(refs)
    block_refs = [refs.pop(0) for _ in pieces]
    start_refs = [refs.pop(0) for _ in starts]
    add_ref = refs.pop(0) if adds else None
    out_refs = [refs.pop(0) for _ in outs]
    held, sums, acc_s, acc_t, weight, sems = refs[:6]
    added = refs[6] if adds else None
    copies = {}
    number = 0

    def begin(key, source, target):
        nonlocal number
        copy = pltpu.make_async_copy(source, target, sems.at[number])
        copy.start()
        copies.setdefault(key, []).append(copy)
        number += 1

    for (name, first), ref in zip(pieces, block_refs):
        begin(name, ref, held.at[pl.ds(at[name], ROWS), pl.ds(first, ref.shape[1])])
    touched = set()
    for names, ref in zip(starts, start_refs):
        for i, name in enumerate(names):
            if name is not None:
                begin("+" + name, ref.at[pl.ds(i * ROWS, ROWS), :], sums.at[pl.ds(at[name], ROWS), :])
                touched.add(name)
    if adds:
        begin("adds", add_ref, added)

    def ready(key):
        for copy in copies.pop(key, []):
            copy.wait()

    def put(names, value):
        first = at[names[0]]
        for i, name in enumerate(names):
            ready("+" + name)
            rows = pl.ds(first + i * ROWS, ROWS)
            part = value[i * ROWS : (i + 1) * ROWS]
            if name in touched:
                sums[rows, :] += part
            else:
                sums[rows, :] = part
                touched.add(name)

    nt = (((1,), (1,)), ((), ()))
    tn = (((0,), (0,)), ((), ()))
    for a, runs in groups:
        halves = sorted([a + "o", a + "s"], key=at.get)
        both = pl.ds(at[halves[0]], 2 * ROWS)
        for run in runs:
            for name in halves + run:
                ready(name)
            many = len(run) * ROWS
            rows = pl.ds(at[run[0]], many)
            part = pl.ds(0, many)
            acc_s[part, :] = lax.dot_general(
                held[rows, pl.ds(0, DS)], held[both, pl.ds(0, DS)], nt, preferred_element_type=jnp.float32
            )
            acc_t[part, :] = lax.dot_general(
                held[rows, pl.ds(DS, 1024)], held[both, pl.ds(DS, 1024)], nt, preferred_element_type=jnp.float32
            )

            @pl.loop(1, DT // 1024)
            def _(step):
                columns = pl.ds(pl.multiple_of(DS + step * 1024, 1024), 1024)
                acc_t[part, :] += lax.dot_general(
                    held[rows, columns], held[both, columns], nt, preferred_element_type=jnp.float32
                )

            for i, name in enumerate(run):
                tile = pl.ds(i * ROWS, ROWS)
                squash_s = jnp.tanh(SCALE_S * acc_s[tile, :])
                squash_t = jnp.tanh(SCALE_T * acc_t[tile, :])
                value = (squash_s - squash_t) * SCALE_S * (1.0 - squash_s * squash_s)
                if name[:3] != a and involution(a, name):
                    value = 0.5 * value
                weight[tile, :] = value.astype(jnp.bfloat16)
            put(run, jnp.dot(weight[part, :], held[both, pl.ds(0, DS)], preferred_element_type=jnp.float32))
            if run[0][:3] != a:
                put(halves, lax.dot_general(
                    weight[part, :], held[rows, pl.ds(0, DS)], tn, preferred_element_type=jnp.float32
                ))
    for key in list(copies):
        ready(key)
    for names, ref in zip(outs, out_refs):
        for i, name in enumerate(names):
            value = sums[pl.ds(at[name], ROWS), :]
            if name in adds:
                value = value + added[pl.ds(adds.index(name) * ROWS, ROWS), :].astype(jnp.float32)
            ref[pl.ds(i * ROWS, ROWS), :] = value.astype(ref.dtype)


def phase(name, layout, groups, blocks, starts, adds, outs):
    pairs = sum(len(run) for _, runs in groups for run in runs)
    most = max(len(run) for _, runs in groups for run in runs) * ROWS
    copies = len(blocks) + sum(sum(n is not None for n in names) for names, _ in starts) + 1
    shapes = [jax.ShapeDtypeStruct((len(names) * ROWS, DS), kind) for names, kind in outs]
    scratch = [
        pltpu.VMEM((len(layout) * ROWS, WIDE), jnp.bfloat16),
        pltpu.VMEM((len(layout) * ROWS, DS), jnp.float32),
        pltpu.VMEM((most, 2 * ROWS), jnp.float32),
        pltpu.VMEM((most, 2 * ROWS), jnp.float32),
        pltpu.VMEM((most, 2 * ROWS), jnp.bfloat16),
        pltpu.SemaphoreType.DMA((copies,)),
    ]
    operands = [array for _, _, array in blocks] + [array for _, array in starts]
    if adds:
        operands.append(adds[1])
        scratch.append(pltpu.VMEM(adds[1].shape, adds[1].dtype))
    return pl.pallas_call(
        functools.partial(
            phase_kernel, layout, groups, [(n, f) for n, f, _ in blocks], [names for names, _ in starts],
            adds[0] if adds else [], [names for names, _ in outs],
        ),
        out_shape=shapes,
        in_specs=[pl.BlockSpec(memory_space=pl.ANY)] * len(operands),
        out_specs=[pl.BlockSpec(memory_space=pltpu.VMEM)] * len(shapes),
        scratch_shapes=scratch,
        compiler_params=pltpu.CompilerParams(vmem_limit_bytes=56 << 20),
        cost_estimate=pl.CostEstimate(
            flops=pairs * 2 * ROWS * 2 * ROWS * (WIDE + 2 * DS) * 2,
            bytes_accessed=sum(x.size * x.dtype.itemsize for x in operands), transcendentals=0,
        ),
        name=name,
    )(*operands)


def local(student, teacher):
    own = unit_rows(student, teacher)
    f32, bf16 = jnp.float32, jnp.bfloat16
    got = {"000o": own, "000s": swap(own)}
    for name in ("010o", "300o", "001o", "003o", "030o"):
        got[name] = fetch(own, offset(name))
    for a in ("010", "300"):
        got[a + "s"] = swap(got[a + "o"])
    got["110o"] = fetch(got["010o"], (1, 0, 0))
    got["200o"] = fetch(got["300o"], (3, 0, 0))
    got["002o"] = fetch(got["003o"], (0, 0, 3))
    got["031o"] = fetch(got["030o"], (0, 0, 1))
    got["033o"] = fetch(got["003o"], (0, 3, 0))

    rows = lambda layout: [(name, 0, got[name]) for name in layout if name in got]
    names_1 = ["000s", "000o", "001o", "003o", "030o", "300o", "300s", "010o", "010s"]
    (sums_1,) = phase("phase_1", LAYOUT_1, GROUPS_1, rows(LAYOUT_1), [], None, [(names_1, f32)])

    for a in ("110", "200"):
        got[a + "s"] = swap(got[a + "o"])
    late = {
        ("032o", 0): fetch(got["031o"][:, :HALF], (0, 0, 1)),
        ("032o", HALF): fetch(got["033o"][:, HALF:], (0, 0, 3)),
        ("210o", 0): fetch(got["200o"][:, :HALF], (0, 1, 0)),
        ("210o", HALF): fetch(got["110o"][:, HALF:], (1, 0, 0)),
    }
    names_s = ["000s", "010s", "300s", "110s", "200s"]
    names_2 = ["010o", "300o", "110o", "200o", "030o", "031o"]
    early = ["001o", "003o", "002o", "033o"]
    siblings, sums_2, home, *done = phase(
        "phase_2", LAYOUT_2, GROUPS_2, rows(LAYOUT_2), [(names_1, sums_1)], None,
        [(names_s, bf16), (names_2, f32), (["000o"], f32)] + [([name], bf16) for name in early],
    )
    siblings = swap(siblings)
    back = [give(value, name) for name, value in zip(early, done)]

    for (name, first), array in list(late.items()):
        late[name[:3] + "s", first] = swap(array)
    last = ["032o", "032s", "210o", "210s", "110o", "200o", "031o", "010o", "300o", "030o"]
    done = phase(
        "phase_3", LAYOUT_3, GROUPS_3, rows(LAYOUT_3) + [(name, first, array) for (name, first), array in late.items()],
        [(names_2, sums_2)], (["none", "010o", "300o", "110o", "200o"], siblings),
        [([name], bf16) for name in last],
    )
    back += [give(value, name) for name, value in zip(last, done)]

    summed = home + siblings[:ROWS].astype(f32)
    for value in back:
        summed = summed + value.astype(f32)
    wide = student.astype(f32)
    recip = 1.0 / jnp.sqrt(jnp.sum(wide * wide, axis=1, keepdims=True) + 1e-06)
    unit_f = wide * recip
    dunit = (4.0 * DS / math.sqrt(16384)) * summed
    inner = jnp.sum(dunit * unit_f, axis=1, keepdims=True)
    return recip * (dunit - inner * unit_f)


def solution(mesh):
    spec = P(("blk", "grp"), None)
    return jax.shard_map(local, mesh=mesh, in_specs=(spec, spec), out_specs=spec, check_vma=False)
```

time: 545 us -> 207 us (0.38)
  waiting for transfers between devices: 368 us -> 98.3 us
  matrix products: 145 us -> 0 us
  Pallas kernels: 0 us -> 52 us
  starting transfers between devices: 2.52 us -> 48.7 us
  between operations: 13.6 us -> 0.31 us
  other arithmetic: 10.2 us -> 2.82 us
    ppermute x14 -> x38, waiting for transfers between devices: 263 us -> 98.3 us  [fetch(): return lax.ppermute(block, ('blk', 'grp'), pairs)]
    dot_general x16 -> x0, matrix products: 145 us -> none  [the longest x8 124 us: local(): accum = accum + jnp.dot(resid, visit_s, preferred_element_type=jnp.float32)]
    reduce_scatter x1 -> x0, waiting for transfers between devices: 105 us -> none  [local(): summed = lax.psum_scatter(accum, 'grp', scatter_dimension=0, tiled=True)]
    pallas_call x0 -> x4, Pallas kernels: none -> 52 us  [the longest x3 51.5 us: phase(): pl.pallas_call(functools.partial(phase_kernel, layout, groups, [(n, f) fo...]
    ppermute x14 -> x38, starting transfers between devices: 2.43 us -> 48.7 us  [fetch(): return lax.ppermute(block, ('blk', 'grp'), pairs)]
  transfers between devices with their start and end apart: 17 -> 38, of which waited for: 11 -> 14; matrix products, arithmetic and copies ran while one was open for 22% -> 0% of each run, Pallas kernels for 0% -> 25%
where the time goes in v1:
time: 207 us
  waiting for transfers between devices  98.3 us (47%)
  Pallas kernels  52 us (25%)
  starting transfers between devices  48.7 us (24%)
  local copies, waits for them, and re-layouts  4.52 us (2%)
  other arithmetic  2.82 us (1%)
    ppermute x38, waiting for transfers between devices, fetch(): return lax.ppermute(block, ('blk', 'grp'), pairs)  98.3 us
    pallas_call x3, Pallas kernels, phase(): pl.pallas_call(functools.partial(phase_kernel, layout, groups, [(n, f) fo...  51.5 us
    ppermute x38, starting transfers between devices, fetch(): return lax.ppermute(block, ('blk', 'grp'), pairs)  48.7 us
    unnamed x48, local copies, waits for them, and re-layouts  4.34 us
  transfers between devices with their start and end apart: 38, of which 14 were waited for; matrix products, arithmetic and copies ran while one was open for 0% of the time, Pallas kernels for 25%

profile of v1, /device:TPU:0, one launch (start us, length us, event | category | flops | bytes accessed | tf_op | source)
XLA Modules:
  0.0 206.6 jit_solution(6060954630391171047)
XLA Ops:
  0.0 0.9 copy-done
  1.0 1.2 copy-done.3
  2.2 0.5 unit_rows.1.refs_1_
  2.7 3.2 %collective-permute-start.1 = (bf16[128,5120]{1,0:T(8,128)(2,1)S(1)}, bf16[128,5120]{1,0:T(8,128)(2,1)S(1)}, u32[]{:S(2)}, u32[]{:S(2)}) collective-permute-start(bf16[128,5120]{1,0:T(8,128)(2,1)S(1)} %unit_rows.1.refs_1_), channel_id=1, source_target_pairs={{16,0},{17,1},{18,2},{19,3},{20,4},{21,5},{22,6},{23,7},{24,8},{25... | collective-permute-start | bytes 3932168 | tf_op jit(solution)/shard_map/ppermute | solution.py:41
  5.8 1.5 collective-permute-start.3
  7.3 0.0 collective-permute-start.7
  7.3 1.9 collective-permute-start.8
  9.2 24.6 %collective-permute-done.1.refs_7_.refs_2_.refs_0_ = bf16[128,5120]{1,0:T(8,128)(2,1)S(1)} collective-permute-done((bf16[128,5120]{1,0:T(8,128)(2,1)S(1)}, bf16[128,5120]{1,0:T(8,128)(2,1)S(1)}, u32[]{:S(2)}, u32[]{:S(2)}) %collective-permute-start.1) | collective-permute-done | bytes 1310752 | tf_op jit(solution)/shard_map/ppermute | solution.py:41
  33.9 4.0 %collective-permute-start.9 = (bf16[128,5120]{1,0:T(8,128)(2,1)S(1)}, bf16[128,5120]{1,0:T(8,128)(2,1)S(1)}, u32[]{:S(2)}, u32[]{:S(2)}) collective-permute-start(bf16[128,5120]{1,0:T(8,128)(2,1)S(1)} %unit_rows.1.refs_1_), channel_id=1, source_target_pairs={{32,0},{33,1},{34,2},{35,3},{36,4},{37,5},{38,6},{39,7},{40,8},{41... | collective-permute-start | bytes 3932168 | tf_op jit(solution)/shard_map/ppermute | solution.py:41
  37.9 2.8 %collective-permute-start.13 = (bf16[128,5120]{1,0:T(8,128)(2,1)S(1)}, bf16[128,5120]{1,0:T(8,128)(2,1)S(1)}, u32[]{:S(2)}, u32[]{:S(2)}) collective-permute-start(bf16[128,5120]{1,0:T(8,128)(2,1)S(1)} %collective-permute-done.1.refs_7_.refs_2_.refs_0_), channel_id=1, source_target_pairs={{2,0},{3,1},{4,2},{5,3},{6,4},{7,5},{0,6},{1,7},{10,8},{11,9},{12,... | collective-permute-start | bytes 3932168 | tf_op jit(solution)/shard_map/ppermute | solution.py:41
  40.7 0.0 collective-permute-done.7.refs_4_.refs_8_
  40.7 0.0 collective-permute-done.8.refs_3_.refs_9_
  40.7 3.3 %collective-permute-start.11 = (bf16[128,5120]{1,0:T(8,128)(2,1)S(1)}, bf16[128,5120]{1,0:T(8,128)(2,1)S(1)}, u32[]{:S(2)}, u32[]{:S(2)}) collective-permute-start(bf16[128,5120]{1,0:T(8,128)(2,1)S(1)} %collective-permute-done.7.refs_4_.refs_8_), channel_id=1, source_target_pairs={{32,0},{33,1},{34,2},{35,3},{36,4},{37,5},{38,6},{39,7},{40,8},{41... | collective-permute-start | bytes 3932168 | tf_op jit(solution)/shard_map/ppermute | solution.py:41
  44.0 0.0 collective-permute-done.refs_0_
  44.0 0.0 collective-permute-start.12
  44.0 23.1 %collective-permute-done.9.refs_2_.refs_10_ = bf16[128,5120]{1,0:T(8,128)(2,1)S(1)} collective-permute-done((bf16[128,5120]{1,0:T(8,128)(2,1)S(1)}, bf16[128,5120]{1,0:T(8,128)(2,1)S(1)}, u32[]{:S(2)}, u32[]{:S(2)}) %collective-permute-start.9) | collective-permute-done | bytes 1310752 | tf_op jit(solution)/shard_map/ppermute | solution.py:41
  67.1 0.4 collective-permute-done.13.refs_14_.refs_2_
  67.5 0.1 collective-permute-start.4
  67.6 3.3 %collective-permute-done.5.refs_6_.refs_3_ = bf16[128,5120]{1,0:T(8,128)(2,1)S(1)} collective-permute-done((bf16[128,5120]{1,0:T(8,128)(2,1)S(1)}, bf16[128,5120]{1,0:T(8,128)(2,1)S(1)}, u32[]{:S(2)}, u32[]{:S(2)}) %collective-permute-start.5) | collective-permute-done | bytes 1310752 | tf_op jit(solution)/shard_map/ppermute | solution.py:41
  71.0 0.1 collective-permute-start.10
  71.1 22.0 %collective-permute-done.11.refs_12_.refs_5_ = bf16[128,5120]{1,0:T(8,128)(2,1)S(1)} collective-permute-done((bf16[128,5120]{1,0:T(8,128)(2,1)S(1)}, bf16[128,5120]{1,0:T(8,128)(2,1)S(1)}, u32[]{:S(2)}, u32[]{:S(2)}) %collective-permute-start.11) | collective-permute-done | bytes 1310752 | tf_op jit(solution)/shard_map/ppermute | solution.py:41
  93.2 0.0 collective-permute-start.14
  93.2 0.0 collective-permute-done.12.refs_13_
  93.2 0.6 collective-permute-start.6
  94.0 0.0 collective-permute-done.2.refs_8_.refs_3_
  94.0 3.8 %collective-permute-start.22 = (bf16[128,2560]{1,0:T(8,128)(2,1)S(1)}, bf16[128,2560]{1,0:T(8,128)(2,1)S(1)}, u32[]{:S(2)}, u32[]{:S(2)}) collective-permute-start(bf16[128,2560]{1,0:T(8,128)(2,1)S(1)} %slice.23), channel_id=1, source_target_pairs={{16,0},{17,1},{18,2},{19,3},{20,4},{21,5},{22,6},{23,7},{24,8},{25... | collective-permute-start | bytes 1966088 | tf_op jit(solution)/shard_map/ppermute | solution.py:41
  97.8 0.0 collective-permute-done.4.refs_6_.refs_5_
  97.8 1.1 copy-done.16
  98.9 2.8 %collective-permute-start.23 = (bf16[128,2560]{1,0:T(8,128)(2,1)S(1)}, bf16[128,2560]{1,0:T(8,128)(2,1)}, u32[]{:S(2)}, u32[]{:S(2)}) collective-permute-start(bf16[128,2560]{1,0:T(8,128)(2,1)S(1)} %slice.24), channel_id=1, source_target_pairs={{2,0},{3,1},{4,2},{5,3},{6,4},{7,5},{0,6},{1,7},{10,8},{11,9},{12,... | collective-permute-start | bytes 1966088 | tf_op jit(solution)/shard_map/ppermute | solution.py:41
  101.6 13.8 %phase_1.1.refs_16_ = f32[1152,1024]{1,0:T(8,128)} custom-call(bf16[128,5120]{1,0:T(8,128)(2,1)} %copy-done.13, bf16[128,5120]{1,0:T(8,128)(2,1)} %copy-done.2, bf16[128,5120]{1,0:T(8,128)(2,1)} %copy-done.14, bf16[128,5120]{1,0:T(8,128)(2,1)} %collective-permute-done.8.refs_3_.refs_9_, bf16[128,5120]{1,0:T(8,128)(2,1)} %copy-done.12, ...), custom_call_target="tpu_custom_call" | custom-call | flops 10334765056 | bytes 11796480 | tf_op jit(solution)/shard_map/phase_1/pallas_call | solution.py:185
  115.5 3.8 %collective-permute-start.20 = (bf16[128,2560]{1,0:T(8,128)(2,1)S(1)}, bf16[128,2560]{1,0:T(8,128)(2,1)S(1)}, u32[]{:S(2)}, u32[]{:S(2)}) collective-permute-start(bf16[128,2560]{1,0:T(8,128)(2,1)S(1)} %slice.21), channel_id=1, source_target_pairs={{32,0},{33,1},{34,2},{35,3},{36,4},{37,5},{38,6},{39,7},{40,8},{41... | collective-permute-start | bytes 1966088 | tf_op jit(solution)/shard_map/ppermute | solution.py:41
  119.3 0.0 collective-permute-start.21
  119.3 25.4 %phase_2.1 = (bf16[640,1024]{1,0:T(8,128)(2,1)}, f32[768,1024]{1,0:T(8,128)}, f32[128,1024]{1,0:T(8,128)}, bf16[128,1024]{1,0:T(8,128)(2,1)}, bf16[128,1024]{1,0...) custom-call(bf16[128,5120]{1,0:T(8,128)(2,1)} %copy-done.13, bf16[128,5120]{1,0:T(8,128)(2,1)} %copy-done.2, ...), custom_call_target="tpu_custom_call" | custom-call | flops 16911433728 | bytes 25690112 | tf_op jit(solution)/shard_map/phase_2/pallas_call | solution.py:185
  144.7 0.1 collective-permute-start.15
  144.8 0.5 collective-permute-start.26
  145.3 0.1 collective-permute-start.27
  145.4 0.4 collective-permute-start.24
  145.8 0.0 collective-permute-done.21.refs_7_
  145.8 0.1 collective-permute-start.25
  145.9 3.4 %collective-permute-done.26.refs_12_ = bf16[128,2560]{1,0:T(8,128)(2,1)S(1)} collective-permute-done((bf16[128,2560]{1,0:T(8,128)(2,1)S(1)}, bf16[128,2560]{1,0:T(8,128)(2,1)S(1)}, u32[]{:S(2)}, u32[]{:S(2)}) %collective-permute-start.26) | collective-permute-done | bytes 655392 | tf_op jit(solution)/shard_map/ppermute | solution.py:41
  149.3 1.3 collective-permute-done.27.refs_13_
  150.7 3.2 %collective-permute-start.17 = (bf16[128,1024]{1,0:T(8,128)(2,1)}, bf16[128,1024]{1,0:T(8,128)(2,1)S(1)}, u32[]{:S(2)}, u32[]{:S(2)}) collective-permute-start(bf16[128,1024]{1,0:T(8,128)(2,1)} %get-tuple-element.25), channel_id=1, source_target_pairs={{32,0},{33,1},{34,2},{35,3},{36,4},{37,5},{38,6},{39,7},{40,8},{41... | collective-permute-start | bytes 786440 | tf_op jit(solution)/shard_map/ppermute | solution.py:41
  153.9 0.3 collective-permute-start.18
  154.2 1.7 collective-permute-start.19
  155.9 1.0 copy-done.9
  157.0 12.2 %phase_3.1 = (bf16[128,1024]{1,0:T(8,128)(2,1)}, bf16[128,1024]{1,0:T(8,128)(2,1)}, bf16[128,1024]{1,0:T(8,128)(2,1)}, bf16[128,1024]{1,0:T(8,128)(2,1)}, bf16[1...) custom-call(bf16[128,5120]{1,0:T(8,128)(2,1)} %copy-done.10, ...), custom_call_target="tpu_custom_call" | custom-call | flops 6576668672 | bytes 17563648 | tf_op jit(solution)/shard_map/phase_3/pallas_call | solution.py:185
  169.2 2.3 %collective-permute-start.28 = (bf16[128,1024]{1,0:T(8,128)(2,1)}, bf16[128,1024]{1,0:T(8,128)(2,1)S(1)}, u32[]{:S(2)}, u32[]{:S(2)}) collective-permute-start(bf16[128,1024]{1,0:T(8,128)(2,1)} %get-tuple-element.29), channel_id=1, source_target_pairs={{80,0},{81,1},{82,2},{83,3},{84,4},{85,5},{86,6},{87,7},{88,8},{89... | collective-permute-start | bytes 786440 | tf_op jit(solution)/shard_map/ppermute | solution.py:41
  171.6 1.7 collective-permute-start.30
  173.3 4.4 %collective-permute-start.31 = (bf16[128,1024]{1,0:T(8,128)(2,1)}, bf16[128,1024]{1,0:T(8,128)(2,1)S(1)}, u32[]{:S(2)}, u32[]{:S(2)}) collective-permute-start(bf16[128,1024]{1,0:T(8,128)(2,1)} %get-tuple-element.32), channel_id=1, source_target_pairs={{29,0},{28,1},{31,2},{30,3},{25,4},{24,5},{27,6},{26,7},{21,8},{20... | collective-permute-start | bytes 786440 | tf_op jit(solution)/shard_map/ppermute | solution.py:41
  177.6 3.5 %collective-permute-done.28 = bf16[128,1024]{1,0:T(8,128)(2,1)S(1)} collective-permute-done((bf16[128,1024]{1,0:T(8,128)(2,1)}, bf16[128,1024]{1,0:T(8,128)(2,1)S(1)}, u32[]{:S(2)}, u32[]{:S(2)}) %collective-permute-start.28) | collective-permute-done | bytes 262176 | tf_op jit(solution)/shard_map/ppermute | solution.py:41
  181.2 0.8 collective-permute-start.33
  182.0 1.4 collective-permute-done.29
  183.3 1.9 collective-permute-start.34
  185.3 0.9 collective-permute-start.35
  186.2 2.8 %collective-permute-done.31 = bf16[128,1024]{1,0:T(8,128)(2,1)S(1)} collective-permute-done((bf16[128,1024]{1,0:T(8,128)(2,1)}, bf16[128,1024]{1,0:T(8,128)(2,1)S(1)}, u32[]{:S(2)}, u32[]{:S(2)}) %collective-permute-start.31) | collective-permute-done | bytes 262176 | tf_op jit(solution)/shard_map/ppermute | solution.py:41
  189.0 0.8 collective-permute-start.36
  189.9 5.7 %collective-permute-done.32 = bf16[128,1024]{1,0:T(8,128)(2,1)S(1)} collective-permute-done((bf16[128,1024]{1,0:T(8,128)(2,1)}, bf16[128,1024]{1,0:T(8,128)(2,1)S(1)}, u32[]{:S(2)}, u32[]{:S(2)}) %collective-permute-start.32) | collective-permute-done | bytes 262176 | tf_op jit(solution)/shard_map/ppermute | solution.py:41
  195.6 1.6 collective-permute-start.37
  197.2 0.1 fusion.5
  197.3 2.7 %collective-permute-done.33 = bf16[128,1024]{1,0:T(8,128)(2,1)S(1)} collective-permute-done((bf16[128,1024]{1,0:T(8,128)(2,1)}, bf16[128,1024]{1,0:T(8,128)(2,1)S(1)}, u32[]{:S(2)}, u32[]{:S(2)}) %collective-permute-start.33) | collective-permute-done | bytes 262176 | tf_op jit(solution)/shard_map/ppermute | solution.py:41
  200.0 0.7 collective-permute-done.35
  200.8 3.2 %collective-permute-done.37 = bf16[128,1024]{1,0:T(8,128)(2,1)S(1)} collective-permute-done((bf16[128,1024]{1,0:T(8,128)(2,1)}, bf16[128,1024]{1,0:T(8,128)(2,1)S(1)}, u32[]{:S(2)}, u32[]{:S(2)}) %collective-permute-start.37) | collective-permute-done | bytes 262176 | tf_op jit(solution)/shard_map/ppermute | solution.py:41
  203.9 1.7 fusion.2
  205.6 1.0 fusion.4
  (72 shorter events, 0.3 us)
Async XLA Ops:
  0.0 0.9 copy-start
  1.0 1.2 copy-start.3
  2.6 91.2 %copy-start.2 = (bf16[128,5120]{1,0:T(8,128)(2,1)}, bf16[128,5120]{1,0:T(8,128)(2,1)S(1)}, u32[]{:S(2)}) copy-start(bf16[128,5120]{1,0:T(8,128)(2,1)S(1)} %unit_rows.1.refs_1_) | copy-start | bytes 3932164
  2.7 31.2 %collective-permute-start.1 = (bf16[128,5120]{1,0:T(8,128)(2,1)S(1)}, bf16[128,5120]{1,0:T(8,128)(2,1)S(1)}, u32[]{:S(2)}, u32[]{:S(2)}) collective-permute-start(bf16[128,5120]{1,0:T(8,128)(2,1)S(1)} %unit_rows.1.refs_1_), channel_id=1, source_target_pairs={{16,0},{17,1},{18,2},{19,3},{20,4},{21,5},{22,6},{23,7},{24,8},{25... | collective-permute-start | bytes 3932168 | tf_op jit(solution)/shard_map/ppermute | solution.py:41
  5.8 32.1 %collective-permute-start.3 = (bf16[128,5120]{1,0:T(8,128)(2,1)S(1)}, bf16[128,5120]{1,0:T(8,128)(2,1)S(1)}, u32[]{:S(2)}, u32[]{:S(2)}) collective-permute-start(bf16[128,5120]{1,0:T(8,128)(2,1)S(1)} %unit_rows.1.refs_1_), channel_id=1, source_target_pairs={{6,0},{7,1},{0,2},{1,3},{2,4},{3,5},{4,6},{5,7},{14,8},{15,9},{8,1... | collective-permute-start | bytes 3932168 | tf_op jit(solution)/shard_map/ppermute | solution.py:41
  7.3 33.4 %collective-permute-start.7 = (bf16[128,5120]{1,0:T(8,128)(2,1)S(1)}, bf16[128,5120]{1,0:T(8,128)(2,1)S(1)}, u32[]{:S(2)}, u32[]{:S(2)}) collective-permute-start(bf16[128,5120]{1,0:T(8,128)(2,1)S(1)} %unit_rows.1.refs_1_), channel_id=1, source_target_pairs={{24,0},{25,1},{26,2},{27,3},{28,4},{29,5},{30,6},{31,7},{16,8},{17... | collective-permute-start | bytes 3932168 | tf_op jit(solution)/shard_map/ppermute | solution.py:41
  7.3 33.4 %collective-permute-start.8 = (bf16[128,5120]{1,0:T(8,128)(2,1)S(1)}, bf16[128,5120]{1,0:T(8,128)(2,1)}, u32[]{:S(2)}, u32[]{:S(2)}) collective-permute-start(bf16[128,5120]{1,0:T(8,128)(2,1)S(1)} %unit_rows.1.refs_1_), channel_id=1, source_target_pairs={{96,0},{97,1},{98,2},{99,3},{100,4},{101,5},{102,6},{103,7},{104,8... | collective-permute-start | bytes 3932168 | tf_op jit(solution)/shard_map/ppermute | solution.py:41
  9.2 34.8 %collective-permute-start = (bf16[128,5120]{1,0:T(8,128)(2,1)S(1)}, bf16[128,5120]{1,0:T(8,128)(2,1)S(1)}, u32[]{:S(2)}, u32[]{:S(2)}) collective-permute-start(bf16[128,5120]{1,0:T(8,128)(2,1)S(1)} %unit_rows.1.refs_1_), channel_id=1, source_target_pairs={{1,0},{0,1},{3,2},{2,3},{5,4},{4,5},{7,6},{6,7},{9,8},{8,9},{11,10... | collective-permute-start | bytes 3932168 | tf_op jit(solution)/shard_map/ppermute | solution.py:41
  33.9 63.9 %copy-start.10 = (bf16[128,5120]{1,0:T(8,128)(2,1)}, bf16[128,5120]{1,0:T(8,128)(2,1)S(1)}, u32[]{:S(2)}) copy-start(bf16[128,5120]{1,0:T(8,128)(2,1)S(1)} %collective-permute-done.1.refs_7_.refs_2_.refs_0_) | copy-start | bytes 3932164
  33.9 33.3 %collective-permute-start.9 = (bf16[128,5120]{1,0:T(8,128)(2,1)S(1)}, bf16[128,5120]{1,0:T(8,128)(2,1)S(1)}, u32[]{:S(2)}, u32[]{:S(2)}) collective-permute-start(bf16[128,5120]{1,0:T(8,128)(2,1)S(1)} %unit_rows.1.refs_1_), channel_id=1, source_target_pairs={{32,0},{33,1},{34,2},{35,3},{36,4},{37,5},{38,6},{39,7},{40,8},{41... | collective-permute-start | bytes 3932168 | tf_op jit(solution)/shard_map/ppermute | solution.py:41
  37.9 59.9 %copy-start.11 = (bf16[128,5120]{1,0:T(8,128)(2,1)}, bf16[128,5120]{1,0:T(8,128)(2,1)S(1)}, u32[]{:S(2)}) copy-start(bf16[128,5120]{1,0:T(8,128)(2,1)S(1)} %collective-permute-done.3.refs_5_.refs_4_.refs_1_) | copy-start | bytes 3932164
  37.9 29.6 %collective-permute-start.13 = (bf16[128,5120]{1,0:T(8,128)(2,1)S(1)}, bf16[128,5120]{1,0:T(8,128)(2,1)S(1)}, u32[]{:S(2)}, u32[]{:S(2)}) collective-permute-start(bf16[128,5120]{1,0:T(8,128)(2,1)S(1)} %collective-permute-done.1.refs_7_.refs_2_.refs_0_), channel_id=1, source_target_pairs={{2,0},{3,1},{4,2},{5,3},{6,4},{7,5},{0,6},{1,7},{10,8},{11,9},{12,... | collective-permute-start | bytes 3932168 | tf_op jit(solution)/shard_map/ppermute | solution.py:41
  40.7 53.1 %copy-start.12 = (bf16[128,5120]{1,0:T(8,128)(2,1)}, bf16[128,5120]{1,0:T(8,128)(2,1)S(1)}, u32[]{:S(2)}) copy-start(bf16[128,5120]{1,0:T(8,128)(2,1)S(1)} %collective-permute-done.7.refs_4_.refs_8_) | copy-start | bytes 3932164
  40.7 30.3 %collective-permute-start.5 = (bf16[128,5120]{1,0:T(8,128)(2,1)S(1)}, bf16[128,5120]{1,0:T(8,128)(2,1)S(1)}, u32[]{:S(2)}, u32[]{:S(2)}) collective-permute-start(bf16[128,5120]{1,0:T(8,128)(2,1)S(1)} %collective-permute-done.3.refs_5_.refs_4_.refs_1_), channel_id=1, source_target_pairs={{6,0},{7,1},{0,2},{1,3},{2,4},{3,5},{4,6},{5,7},{14,8},{15,9},{8,1... | collective-permute-start | bytes 3932168 | tf_op jit(solution)/shard_map/ppermute | solution.py:41
  40.7 52.5 %collective-permute-start.11 = (bf16[128,5120]{1,0:T(8,128)(2,1)S(1)}, bf16[128,5120]{1,0:T(8,128)(2,1)S(1)}, u32[]{:S(2)}, u32[]{:S(2)}) collective-permute-start(bf16[128,5120]{1,0:T(8,128)(2,1)S(1)} %collective-permute-done.7.refs_4_.refs_8_), channel_id=1, source_target_pairs={{32,0},{33,1},{34,2},{35,3},{36,4},{37,5},{38,6},{39,7},{40,8},{41... | collective-permute-start | bytes 3932168 | tf_op jit(solution)/shard_map/ppermute | solution.py:41
  44.0 49.1 %copy-start.13 = (bf16[128,5120]{1,0:T(8,128)(2,1)}, bf16[128,5120]{1,0:T(8,128)(2,1)S(1)}, u32[]{:S(2)}) copy-start(bf16[128,5120]{1,0:T(8,128)(2,1)S(1)} %collective-permute-done.refs_0_) | copy-start | bytes 3932164
  44.0 49.1 %collective-permute-start.12 = (bf16[128,5120]{1,0:T(8,128)(2,1)}, bf16[128,5120]{1,0:T(8,128)(2,1)S(1)}, u32[]{:S(2)}, u32[]{:S(2)}) collective-permute-start(bf16[128,5120]{1,0:T(8,128)(2,1)} %collective-permute-done.8.refs_3_.refs_9_), channel_id=1, source_target_pairs={{24,0},{25,1},{26,2},{27,3},{28,4},{29,5},{30,6},{31,7},{16,8},{17... | collective-permute-start | bytes 3932168 | tf_op jit(solution)/shard_map/ppermute | solution.py:41
  67.1 26.0 %copy-start.14 = (bf16[128,5120]{1,0:T(8,128)(2,1)}, bf16[128,5120]{1,0:T(8,128)(2,1)S(1)}, u32[]{:S(2)}) copy-start(bf16[128,5120]{1,0:T(8,128)(2,1)S(1)} %collective-permute-done.9.refs_2_.refs_10_) | copy-start | bytes 3932164
  67.1 26.9 %collective-permute-start.2 = (bf16[128,5120]{1,0:T(8,128)(2,1)S(1)}, bf16[128,5120]{1,0:T(8,128)(2,1)S(1)}, u32[]{:S(2)}, u32[]{:S(2)}) collective-permute-start(bf16[128,5120]{1,0:T(8,128)(2,1)S(1)} %collective-permute-done.1.refs_7_.refs_2_.refs_0_), channel_id=1, source_target_pairs={{1,0},{0,1},{3,2},{2,3},{5,4},{4,5},{7,6},{6,7},{9,8},{8,9},{11,10... | collective-permute-start | bytes 3932168 | tf_op jit(solution)/shard_map/ppermute | solution.py:41
  67.5 26.3 %copy-start.5 = (bf16[128,5120]{1,0:T(8,128)(2,1)}, bf16[128,5120]{1,0:T(8,128)(2,1)S(1)}, u32[]{:S(2)}) copy-start(bf16[128,5120]{1,0:T(8,128)(2,1)S(1)} %collective-permute-done.13.refs_14_.refs_2_) | copy-start | bytes 3932164
  67.5 30.2 %collective-permute-start.4 = (bf16[128,5120]{1,0:T(8,128)(2,1)S(1)}, bf16[128,5120]{1,0:T(8,128)(2,1)S(1)}, u32[]{:S(2)}, u32[]{:S(2)}) collective-permute-start(bf16[128,5120]{1,0:T(8,128)(2,1)S(1)} %collective-permute-done.3.refs_5_.refs_4_.refs_1_), channel_id=1, source_target_pairs={{1,0},{0,1},{3,2},{2,3},{5,4},{4,5},{7,6},{6,7},{9,8},{8,9},{11,10... | collective-permute-start | bytes 3932168 | tf_op jit(solution)/shard_map/ppermute | solution.py:41
  71.0 44.5 %copy-start.6 = (bf16[128,5120]{1,0:T(8,128)(2,1)}, bf16[128,5120]{1,0:T(8,128)(2,1)S(1)}, u32[]{:S(2)}) copy-start(bf16[128,5120]{1,0:T(8,128)(2,1)S(1)} %collective-permute-done.5.refs_6_.refs_3_) | copy-start | bytes 3932164
  71.0 44.5 %collective-permute-start.10 = (bf16[128,5120]{1,0:T(8,128)(2,1)}, bf16[128,5120]{1,0:T(8,128)(2,1)}, u32[]{:S(2)}, u32[]{:S(2)}) collective-permute-start(bf16[128,5120]{1,0:T(8,128)(2,1)} %collective-permute-done.8.refs_3_.refs_9_), channel_id=1, source_target_pairs={{96,0},{97,1},{98,2},{99,3},{100,4},{101,5},{102,6},{103,7},{104,8... | collective-permute-start | bytes 3932168 | tf_op jit(solution)/shard_map/ppermute | solution.py:41
  93.1 22.3 %copy-start.7 = (bf16[128,5120]{1,0:T(8,128)(2,1)}, bf16[128,5120]{1,0:T(8,128)(2,1)S(1)}, u32[]{:S(2)}) copy-start(bf16[128,5120]{1,0:T(8,128)(2,1)S(1)} %collective-permute-done.11.refs_12_.refs_5_) | copy-start | bytes 3932164
  93.2 26.1 %collective-permute-start.14 = (bf16[128,5120]{1,0:T(8,128)(2,1)S(1)}, bf16[128,5120]{1,0:T(8,128)(2,1)}, u32[]{:S(2)}, u32[]{:S(2)}) collective-permute-start(bf16[128,5120]{1,0:T(8,128)(2,1)S(1)} %collective-permute-done.13.refs_14_.refs_2_), channel_id=1, source_target_pairs={{1,0},{0,1},{3,2},{2,3},{5,4},{4,5},{7,6},{6,7},{9,8},{8,9},{11,10... | collective-permute-start | bytes 3932168 | tf_op jit(solution)/shard_map/ppermute | solution.py:41
  93.2 4.6 %copy-start.8 = (bf16[128,5120]{1,0:T(8,128)(2,1)}, bf16[128,5120]{1,0:T(8,128)(2,1)S(1)}, u32[]{:S(2)}) copy-start(bf16[128,5120]{1,0:T(8,128)(2,1)S(1)} %collective-permute-done.12.refs_13_) | copy-start | bytes 3932164
  93.2 26.1 %collective-permute-start.6 = (bf16[128,5120]{1,0:T(8,128)(2,1)S(1)}, bf16[128,5120]{1,0:T(8,128)(2,1)}, u32[]{:S(2)}, u32[]{:S(2)}) collective-permute-start(bf16[128,5120]{1,0:T(8,128)(2,1)S(1)} %collective-permute-done.5.refs_6_.refs_3_), channel_id=1, source_target_pairs={{1,0},{0,1},{3,2},{2,3},{5,4},{4,5},{7,6},{6,7},{9,8},{8,9},{11,10... | collective-permute-start | bytes 3932168 | tf_op jit(solution)/shard_map/ppermute | solution.py:41
  94.0 3.8 %copy-start.15 = (bf16[128,5120]{1,0:T(8,128)(2,1)}, bf16[128,5120]{1,0:T(8,128)(2,1)S(1)}, u32[]{:S(2)}) copy-start(bf16[128,5120]{1,0:T(8,128)(2,1)S(1)} %collective-permute-done.2.refs_8_.refs_3_) | copy-start | bytes 3932164
  94.0 50.8 %collective-permute-start.22 = (bf16[128,2560]{1,0:T(8,128)(2,1)S(1)}, bf16[128,2560]{1,0:T(8,128)(2,1)S(1)}, u32[]{:S(2)}, u32[]{:S(2)}) collective-permute-start(bf16[128,2560]{1,0:T(8,128)(2,1)S(1)} %slice.23), channel_id=1, source_target_pairs={{16,0},{17,1},{18,2},{19,3},{20,4},{21,5},{22,6},{23,7},{24,8},{25... | collective-permute-start | bytes 1966088 | tf_op jit(solution)/shard_map/ppermute | solution.py:41
  97.8 1.1 copy-start.16
  98.9 46.5 %collective-permute-start.23 = (bf16[128,2560]{1,0:T(8,128)(2,1)S(1)}, bf16[128,2560]{1,0:T(8,128)(2,1)}, u32[]{:S(2)}, u32[]{:S(2)}) collective-permute-start(bf16[128,2560]{1,0:T(8,128)(2,1)S(1)} %slice.24), channel_id=1, source_target_pairs={{2,0},{3,1},{4,2},{5,3},{6,4},{7,5},{0,6},{1,7},{10,8},{11,9},{12,... | collective-permute-start | bytes 1966088 | tf_op jit(solution)/shard_map/ppermute | solution.py:41
  115.5 29.9 %collective-permute-start.20 = (bf16[128,2560]{1,0:T(8,128)(2,1)S(1)}, bf16[128,2560]{1,0:T(8,128)(2,1)S(1)}, u32[]{:S(2)}, u32[]{:S(2)}) collective-permute-start(bf16[128,2560]{1,0:T(8,128)(2,1)S(1)} %slice.21), channel_id=1, source_target_pairs={{32,0},{33,1},{34,2},{35,3},{36,4},{37,5},{38,6},{39,7},{40,8},{41... | collective-permute-start | bytes 1966088 | tf_op jit(solution)/shard_map/ppermute | solution.py:41
  119.3 26.6 %collective-permute-start.21 = (bf16[128,2560]{1,0:T(8,128)(2,1)S(1)}, bf16[128,2560]{1,0:T(8,128)(2,1)S(1)}, u32[]{:S(2)}, u32[]{:S(2)}) collective-permute-start(bf16[128,2560]{1,0:T(8,128)(2,1)S(1)} %slice.22), channel_id=1, source_target_pairs={{96,0},{97,1},{98,2},{99,3},{100,4},{101,5},{102,6},{103,7},{104,8... | collective-permute-start | bytes 1966088 | tf_op jit(solution)/shard_map/ppermute | solution.py:41
  144.7 11.2 %collective-permute-start.15 = (bf16[640,1024]{1,0:T(8,128)(2,1)}, bf16[640,1024]{1,0:T(8,128)(2,1)S(1)}, u32[]{:S(2)}, u32[]{:S(2)}) collective-permute-start(bf16[640,1024]{1,0:T(8,128)(2,1)} %get-tuple-element.23), channel_id=1, source_target_pairs={{1,0},{0,1},{3,2},{2,3},{5,4},{4,5},{7,6},{6,7},{9,8},{8,9},{11,10... | collective-permute-start | bytes 3932168 | tf_op jit(solution)/shard_map/ppermute | solution.py:41
  144.8 11.1 %copy-start.17 = (bf16[128,2560]{1,0:T(8,128)(2,1)}, bf16[128,2560]{1,0:T(8,128)(2,1)S(1)}, u32[]{:S(2)}) copy-start(bf16[128,2560]{1,0:T(8,128)(2,1)S(1)} %collective-permute-done.22.refs_8_) | copy-start | bytes 1966084
  144.8 4.5 %collective-permute-start.26 = (bf16[128,2560]{1,0:T(8,128)(2,1)S(1)}, bf16[128,2560]{1,0:T(8,128)(2,1)S(1)}, u32[]{:S(2)}, u32[]{:S(2)}) collective-permute-start(bf16[128,2560]{1,0:T(8,128)(2,1)S(1)} %collective-permute-done.22.refs_8_), channel_id=1, source_target_pairs={{1,0},{0,1},{3,2},{2,3},{5,4},{4,5},{7,6},{6,7},{9,8},{8,9},{11,10... | collective-permute-start | bytes 1966088 | tf_op jit(solution)/shard_map/ppermute | solution.py:41
  145.3 5.3 %collective-permute-start.27 = (bf16[128,2560]{1,0:T(8,128)(2,1)}, bf16[128,2560]{1,0:T(8,128)(2,1)S(1)}, u32[]{:S(2)}, u32[]{:S(2)}) collective-permute-start(bf16[128,2560]{1,0:T(8,128)(2,1)} %collective-permute-done.23.refs_9_), channel_id=1, source_target_pairs={{1,0},{0,1},{3,2},{2,3},{5,4},{4,5},{7,6},{6,7},{9,8},{8,9},{11,10... | collective-permute-start | bytes 1966088 | tf_op jit(solution)/shard_map/ppermute | solution.py:41
  145.4 10.4 %copy-start.18 = (bf16[128,2560]{1,0:T(8,128)(2,1)}, bf16[128,2560]{1,0:T(8,128)(2,1)S(1)}, u32[]{:S(2)}) copy-start(bf16[128,2560]{1,0:T(8,128)(2,1)S(1)} %collective-permute-done.20.refs_6_) | copy-start | bytes 1966084
  145.4 8.5 %collective-permute-start.24 = (bf16[128,2560]{1,0:T(8,128)(2,1)S(1)}, bf16[128,2560]{1,0:T(8,128)(2,1)S(1)}, u32[]{:S(2)}, u32[]{:S(2)}) collective-permute-start(bf16[128,2560]{1,0:T(8,128)(2,1)S(1)} %collective-permute-done.20.refs_6_), channel_id=1, source_target_pairs={{1,0},{0,1},{3,2},{2,3},{5,4},{4,5},{7,6},{6,7},{9,8},{8,9},{11,10... | collective-permute-start | bytes 1966088 | tf_op jit(solution)/shard_map/ppermute | solution.py:41
  145.8 10.0 %copy-start.19 = (bf16[128,2560]{1,0:T(8,128)(2,1)}, bf16[128,2560]{1,0:T(8,128)(2,1)S(1)}, u32[]{:S(2)}) copy-start(bf16[128,2560]{1,0:T(8,128)(2,1)S(1)} %collective-permute-done.21.refs_7_) | copy-start | bytes 1966084
  145.8 8.3 %collective-permute-start.25 = (bf16[128,2560]{1,0:T(8,128)(2,1)S(1)}, bf16[128,2560]{1,0:T(8,128)(2,1)S(1)}, u32[]{:S(2)}, u32[]{:S(2)}) collective-permute-start(bf16[128,2560]{1,0:T(8,128)(2,1)S(1)} %collective-permute-done.21.refs_7_), channel_id=1, source_target_pairs={{1,0},{0,1},{3,2},{2,3},{5,4},{4,5},{7,6},{6,7},{9,8},{8,9},{11,10... | collective-permute-start | bytes 1966088 | tf_op jit(solution)/shard_map/ppermute | solution.py:41
  149.3 6.6 %copy-start.20 = (bf16[128,2560]{1,0:T(8,128)(2,1)}, bf16[128,2560]{1,0:T(8,128)(2,1)S(1)}, u32[]{:S(2)}) copy-start(bf16[128,2560]{1,0:T(8,128)(2,1)S(1)} %collective-permute-done.26.refs_12_) | copy-start | bytes 1966084
  149.3 22.2 %collective-permute-start.16 = (bf16[128,1024]{1,0:T(8,128)(2,1)}, bf16[128,1024]{1,0:T(8,128)(2,1)S(1)}, u32[]{:S(2)}, u32[]{:S(2)}) collective-permute-start(bf16[128,1024]{1,0:T(8,128)(2,1)} %get-tuple-element.24), channel_id=1, source_target_pairs={{96,0},{97,1},{98,2},{99,3},{100,4},{101,5},{102,6},{103,7},{104,8... | collective-permute-start | bytes 786440 | tf_op jit(solution)/shard_map/ppermute | solution.py:41
  150.7 5.2 %copy-start.21 = (bf16[128,2560]{1,0:T(8,128)(2,1)}, bf16[128,2560]{1,0:T(8,128)(2,1)S(1)}, u32[]{:S(2)}) copy-start(bf16[128,2560]{1,0:T(8,128)(2,1)S(1)} %collective-permute-done.27.refs_13_) | copy-start | bytes 1966084
  150.7 20.9 %collective-permute-start.17 = (bf16[128,1024]{1,0:T(8,128)(2,1)}, bf16[128,1024]{1,0:T(8,128)(2,1)S(1)}, u32[]{:S(2)}, u32[]{:S(2)}) collective-permute-start(bf16[128,1024]{1,0:T(8,128)(2,1)} %get-tuple-element.25), channel_id=1, source_target_pairs={{32,0},{33,1},{34,2},{35,3},{36,4},{37,5},{38,6},{39,7},{40,8},{41... | collective-permute-start | bytes 786440 | tf_op jit(solution)/shard_map/ppermute | solution.py:41
  153.9 2.0 copy-start.22
  153.9 19.4 %collective-permute-start.18 = (bf16[128,1024]{1,0:T(8,128)(2,1)}, bf16[128,1024]{1,0:T(8,128)(2,1)S(1)}, u32[]{:S(2)}, u32[]{:S(2)}) collective-permute-start(bf16[128,1024]{1,0:T(8,128)(2,1)} %get-tuple-element.26), channel_id=1, source_target_pairs={{64,0},{65,1},{66,2},{67,3},{68,4},{69,5},{70,6},{71,7},{72,8},{73... | collective-permute-start | bytes 786440 | tf_op jit(solution)/shard_map/ppermute | solution.py:41
  154.2 1.8 copy-start.23
  154.2 23.5 %collective-permute-start.19 = (bf16[128,1024]{1,0:T(8,128)(2,1)}, bf16[128,1024]{1,0:T(8,128)(2,1)S(1)}, u32[]{:S(2)}, u32[]{:S(2)}) collective-permute-start(bf16[128,1024]{1,0:T(8,128)(2,1)} %get-tuple-element.27), channel_id=1, source_target_pairs={{48,0},{49,1},{50,2},{51,3},{52,4},{53,5},{54,6},{55,7},{56,8},{57... | collective-permute-start | bytes 786440 | tf_op jit(solution)/shard_map/ppermute | solution.py:41
  155.9 1.1 copy-start.9
  157.0 40.2 %copy-start.1 = (bf16[128,1024]{1,0:T(8,128)(2,1)S(1)}, bf16[128,1024]{1,0:T(8,128)(2,1)}, u32[]{:S(2)}) copy-start(bf16[128,1024]{1,0:T(8,128)(2,1)} %student.1) | copy-start | bytes 786436
  157.0 47.0 %copy-start.4 = (f32[128,1024]{1,0:T(8,128)S(1)}, f32[128,1024]{1,0:T(8,128)}, u32[]{:S(2)}) copy-start(f32[128,1024]{1,0:T(8,128)} %get-tuple-element.22) | copy-start | bytes 1572868
  169.2 11.9 %collective-permute-start.28 = (bf16[128,1024]{1,0:T(8,128)(2,1)}, bf16[128,1024]{1,0:T(8,128)(2,1)S(1)}, u32[]{:S(2)}, u32[]{:S(2)}) collective-permute-start(bf16[128,1024]{1,0:T(8,128)(2,1)} %get-tuple-element.29), channel_id=1, source_target_pairs={{80,0},{81,1},{82,2},{83,3},{84,4},{85,5},{86,6},{87,7},{88,8},{89... | collective-permute-start | bytes 786440 | tf_op jit(solution)/shard_map/ppermute | solution.py:41
  171.6 11.8 %collective-permute-start.29 = (bf16[128,1024]{1,0:T(8,128)(2,1)}, bf16[128,1024]{1,0:T(8,128)(2,1)S(1)}, u32[]{:S(2)}, u32[]{:S(2)}) collective-permute-start(bf16[128,1024]{1,0:T(8,128)(2,1)} %get-tuple-element.30), channel_id=1, source_target_pairs={{81,0},{80,1},{83,2},{82,3},{85,4},{84,5},{87,6},{86,7},{89,8},{88... | collective-permute-start | bytes 786440 | tf_op jit(solution)/shard_map/ppermute | solution.py:41
  171.6 13.7 %collective-permute-start.30 = (bf16[128,1024]{1,0:T(8,128)(2,1)}, bf16[128,1024]{1,0:T(8,128)(2,1)S(1)}, u32[]{:S(2)}, u32[]{:S(2)}) collective-permute-start(bf16[128,1024]{1,0:T(8,128)(2,1)} %get-tuple-element.31), channel_id=1, source_target_pairs={{28,0},{29,1},{30,2},{31,3},{24,4},{25,5},{26,6},{27,7},{20,8},{21... | collective-permute-start | bytes 786440 | tf_op jit(solution)/shard_map/ppermute | solution.py:41
  173.3 15.8 %collective-permute-start.31 = (bf16[128,1024]{1,0:T(8,128)(2,1)}, bf16[128,1024]{1,0:T(8,128)(2,1)S(1)}, u32[]{:S(2)}, u32[]{:S(2)}) collective-permute-start(bf16[128,1024]{1,0:T(8,128)(2,1)} %get-tuple-element.32), channel_id=1, source_target_pairs={{29,0},{28,1},{31,2},{30,3},{25,4},{24,5},{27,6},{26,7},{21,8},{20... | collective-permute-start | bytes 786440 | tf_op jit(solution)/shard_map/ppermute | solution.py:41
  177.6 18.0 %collective-permute-start.32 = (bf16[128,1024]{1,0:T(8,128)(2,1)}, bf16[128,1024]{1,0:T(8,128)(2,1)S(1)}, u32[]{:S(2)}, u32[]{:S(2)}) collective-permute-start(bf16[128,1024]{1,0:T(8,128)(2,1)} %get-tuple-element.33), channel_id=1, source_target_pairs={{30,0},{31,1},{24,2},{25,3},{26,4},{27,5},{28,6},{29,7},{22,8},{23... | collective-permute-start | bytes 786440 | tf_op jit(solution)/shard_map/ppermute | solution.py:41
  181.2 18.9 %collective-permute-start.33 = (bf16[128,1024]{1,0:T(8,128)(2,1)}, bf16[128,1024]{1,0:T(8,128)(2,1)S(1)}, u32[]{:S(2)}, u32[]{:S(2)}) collective-permute-start(bf16[128,1024]{1,0:T(8,128)(2,1)} %get-tuple-element.34), channel_id=1, source_target_pairs={{4,0},{5,1},{6,2},{7,3},{0,4},{1,5},{2,6},{3,7},{12,8},{13,9},{14,... | collective-permute-start | bytes 786440 | tf_op jit(solution)/shard_map/ppermute | solution.py:41
  183.3 16.7 %collective-permute-start.34 = (bf16[128,1024]{1,0:T(8,128)(2,1)}, bf16[128,1024]{1,0:T(8,128)(2,1)S(1)}, u32[]{:S(2)}, u32[]{:S(2)}) collective-permute-start(bf16[128,1024]{1,0:T(8,128)(2,1)} %get-tuple-element.35), channel_id=1, source_target_pairs={{112,0},{113,1},{114,2},{115,3},{116,4},{117,5},{118,6},{119,7},{1... | collective-permute-start | bytes 786440 | tf_op jit(solution)/shard_map/ppermute | solution.py:41
  185.3 15.5 %collective-permute-start.35 = (bf16[128,1024]{1,0:T(8,128)(2,1)}, bf16[128,1024]{1,0:T(8,128)(2,1)S(1)}, u32[]{:S(2)}, u32[]{:S(2)}) collective-permute-start(bf16[128,1024]{1,0:T(8,128)(2,1)} %get-tuple-element.36), channel_id=1, source_target_pairs={{24,0},{25,1},{26,2},{27,3},{28,4},{29,5},{30,6},{31,7},{16,8},{17... | collective-permute-start | bytes 786440 | tf_op jit(solution)/shard_map/ppermute | solution.py:41
  189.0 11.8 %collective-permute-start.36 = (bf16[128,1024]{1,0:T(8,128)(2,1)}, bf16[128,1024]{1,0:T(8,128)(2,1)S(1)}, u32[]{:S(2)}, u32[]{:S(2)}) collective-permute-start(bf16[128,1024]{1,0:T(8,128)(2,1)} %get-tuple-element.37), channel_id=1, source_target_pairs={{2,0},{3,1},{4,2},{5,3},{6,4},{7,5},{0,6},{1,7},{10,8},{11,9},{12,... | collective-permute-start | bytes 786440 | tf_op jit(solution)/shard_map/ppermute | solution.py:41
  195.6 8.3 %collective-permute-start.37 = (bf16[128,1024]{1,0:T(8,128)(2,1)}, bf16[128,1024]{1,0:T(8,128)(2,1)S(1)}, u32[]{:S(2)}, u32[]{:S(2)}) collective-permute-start(bf16[128,1024]{1,0:T(8,128)(2,1)} %get-tuple-element.38), channel_id=1, source_target_pairs={{16,0},{17,1},{18,2},{19,3},{20,4},{21,5},{22,6},{23,7},{24,8},{25... | collective-permute-start | bytes 786440 | tf_op jit(solution)/shard_map/ppermute | solution.py:41

commit v2 on v1

v2 whole, which is shorter than its diff:
```python
import functools
import itertools
import math

import jax
import jax.numpy as jnp
from jax import lax
from jax.experimental import pallas as pl
from jax.experimental.pallas import tpu as pltpu
from jax.sharding import PartitionSpec as P

ROWS = 128
DS, DT = 1024, 4096
WIDE = DS + DT
HALF = WIDE // 2
PM = 2
SCALE_S, SCALE_T = math.sqrt(DS), math.sqrt(DT)

LAYOUT_1 = ["000s", "000o", "001o", "003o", "030o", "300o", "300s", "010o", "010s"]
GROUPS_1 = [("000", [["000o"], ["001o"]]), ("300", [["000o", "001o", "003o", "030o"]]),
            ("010", [["000o", "001o", "003o", "030o", "300o"]])]
LAYOUT_2 = ["000s", "000o", "010o", "010s", "300o", "300s", "200o", "200s",
            "030o", "003o", "001o", "002o", "031o", "033o", "110o", "110s"]
GROUPS_2 = [("000", [["002o"], ["200o"]]), ("010", [["002o", "031o"]]), ("300", [["002o", "031o", "033o", "110o"]]),
            ("200", [["001o", "002o", "031o", "033o"]]), ("110", [["030o", "003o", "001o", "002o", "031o", "033o"]])]
LAYOUT_3 = ["032o", "032s", "010o", "300o", "110o", "200o", "210o", "210s", "030o", "031o"]
GROUPS_3 = [("032", [["010o", "300o", "110o", "200o", "210o"]]), ("210", [["030o", "031o"]])]


def offset(name):
    return tuple(int(t) for t in name[:3])


def fetch(block, distance, flip=False):
    dx, dy, dz = distance
    pairs = []
    for z, low, high, x, core in itertools.product(range(4), range(2), range(2), range(4), range(2)):
        y = (2 * high + low + dy) % 4
        source = ((((z + dz) % 4 * 2 + y % 2) * 2 + y // 2) * 4 + (x + dx) % 4) * 2 + (core ^ int(flip))
        target = (((z * 2 + low) * 2 + high) * 4 + x) * 2 + core
        pairs.append((source, target))
    return lax.ppermute(block, ("chip", "core"), pairs)


def swap(block):
    return fetch(block, (0, 0, 0), True)


def sibling(block):
    both = lax.all_gather(block, "core", axis=0, tiled=True)
    return lax.dynamic_slice_in_dim(both, (1 - lax.axis_index("core")) * ROWS, ROWS)


def give(block, name):
    return fetch(block, tuple(-t for t in offset(name)), name[3] == "s")


def unit_kernel(student, teacher, out):
    for source, first, width in ((student, 0, DS), (teacher, DS, DT)):
        wide = source[...].astype(jnp.float32)
        recip = 1.0 / jnp.sqrt(jnp.sum(wide * wide, axis=1, keepdims=True) + 1e-06)
        out[:, first : first + width] = (wide * recip).astype(jnp.bfloat16)


def unit_rows(student, teacher):
    return pl.pallas_call(
        unit_kernel,
        out_shape=jax.ShapeDtypeStruct((ROWS, WIDE), jnp.bfloat16),
        in_specs=[pl.BlockSpec(memory_space=pltpu.VMEM)] * 2,
        out_specs=pl.BlockSpec(memory_space=pltpu.VMEM),
        compiler_params=pltpu.CompilerParams(vmem_limit_bytes=16 << 20),
        name="unit_rows",
    )(student, teacher)


def involution(one, two):
    return all((2 * (s - t)) % 4 == 0 for s, t in zip(offset(one), offset(two)))


def phase_kernel(layout, groups, pieces, starts, adds, outs, *refs):
    at = {name: i * ROWS for i, name in enumerate(layout)}
    refs = list(refs)
    block_refs = [refs.pop(0) for _ in pieces]
    start_refs = [refs.pop(0) for _ in starts]
    add_ref = refs.pop(0) if adds else None
    out_refs = [refs.pop(0) for _ in outs]
    sums, weight = refs
    blocks = {}
    for (name, first), ref in zip(pieces, block_refs):
        blocks.setdefault(name, []).append((first, ref))
    so_far = {}
    for names, ref in zip(starts, start_refs):
        for i, name in enumerate(names):
            so_far[name] = ref.at[pl.ds(i * ROWS, ROWS), :]

    def read(names, first, width):
        rows = []
        for name in names:
            parts = []
            for start, ref in sorted(blocks[name], key=lambda item: item[0]):
                low, high = max(first, start), min(first + width, start + ref.shape[1])
                if low < high:
                    parts.append(ref[:, low - start : high - start])
            rows.append(parts[0] if len(parts) == 1 else jnp.concatenate(parts, axis=1))
        return rows[0] if len(rows) == 1 else jnp.concatenate(rows, axis=0)

    touched = set()

    def put(names, value):
        for i, name in enumerate(names):
            rows = pl.ds(at[name], ROWS)
            part = value[i * ROWS : (i + 1) * ROWS]
            if name in touched:
                sums[rows, :] += part
            elif name in so_far:
                sums[rows, :] = part + so_far[name][...]
            else:
                sums[rows, :] = part
            touched.add(name)

    nt = (((1,), (1,)), ((), ()))
    tn = (((0,), (0,)), ((), ()))
    halves = [sorted([a + "o", a + "s"], key=at.get) for a, _ in groups]
    for number, (a, runs) in enumerate(groups):
        both = halves[number]
        columns = pl.ds(number * 2 * ROWS, 2 * ROWS)
        for run in runs:
            for i in range(0, len(run), PM):
                piece = run[i : i + PM]
                gram_s = lax.dot_general(
                    read(piece, 0, DS), read(both, 0, DS), nt, preferred_element_type=jnp.float32
                )
                gram_t = lax.dot_general(
                    read(piece, DS, DT), read(both, DS, DT), nt, preferred_element_type=jnp.float32
                )
                for j, name in enumerate(piece):
                    squash_s = jnp.tanh(SCALE_S * gram_s[j * ROWS : (j + 1) * ROWS])
                    squash_t = jnp.tanh(SCALE_T * gram_t[j * ROWS : (j + 1) * ROWS])
                    value = (squash_s - squash_t) * SCALE_S * (1.0 - squash_s * squash_s)
                    if name[:3] != a and involution(a, name):
                        value = 0.5 * value
                    weight[pl.ds(at[name], ROWS), columns] = value.astype(jnp.bfloat16)
            if run[0][:3] != a:
                put(both, lax.dot_general(
                    weight[pl.ds(at[run[0]], len(run) * ROWS), columns], read(run, 0, DS), tn,
                    preferred_element_type=jnp.float32,
                ))
    met = {}
    for number, (a, runs) in enumerate(groups):
        for run in runs:
            for name in run:
                met.setdefault(name, []).append(number)
    merged = []
    for name in sorted(met, key=at.get):
        if merged and met[merged[-1][-1]] == met[name] and at[merged[-1][-1]] + ROWS == at[name]:
            merged[-1].append(name)
        else:
            merged.append([name])
    for run in merged:
        first, last = met[run[0]][0], met[run[0]][-1] + 1
        put(run, jnp.dot(
            weight[pl.ds(at[run[0]], len(run) * ROWS), pl.ds(first * 2 * ROWS, (last - first) * 2 * ROWS)],
            read(sum(halves[first:last], []), 0, DS), preferred_element_type=jnp.float32,
        ))
    for names, ref in zip(outs, out_refs):
        for i, name in enumerate(names):
            value = sums[pl.ds(at[name], ROWS), :] if name in touched else so_far[name][...]
            if name in adds:
                value = value + add_ref[pl.ds(adds.index(name) * ROWS, ROWS), :].astype(jnp.float32)
            ref[pl.ds(i * ROWS, ROWS), :] = value.astype(ref.dtype)


def phase(name, layout, groups, blocks, starts, adds, outs):
    pairs = sum(len(run) for _, runs in groups for run in runs)
    shapes = [jax.ShapeDtypeStruct((len(names) * ROWS, DS), kind) for names, kind in outs]
    operands = [array for _, _, array in blocks] + [array for _, array in starts]
    if adds:
        operands.append(adds[1])
    return pl.pallas_call(
        functools.partial(
            phase_kernel, layout, groups, [(n, f) for n, f, _ in blocks], [names for names, _ in starts],
            adds[0] if adds else [], [names for names, _ in outs],
        ),
        out_shape=shapes,
        in_specs=[pl.BlockSpec(memory_space=pltpu.VMEM)] * len(operands),
        out_specs=[pl.BlockSpec(memory_space=pltpu.VMEM)] * len(shapes),
        scratch_shapes=[
            pltpu.VMEM((len(layout) * ROWS, DS), jnp.float32),
            pltpu.VMEM((len(layout) * ROWS, len(groups) * 2 * ROWS), jnp.bfloat16),
        ],
        compiler_params=pltpu.CompilerParams(vmem_limit_bytes=20 << 20),
        cost_estimate=pl.CostEstimate(
            flops=pairs * 2 * ROWS * 2 * ROWS * (WIDE + 2 * DS) * 2,
            bytes_accessed=sum(x.size * x.dtype.itemsize for x in operands), transcendentals=0,
        ),
        name=name,
    )(*operands)


def after(value, *others):
    return lax.optimization_barrier((value, *others))[0]


def local(student, teacher):
    own = unit_rows(student, teacher)
    f32, bf16 = jnp.float32, jnp.bfloat16
    got = {"000o": own, "000s": sibling(own)}
    for name in ("010o", "300o", "030o", "003o", "001o"):
        got[name] = fetch(own, offset(name))
    for a in ("010", "300"):
        got[a + "s"] = swap(after(got[a + "o"], got["001o"], got["000s"]))
    got["110o"] = fetch(got["010o"], (1, 0, 0))
    got["200o"] = fetch(got["300o"], (3, 0, 0))
    got["031o"] = fetch(got["030o"], (0, 0, 1))
    middle = after(got["003o"], got["010s"], got["300s"])
    got["033o"] = fetch(middle, (0, 3, 0))
    got["002o"] = fetch(middle, (0, 0, 3))

    rows = lambda layout: [(name, 0, got[name]) for name in layout if name in got]
    names_1 = ["000s", "000o", "001o", "003o", "030o", "300o", "300s", "010o", "010s"]
    (sums_1,) = phase("phase_1", LAYOUT_1, GROUPS_1, rows(LAYOUT_1), [], None, [(names_1, f32)])

    got, sums_1 = lax.optimization_barrier((got, sums_1))
    for a in ("110", "200"):
        got[a + "s"] = swap(got[a + "o"])
    late = {
        ("210o", HALF): fetch(got["110o"][:, HALF:], (1, 0, 0)),
        ("210o", 0): fetch(got["200o"][:, :HALF], (0, 1, 0)),
        ("032o", 0): fetch(got["031o"][:, :HALF], (0, 0, 1)),
        ("032o", HALF): fetch(after(got["033o"], got["110s"], got["200s"])[:, HALF:], (0, 0, 3)),
    }
    names_s = ["000s", "010s", "300s", "110s", "200s"]
    names_2 = ["010o", "300o", "110o", "200o", "030o", "031o"]
    early = ["001o", "003o", "033o", "002o"]
    siblings, sums_2, home, *done = phase(
        "phase_2", LAYOUT_2, GROUPS_2, rows(LAYOUT_2), [(names_1, sums_1)], None,
        [(names_s, bf16), (names_2, f32), (["000o"], f32)] + [([name], bf16) for name in early],
    )
    *arrays, siblings, sums_2, home = lax.optimization_barrier((*late.values(), siblings, sums_2, home))
    late = dict(zip(late, arrays))
    for (name, first), array in list(late.items()):
        late[name[:3] + "s", first] = swap(array)
    siblings = swap(siblings)
    back = [give(value, name) for name, value in zip(early, done)]

    near = ["010o", "300o", "030o", "200o"]
    crossing, sum_032, sum_210, sum_031, sum_110, *done = phase(
        "phase_3", LAYOUT_3, GROUPS_3, rows(LAYOUT_3) + [(name, first, array) for (name, first), array in late.items()],
        [(names_2, sums_2)], (["none", "010o", "300o", "110o", "200o"], siblings),
        [(["032s", "210s"], bf16)] + [([name], f32) for name in ("032o", "210o", "031o", "110o")]
        + [([name], bf16) for name in near],
    )
    crossing, back[0], back[1] = lax.optimization_barrier((crossing, back[0], back[1]))
    crossing = swap(crossing).astype(f32)
    to_031 = fetch((sum_032 + crossing[:ROWS]).astype(bf16), (0, 0, 3))
    to_110 = fetch((sum_210 + crossing[ROWS:]).astype(bf16), (3, 0, 0))
    back += [give(value, name) for name, value in zip(near, done)]
    back.append(give((sum_031 + to_031.astype(f32)).astype(bf16), "031o"))
    back.append(give((sum_110 + to_110.astype(f32)).astype(bf16), "110o"))

    summed = home + siblings[:ROWS].astype(f32)
    for value in back:
        summed = summed + value.astype(f32)
    wide = student.astype(f32)
    recip = 1.0 / jnp.sqrt(jnp.sum(wide * wide, axis=1, keepdims=True) + 1e-06)
    unit_f = wide * recip
    dunit = (4.0 * DS / math.sqrt(16384)) * summed
    inner = jnp.sum(dunit * unit_f, axis=1, keepdims=True)
    return recip * (dunit - inner * unit_f)


def solution(mesh):
    cores = jax.sharding.Mesh(mesh.devices.reshape(-1, 2), ("chip", "core"))
    spec = P(("chip", "core"), None)
    return jax.shard_map(local, mesh=cores, in_specs=(spec, spec), out_specs=spec, check_vma=False)
```

time: 207 us -> 163 us (0.79)
  waiting for transfers between devices: 98.3 us -> 69.6 us
  Pallas kernels: 52 us -> 33.9 us
  between operations: 0.31 us -> 13.6 us
  starting transfers between devices: 48.7 us -> 38.9 us
    ppermute x38 -> x36, waiting for transfers between devices: 98.3 us -> 61.7 us  [fetch(): return lax.ppermute(block, ('chip', 'core'), pairs)]
    pallas_call x3, Pallas kernels: 51.5 us -> 32.4 us  [phase(): pl.pallas_call(functools.partial(phase_kernel, layout, groups, [(n, f) fo...]
    ppermute x38 -> x36, starting transfers between devices: 48.7 us -> 38.9 us  [fetch(): return lax.ppermute(block, ('chip', 'core'), pairs)]
    all_gather x0 -> x1, waiting for transfers between devices: none -> 7.94 us  [sibling(): both = lax.all_gather(block, 'core', axis=0, tiled=True)]
    unnamed x48 -> x6, local copies, waits for them, and re-layouts: 4.34 us -> 2.18 us
  transfers between devices with their start and end apart: 38 -> 37, of which waited for: 14 -> 18; matrix products, arithmetic and copies ran while one was open for 0% -> 1% of each run, Pallas kernels for 25% -> 20%
where the time goes in v2:
time: 163 us; the launch traced here: 162 us
  waiting for transfers between devices  69.6 us (43%)
  starting transfers between devices  38.9 us (24%)
  Pallas kernels  33.9 us (21%)
  between operations  13.6 us (8%)
  local copies, waits for them, and re-layouts  3.75 us (2%)
  other arithmetic  2.09 us (1%)
    ppermute x36, waiting for transfers between devices, fetch(): return lax.ppermute(block, ('chip', 'core'), pairs)  61.7 us
    ppermute x36, starting transfers between devices, fetch(): return lax.ppermute(block, ('chip', 'core'), pairs)  38.9 us
    pallas_call x3, Pallas kernels, phase(): pl.pallas_call(functools.partial(phase_kernel, layout, groups, [(n, f) fo...  32.4 us
    all_gather x1, waiting for transfers between devices, sibling(): both = lax.all_gather(block, 'core', axis=0, tiled=True)  7.94 us
  transfers between devices with their start and end apart: 37, of which 18 were waited for; matrix products, arithmetic and copies ran while one was open for 1% of the time, Pallas kernels for 20%

profile of v2, /device:TPU:0, one launch (start us, length us, event | category | flops | bytes accessed | tf_op | source)
XLA Modules:
  0.0 161.9 jit_solution(4544475520157944441)
XLA Ops:
  6.5 0.9 copy-done
  7.5 1.2 copy-done.2
  8.7 1.5 unit_rows.1.refs_1_
  10.3 0.0 all-gather.2.cloned.1.call-update
  10.3 4.2 %collective-permute-start = (bf16[128,5120]{1,0:T(8,128)(2,1)}, bf16[128,5120]{1,0:T(8,128)(2,1)}, u32[]{:S(2)}, u32[]{:S(2)}) collective-permute-start(bf16[128,5120]{1,0:T(8,128)(2,1)} %unit_rows.1.refs_1_), channel_id=1, source_target_pairs={{32,0},{33,1},{34,2},{35,3},{36,4},{37,5},{38,6},{39,7},{40,8},{41... | collective-permute-start | bytes 3932168 | tf_op jit(solution)/shard_map/ppermute | solution.py:42
  14.5 1.5 collective-permute-start.4
  16.0 3.0 %collective-permute-start.2 = (bf16[128,5120]{1,0:T(8,128)(2,1)}, bf16[128,5120]{1,0:T(8,128)(2,1)S(1)}, u32[]{:S(2)}, u32[]{:S(2)}) collective-permute-start(bf16[128,5120]{1,0:T(8,128)(2,1)} %unit_rows.1.refs_1_), channel_id=1, source_target_pairs={{16,0},{17,1},{18,2},{19,3},{20,4},{21,5},{22,6},{23,7},{24,8},{25... | collective-permute-start | bytes 3932168 | tf_op jit(solution)/shard_map/ppermute | solution.py:42
  19.0 7.9 %all-gather.2.cloned.1.call-done = bf16[256,5120]{1,0:T(8,128)(2,1)} async-done(((bf16[128,5120]{1,0:T(8,128)(2,1)}), bf16[256,5120]{1,0:T(8,128)(2,1)}) %all-gather.2.cloned.1.call-update) | async-done | bytes 2621456 | tf_op jit(solution)/shard_map/all_gather | solution.py:50
  26.9 1.4 constant_dynamic-slice_fusion.refs_0_
  28.3 14.5 %collective-permute-done.refs_2_.refs_10_ = bf16[128,5120]{1,0:T(8,128)(2,1)} collective-permute-done((bf16[128,5120]{1,0:T(8,128)(2,1)}, bf16[128,5120]{1,0:T(8,128)(2,1)}, u32[]{:S(2)}, u32[]{:S(2)}) %collective-permute-start) | collective-permute-done | bytes 1310752 | tf_op jit(solution)/shard_map/ppermute | solution.py:42
  42.8 3.3 %collective-permute-done.4.refs_5_.refs_4_.refs_1_ = bf16[128,5120]{1,0:T(8,128)(2,1)S(1)} collective-permute-done((bf16[128,5120]{1,0:T(8,128)(2,1)}, bf16[128,5120]{1,0:T(8,128)(2,1)S(1)}, u32[]{:S(2)}, u32[]{:S(2)}) %collective-permute-start.4) | collective-permute-done | bytes 1310752 | tf_op jit(solution)/shard_map/ppermute | solution.py:42
  46.1 0.6 collective-permute-done.2.refs_7_.refs_2_.refs_0_
  46.8 1.7 %collective-permute-start.10 = (bf16[128,5120]{1,0:T(8,128)(2,1)S(1)}, bf16[128,5120]{1,0:T(8,128)(2,1)S(1)}, u32[]{:S(2)}, u32[]{:S(2)}) collective-permute-start(bf16[128,5120]{1,0:T(8,128)(2,1)S(1)} %collective-permute-done.2.refs_7_.refs_2_.refs_0_), channel_id=1, source_target_pairs={{2,0},{3,1},{4,2},{5,3},{6,4},{7,5},{0,6},{1,7},{10,8},{11,9},{12,... | collective-permute-start | bytes 3932168 | tf_op jit(solution)/shard_map/ppermute | solution.py:42
  48.5 1.7 %collective-permute-done.1.refs_3_.refs_9_ = bf16[128,5120]{1,0:T(8,128)(2,1)} collective-permute-done((bf16[128,5120]{1,0:T(8,128)(2,1)}, bf16[128,5120]{1,0:T(8,128)(2,1)}, u32[]{:S(2)}, u32[]{:S(2)}) %collective-permute-start.1) | collective-permute-done | bytes 1310752 | tf_op jit(solution)/shard_map/ppermute | solution.py:42
  50.2 1.5 collective-permute-start.11
  51.7 1.5 collective-permute-start.8
  53.1 0.0 collective-permute-done.5.refs_6_.refs_5_
  53.1 0.0 collective-permute-done.3.refs_8_.refs_3_
  53.2 0.6 collective-permute-start.6
  53.7 11.0 %phase_1.1.refs_16_ = f32[1152,1024]{1,0:T(8,128)S(1)} custom-call(bf16[128,5120]{1,0:T(8,128)(2,1)S(1)} %constant_dynamic-slice_fusion.refs_0_, bf16[128,5120]{1,0:T(8,128)(2,1)} %unit_rows.1.refs_1_, bf16[128,5120]{1,0:T(8,128)(2,1)} %collective-permute-done.refs_2_.refs_10_, bf16[128,5120]{1,0:T(8,128)(2,1)} %collective-permute-done.1.refs_3_.refs_9_, ...), custom_call_target="tpu_custom_call" | custom-call | flops 10334765056 | bytes 11796480 | tf_op jit(solution)/shard_map/phase_1/pallas_call | solution.py:179
  64.7 13.3 %collective-permute-done.10.refs_14_.refs_2_ = bf16[128,5120]{1,0:T(8,128)(2,1)S(1)} collective-permute-done((bf16[128,5120]{1,0:T(8,128)(2,1)S(1)}, bf16[128,5120]{1,0:T(8,128)(2,1)S(1)}, u32[]{:S(2)}, u32[]{:S(2)}) %collective-permute-start.10) | collective-permute-done | bytes 1310752 | tf_op jit(solution)/shard_map/ppermute | solution.py:42
  78.0 2.7 %collective-permute-done.11.refs_6_.refs_3_ = bf16[128,5120]{1,0:T(8,128)(2,1)S(1)} collective-permute-done((bf16[128,5120]{1,0:T(8,128)(2,1)S(1)}, bf16[128,5120]{1,0:T(8,128)(2,1)S(1)}, u32[]{:S(2)}, u32[]{:S(2)}) %collective-permute-start.11) | collective-permute-done | bytes 1310752 | tf_op jit(solution)/shard_map/ppermute | solution.py:42
  80.7 2.6 %collective-permute-done.6.refs_11_ = bf16[128,5120]{1,0:T(8,128)(2,1)S(1)} collective-permute-done((bf16[128,5120]{1,0:T(8,128)(2,1)}, bf16[128,5120]{1,0:T(8,128)(2,1)S(1)}, u32[]{:S(2)}, u32[]{:S(2)}) %collective-permute-start.6) | collective-permute-done | bytes 1310752 | tf_op jit(solution)/shard_map/ppermute | solution.py:42
  83.3 0.1 collective-permute-done.9.refs_13_
  83.4 0.5 collective-permute-start.16
  84.0 2.6 %collective-permute-start.12 = (bf16[128,2560]{1,0:T(8,128)(2,1)S(1)}, bf16[128,2560]{1,0:T(8,128)(2,1)S(1)}, u32[]{:S(2)}, u32[]{:S(2)}) collective-permute-start(bf16[128,2560]{1,0:T(8,128)(2,1)S(1)} %slice.21), channel_id=1, source_target_pairs={{2,0},{3,1},{4,2},{5,3},{6,4},{7,5},{0,6},{1,7},{10,8},{11,9},{12,... | collective-permute-start | bytes 1966088 | tf_op jit(solution)/shard_map/ppermute | solution.py:42
  86.6 1.9 %collective-permute-start.13 = (bf16[128,2560]{1,0:T(8,128)(2,1)S(1)}, bf16[128,2560]{1,0:T(8,128)(2,1)S(1)}, u32[]{:S(2)}, u32[]{:S(2)}) collective-permute-start(bf16[128,2560]{1,0:T(8,128)(2,1)S(1)} %slice.22), channel_id=1, source_target_pairs={{16,0},{17,1},{18,2},{19,3},{20,4},{21,5},{22,6},{23,7},{24,8},{25... | collective-permute-start | bytes 1966088 | tf_op jit(solution)/shard_map/ppermute | solution.py:42
  88.6 1.8 %collective-permute-start.14 = (bf16[128,2560]{1,0:T(8,128)(2,1)S(1)}, bf16[128,2560]{1,0:T(8,128)(2,1)S(1)}, u32[]{:S(2)}, u32[]{:S(2)}) collective-permute-start(bf16[128,2560]{1,0:T(8,128)(2,1)S(1)} %slice.23), channel_id=1, source_target_pairs={{32,0},{33,1},{34,2},{35,3},{36,4},{37,5},{38,6},{39,7},{40,8},{41... | collective-permute-start | bytes 1966088 | tf_op jit(solution)/shard_map/ppermute | solution.py:42
  90.4 0.4 collective-permute-start.17
  90.8 15.1 %phase_2.1 = (bf16[640,1024]{1,0:T(8,128)(2,1)S(1)}, f32[768,1024]{1,0:T(8,128)S(1)}, f32[128,1024]{1,0:T(8,128)S(1)}, bf16[128,1024]{1,0:T(8,128)(2,1)S(1)}, bf...) custom-call(bf16[128,5120]{1,0:T(8,128)(2,1)S(1)} %constant_dynamic-slice_fusion.refs_0_, ...), custom_call_target="tpu_custom_call" | custom-call | flops 16911433728 | bytes 25690112 | tf_op jit(solution)/shard_map/phase_2/pallas_call | solution.py:179
  105.9 1.6 collective-permute-done.17.refs_9_
  107.5 0.5 collective-permute-start.19
  108.0 0.0 collective-permute-start.20
  108.0 0.5 collective-permute-start.21
  108.5 0.0 collective-permute-start.22
  108.6 2.9 %collective-permute-done.19.refs_10_ = bf16[128,2560]{1,0:T(8,128)(2,1)S(1)} collective-permute-done((bf16[128,2560]{1,0:T(8,128)(2,1)S(1)}, bf16[128,2560]{1,0:T(8,128)(2,1)S(1)}, u32[]{:S(2)}, u32[]{:S(2)}) %collective-permute-start.19) | collective-permute-done | bytes 655392 | tf_op jit(solution)/shard_map/ppermute | solution.py:42
  111.5 0.0 collective-permute-start.23
  111.5 0.9 collective-permute-done.20.refs_11_
  112.4 2.3 %collective-permute-start.24 = (bf16[128,1024]{1,0:T(8,128)(2,1)S(1)}, bf16[128,1024]{1,0:T(8,128)(2,1)S(1)}, u32[]{:S(2)}, u32[]{:S(2)}) collective-permute-start(bf16[128,1024]{1,0:T(8,128)(2,1)S(1)} %get-tuple-element.81), channel_id=1, source_target_pairs={{32,0},{33,1},{34,2},{35,3},{36,4},{37,5},{38,6},{39,7},{40,8},{41... | collective-permute-start | bytes 786440 | tf_op jit(solution)/shard_map/ppermute | solution.py:42
  114.8 6.3 %phase_3.1 = (bf16[256,1024]{1,0:T(8,128)(2,1)S(1)}, f32[128,1024]{1,0:T(8,128)S(1)}, f32[128,1024]{1,0:T(8,128)S(1)}, f32[128,1024]{1,0:T(8,128)S(1)}, f32[128,...) custom-call(bf16[128,5120]{1,0:T(8,128)(2,1)S(1)} %collective-permut, ...), custom_call_target="tpu_custom_call" | custom-call | flops 6576668672 | bytes 17563648 | tf_op jit(solution)/shard_map/phase_3/pallas_call | solution.py:179
  121.1 0.1 collective-permute-start.31
  121.2 1.9 %collective-permute-done.31 = bf16[256,1024]{1,0:T(8,128)(2,1)S(1)} collective-permute-done((bf16[256,1024]{1,0:T(8,128)(2,1)S(1)}, bf16[256,1024]{1,0:T(8,128)(2,1)S(1)}, u32[]{:S(2)}, u32[]{:S(2)}) %collective-permute-start.31) | collective-permute-done | bytes 524320 | tf_op jit(solution)/shard_map/ppermute | solution.py:42
  123.1 0.1 convert_element_type.67
  123.2 0.2 fusion.7
  123.4 0.0 copy-start.1
  123.4 0.1 collective-permute-start.32
  123.5 0.5 collective-permute-start.34
  124.0 4.7 %collective-permute-start.25 = (bf16[128,1024]{1,0:T(8,128)(2,1)S(1)}, bf16[128,1024]{1,0:T(8,128)(2,1)S(1)}, u32[]{:S(2)}, u32[]{:S(2)}) collective-permute-start(bf16[128,1024]{1,0:T(8,128)(2,1)S(1)} %get-tuple-element.84), channel_id=1, source_target_pairs={{48,0},{49,1},{50,2},{51,3},{52,4},{53,5},{54,6},{55,7},{56,8},{57... | collective-permute-start | bytes 786440 | tf_op jit(solution)/shard_map/ppermute | solution.py:42
  128.7 0.1 collective-permute-start.26
  128.9 4.1 %collective-permute-done.32 = bf16[128,1024]{1,0:T(8,128)(2,1)S(1)} collective-permute-done((bf16[128,1024]{1,0:T(8,128)(2,1)S(1)}, bf16[128,1024]{1,0:T(8,128)(2,1)S(1)}, u32[]{:S(2)}, u32[]{:S(2)}) %collective-permute-start.32) | collective-permute-done | bytes 262176 | tf_op jit(solution)/shard_map/ppermute | solution.py:42
  133.0 1.4 collective-permute-start.28
  134.5 0.1 add_convert_fusion.1
  134.5 2.0 %collective-permute-start.29 = (bf16[128,1024]{1,0:T(8,128)(2,1)S(1)}, bf16[128,1024]{1,0:T(8,128)(2,1)S(1)}, u32[]{:S(2)}, u32[]{:S(2)}) collective-permute-start(bf16[128,1024]{1,0:T(8,128)(2,1)S(1)} %get-tuple-element.88), channel_id=1, source_target_pairs={{16,0},{17,1},{18,2},{19,3},{20,4},{21,5},{22,6},{23,7},{24,8},{25... | collective-permute-start | bytes 786440 | tf_op jit(solution)/shard_map/ppermute | solution.py:42
  136.5 0.1 add_convert_fusion
  136.6 1.4 collective-permute-start.30
  138.0 1.7 %collective-permute-done.26 = bf16[128,1024]{1,0:T(8,128)(2,1)S(1)} collective-permute-done((bf16[128,1024]{1,0:T(8,128)(2,1)S(1)}, bf16[128,1024]{1,0:T(8,128)(2,1)S(1)}, u32[]{:S(2)}, u32[]{:S(2)}) %collective-permute-start.26) | collective-permute-done | bytes 262176 | tf_op jit(solution)/shard_map/ppermute | solution.py:42
  139.7 3.2 %collective-permute-start.33 = (bf16[128,1024]{1,0:T(8,128)(2,1)S(1)}, bf16[128,1024]{1,0:T(8,128)(2,1)S(1)}, u32[]{:S(2)}, u32[]{:S(2)}) collective-permute-start(bf16[128,1024]{1,0:T(8,128)(2,1)S(1)} %add_convert_fusion.1), channel_id=1, source_target_pairs={{112,0},{113,1},{114,2},{115,3},{116,4},{117,5},{118,6},{119,7},{1... | collective-permute-start | bytes 786440 | tf_op jit(solution)/shard_map/ppermute | solution.py:42
  142.9 0.7 collective-permute-start.35
  143.7 0.1 fusion.5
  143.8 1.3 collective-permute-done.30
  145.1 4.2 %collective-permute-done.33 = bf16[128,1024]{1,0:T(8,128)(2,1)S(1)} collective-permute-done((bf16[128,1024]{1,0:T(8,128)(2,1)S(1)}, bf16[128,1024]{1,0:T(8,128)(2,1)S(1)}, u32[]{:S(2)}, u32[]{:S(2)}) %collective-permute-start.33) | collective-permute-done | bytes 262176 | tf_op jit(solution)/shard_map/ppermute | solution.py:42
  149.3 4.2 %collective-permute-done.35 = bf16[128,1024]{1,0:T(8,128)(2,1)S(1)} collective-permute-done((bf16[128,1024]{1,0:T(8,128)(2,1)S(1)}, bf16[128,1024]{1,0:T(8,128)(2,1)S(1)}, u32[]{:S(2)}, u32[]{:S(2)}) %collective-permute-start.35) | collective-permute-done | bytes 262176 | tf_op jit(solution)/shard_map/ppermute | solution.py:42
  153.5 0.5 fusion.2
  154.0 1.0 fusion.4
  (34 shorter events, 0.3 us)
Async XLA Ops:
  6.5 20.4 %all-gather.2.cloned.1.call-start = ((), (), s32[]{:S(2)}) async-start(), calls=%async_computation | async-start | bytes 3932160 | tf_op jit(solution)/shard_map/all_gather | solution.py:50
  6.5 0.9 copy-start
  7.5 1.2 copy-start.2
  10.3 32.5 %collective-permute-start = (bf16[128,5120]{1,0:T(8,128)(2,1)}, bf16[128,5120]{1,0:T(8,128)(2,1)}, u32[]{:S(2)}, u32[]{:S(2)}) collective-permute-start(bf16[128,5120]{1,0:T(8,128)(2,1)} %unit_rows.1.refs_1_), channel_id=1, source_target_pairs={{32,0},{33,1},{34,2},{35,3},{36,4},{37,5},{38,6},{39,7},{40,8},{41... | collective-permute-start | bytes 3932168 | tf_op jit(solution)/shard_map/ppermute | solution.py:42
  14.5 31.7 %collective-permute-start.4 = (bf16[128,5120]{1,0:T(8,128)(2,1)}, bf16[128,5120]{1,0:T(8,128)(2,1)S(1)}, u32[]{:S(2)}, u32[]{:S(2)}) collective-permute-start(bf16[128,5120]{1,0:T(8,128)(2,1)} %unit_rows.1.refs_1_), channel_id=1, source_target_pairs={{6,0},{7,1},{0,2},{1,3},{2,4},{3,5},{4,6},{5,7},{14,8},{15,9},{8,1... | collective-permute-start | bytes 3932168 | tf_op jit(solution)/shard_map/ppermute | solution.py:42
  16.0 30.8 %collective-permute-start.2 = (bf16[128,5120]{1,0:T(8,128)(2,1)}, bf16[128,5120]{1,0:T(8,128)(2,1)S(1)}, u32[]{:S(2)}, u32[]{:S(2)}) collective-permute-start(bf16[128,5120]{1,0:T(8,128)(2,1)} %unit_rows.1.refs_1_), channel_id=1, source_target_pairs={{16,0},{17,1},{18,2},{19,3},{20,4},{21,5},{22,6},{23,7},{24,8},{25... | collective-permute-start | bytes 3932168 | tf_op jit(solution)/shard_map/ppermute | solution.py:42
  19.0 31.2 %collective-permute-start.1 = (bf16[128,5120]{1,0:T(8,128)(2,1)}, bf16[128,5120]{1,0:T(8,128)(2,1)}, u32[]{:S(2)}, u32[]{:S(2)}) collective-permute-start(bf16[128,5120]{1,0:T(8,128)(2,1)} %unit_rows.1.refs_1_), channel_id=1, source_target_pairs={{96,0},{97,1},{98,2},{99,3},{100,4},{101,5},{102,6},{103,7},{104,8... | collective-permute-start | bytes 3932168 | tf_op jit(solution)/shard_map/ppermute | solution.py:42
  19.0 32.7 %collective-permute-start.7 = (bf16[128,5120]{1,0:T(8,128)(2,1)}, bf16[128,5120]{1,0:T(8,128)(2,1)}, u32[]{:S(2)}, u32[]{:S(2)}) collective-permute-start(bf16[128,5120]{1,0:T(8,128)(2,1)} %unit_rows.1.refs_1_), channel_id=1, source_target_pairs={{24,0},{25,1},{26,2},{27,3},{28,4},{29,5},{30,6},{31,7},{16,8},{17... | collective-permute-start | bytes 3932168 | tf_op jit(solution)/shard_map/ppermute | solution.py:42
  46.1 7.0 %collective-permute-start.5 = (bf16[128,5120]{1,0:T(8,128)(2,1)S(1)}, bf16[128,5120]{1,0:T(8,128)(2,1)S(1)}, u32[]{:S(2)}, u32[]{:S(2)}) collective-permute-start(bf16[128,5120]{1,0:T(8,128)(2,1)S(1)} %collective-permute-done.4.refs_5_.refs_4_.refs_1_), channel_id=1, source_target_pairs={{1,0},{0,1},{3,2},{2,3},{5,4},{4,5},{7,6},{6,7},{9,8},{8,9},{11,10... | collective-permute-start | bytes 3932168 | tf_op jit(solution)/shard_map/ppermute | solution.py:42
  46.8 6.4 %collective-permute-start.3 = (bf16[128,5120]{1,0:T(8,128)(2,1)S(1)}, bf16[128,5120]{1,0:T(8,128)(2,1)S(1)}, u32[]{:S(2)}, u32[]{:S(2)}) collective-permute-start(bf16[128,5120]{1,0:T(8,128)(2,1)S(1)} %collective-permute-done.2.refs_7_.refs_2_.refs_0_), channel_id=1, source_target_pairs={{1,0},{0,1},{3,2},{2,3},{5,4},{4,5},{7,6},{6,7},{9,8},{8,9},{11,10... | collective-permute-start | bytes 3932168 | tf_op jit(solution)/shard_map/ppermute | solution.py:42
  46.8 31.2 %collective-permute-start.10 = (bf16[128,5120]{1,0:T(8,128)(2,1)S(1)}, bf16[128,5120]{1,0:T(8,128)(2,1)S(1)}, u32[]{:S(2)}, u32[]{:S(2)}) collective-permute-start(bf16[128,5120]{1,0:T(8,128)(2,1)S(1)} %collective-permute-done.2.refs_7_.refs_2_.refs_0_), channel_id=1, source_target_pairs={{2,0},{3,1},{4,2},{5,3},{6,4},{7,5},{0,6},{1,7},{10,8},{11,9},{12,... | collective-permute-start | bytes 3932168 | tf_op jit(solution)/shard_map/ppermute | solution.py:42
  50.2 30.5 %collective-permute-start.11 = (bf16[128,5120]{1,0:T(8,128)(2,1)S(1)}, bf16[128,5120]{1,0:T(8,128)(2,1)S(1)}, u32[]{:S(2)}, u32[]{:S(2)}) collective-permute-start(bf16[128,5120]{1,0:T(8,128)(2,1)S(1)} %collective-permute-done.4.refs_5_.refs_4_.refs_1_), channel_id=1, source_target_pairs={{6,0},{7,1},{0,2},{1,3},{2,4},{3,5},{4,6},{5,7},{14,8},{15,9},{8,1... | collective-permute-start | bytes 3932168 | tf_op jit(solution)/shard_map/ppermute | solution.py:42
  51.7 29.0 %collective-permute-start.8 = (bf16[128,5120]{1,0:T(8,128)(2,1)}, bf16[128,5120]{1,0:T(8,128)(2,1)S(1)}, u32[]{:S(2)}, u32[]{:S(2)}) collective-permute-start(bf16[128,5120]{1,0:T(8,128)(2,1)} %collective-permute-done.7.refs_4_.refs_8_), channel_id=1, source_target_pairs={{32,0},{33,1},{34,2},{35,3},{36,4},{37,5},{38,6},{39,7},{40,8},{41... | collective-permute-start | bytes 3932168 | tf_op jit(solution)/shard_map/ppermute | solution.py:42
  53.2 30.1 %collective-permute-start.6 = (bf16[128,5120]{1,0:T(8,128)(2,1)}, bf16[128,5120]{1,0:T(8,128)(2,1)S(1)}, u32[]{:S(2)}, u32[]{:S(2)}) collective-permute-start(bf16[128,5120]{1,0:T(8,128)(2,1)} %collective-permute-done.1.refs_3_.refs_9_), channel_id=1, source_target_pairs={{96,0},{97,1},{98,2},{99,3},{100,4},{101,5},{102,6},{103,7},{104,8... | collective-permute-start | bytes 3932168 | tf_op jit(solution)/shard_map/ppermute | solution.py:42
  53.7 29.7 %collective-permute-start.9 = (bf16[128,5120]{1,0:T(8,128)(2,1)}, bf16[128,5120]{1,0:T(8,128)(2,1)S(1)}, u32[]{:S(2)}, u32[]{:S(2)}) collective-permute-start(bf16[128,5120]{1,0:T(8,128)(2,1)} %collective-permute-done.1.refs_3_.refs_9_), channel_id=1, source_target_pairs={{24,0},{25,1},{26,2},{27,3},{28,4},{29,5},{30,6},{31,7},{16,8},{17... | collective-permute-start | bytes 3932168 | tf_op jit(solution)/shard_map/ppermute | solution.py:42
  83.4 7.0 %collective-permute-start.15 = (bf16[128,5120]{1,0:T(8,128)(2,1)S(1)}, bf16[128,5120]{1,0:T(8,128)(2,1)S(1)}, u32[]{:S(2)}, u32[]{:S(2)}) collective-permute-start(bf16[128,5120]{1,0:T(8,128)(2,1)S(1)} %collective-permute-done.10.refs_14_.refs_2_), channel_id=1, source_target_pairs={{1,0},{0,1},{3,2},{2,3},{5,4},{4,5},{7,6},{6,7},{9,8},{8,9},{11,10... | collective-permute-start | bytes 3932168 | tf_op jit(solution)/shard_map/ppermute | solution.py:42
  83.4 7.0 %collective-permute-start.16 = (bf16[128,5120]{1,0:T(8,128)(2,1)S(1)}, bf16[128,5120]{1,0:T(8,128)(2,1)S(1)}, u32[]{:S(2)}, u32[]{:S(2)}) collective-permute-start(bf16[128,5120]{1,0:T(8,128)(2,1)S(1)} %collective-permute-done.11.refs_6_.refs_3_), channel_id=1, source_target_pairs={{1,0},{0,1},{3,2},{2,3},{5,4},{4,5},{7,6},{6,7},{9,8},{8,9},{11,10... | collective-permute-start | bytes 3932168 | tf_op jit(solution)/shard_map/ppermute | solution.py:42
  84.0 21.9 %collective-permute-start.12 = (bf16[128,2560]{1,0:T(8,128)(2,1)S(1)}, bf16[128,2560]{1,0:T(8,128)(2,1)S(1)}, u32[]{:S(2)}, u32[]{:S(2)}) collective-permute-start(bf16[128,2560]{1,0:T(8,128)(2,1)S(1)} %slice.21), channel_id=1, source_target_pairs={{2,0},{3,1},{4,2},{5,3},{6,4},{7,5},{0,6},{1,7},{10,8},{11,9},{12,... | collective-permute-start | bytes 1966088 | tf_op jit(solution)/shard_map/ppermute | solution.py:42
  86.6 19.3 %collective-permute-start.13 = (bf16[128,2560]{1,0:T(8,128)(2,1)S(1)}, bf16[128,2560]{1,0:T(8,128)(2,1)S(1)}, u32[]{:S(2)}, u32[]{:S(2)}) collective-permute-start(bf16[128,2560]{1,0:T(8,128)(2,1)S(1)} %slice.22), channel_id=1, source_target_pairs={{16,0},{17,1},{18,2},{19,3},{20,4},{21,5},{22,6},{23,7},{24,8},{25... | collective-permute-start | bytes 1966088 | tf_op jit(solution)/shard_map/ppermute | solution.py:42
  88.6 17.3 %collective-permute-start.14 = (bf16[128,2560]{1,0:T(8,128)(2,1)S(1)}, bf16[128,2560]{1,0:T(8,128)(2,1)S(1)}, u32[]{:S(2)}, u32[]{:S(2)}) collective-permute-start(bf16[128,2560]{1,0:T(8,128)(2,1)S(1)} %slice.23), channel_id=1, source_target_pairs={{32,0},{33,1},{34,2},{35,3},{36,4},{37,5},{38,6},{39,7},{40,8},{41... | collective-permute-start | bytes 1966088 | tf_op jit(solution)/shard_map/ppermute | solution.py:42
  90.4 17.1 %collective-permute-start.17 = (bf16[128,2560]{1,0:T(8,128)(2,1)S(1)}, bf16[128,2560]{1,0:T(8,128)(2,1)S(1)}, u32[]{:S(2)}, u32[]{:S(2)}) collective-permute-start(bf16[128,2560]{1,0:T(8,128)(2,1)S(1)} %slice.24), channel_id=1, source_target_pairs={{96,0},{97,1},{98,2},{99,3},{100,4},{101,5},{102,6},{103,7},{104,8... | collective-permute-start | bytes 1966088 | tf_op jit(solution)/shard_map/ppermute | solution.py:42
  107.5 7.2 %collective-permute-start.18 = (bf16[640,1024]{1,0:T(8,128)(2,1)S(1)}, bf16[640,1024]{1,0:T(8,128)(2,1)S(1)}, u32[]{:S(2)}, u32[]{:S(2)}) collective-permute-start(bf16[640,1024]{1,0:T(8,128)(2,1)S(1)} %get-tuple-element.73), channel_id=1, source_target_pairs={{1,0},{0,1},{3,2},{2,3},{5,4},{4,5},{7,6},{6,7},{9,8},{8,9},{11,10... | collective-permute-start | bytes 3932168 | tf_op jit(solution)/shard_map/ppermute | solution.py:42
  107.5 4.0 %collective-permute-start.19 = (bf16[128,2560]{1,0:T(8,128)(2,1)S(1)}, bf16[128,2560]{1,0:T(8,128)(2,1)S(1)}, u32[]{:S(2)}, u32[]{:S(2)}) collective-permute-start(bf16[128,2560]{1,0:T(8,128)(2,1)S(1)} %collective-permute-done.12.refs_6_), channel_id=1, source_target_pairs={{1,0},{0,1},{3,2},{2,3},{5,4},{4,5},{7,6},{6,7},{9,8},{8,9},{11,10... | collective-permute-start | bytes 1966088 | tf_op jit(solution)/shard_map/ppermute | solution.py:42
  108.0 4.4 %collective-permute-start.20 = (bf16[128,2560]{1,0:T(8,128)(2,1)S(1)}, bf16[128,2560]{1,0:T(8,128)(2,1)S(1)}, u32[]{:S(2)}, u32[]{:S(2)}) collective-permute-start(bf16[128,2560]{1,0:T(8,128)(2,1)S(1)} %collective-permute-done.13.refs_7_), channel_id=1, source_target_pairs={{1,0},{0,1},{3,2},{2,3},{5,4},{4,5},{7,6},{6,7},{9,8},{8,9},{11,10... | collective-permute-start | bytes 1966088 | tf_op jit(solution)/shard_map/ppermute | solution.py:42
  108.0 6.7 %collective-permute-start.21 = (bf16[128,2560]{1,0:T(8,128)(2,1)S(1)}, bf16[128,2560]{1,0:T(8,128)(2,1)S(1)}, u32[]{:S(2)}, u32[]{:S(2)}) collective-permute-start(bf16[128,2560]{1,0:T(8,128)(2,1)S(1)} %collective-permute-done.14.refs_8_), channel_id=1, source_target_pairs={{1,0},{0,1},{3,2},{2,3},{5,4},{4,5},{7,6},{6,7},{9,8},{8,9},{11,10... | collective-permute-start | bytes 1966088 | tf_op jit(solution)/shard_map/ppermute | solution.py:42
  108.5 6.2 %collective-permute-start.22 = (bf16[128,2560]{1,0:T(8,128)(2,1)S(1)}, bf16[128,2560]{1,0:T(8,128)(2,1)S(1)}, u32[]{:S(2)}, u32[]{:S(2)}) collective-permute-start(bf16[128,2560]{1,0:T(8,128)(2,1)S(1)} %collective-permute-done.17.refs_9_), channel_id=1, source_target_pairs={{1,0},{0,1},{3,2},{2,3},{5,4},{4,5},{7,6},{6,7},{9,8},{8,9},{11,10... | collective-permute-start | bytes 1966088 | tf_op jit(solution)/shard_map/ppermute | solution.py:42
  111.5 9.6 %collective-permute-start.23 = (bf16[128,1024]{1,0:T(8,128)(2,1)S(1)}, bf16[128,1024]{1,0:T(8,128)(2,1)S(1)}, u32[]{:S(2)}, u32[]{:S(2)}) collective-permute-start(bf16[128,1024]{1,0:T(8,128)(2,1)S(1)} %get-tuple-element.80), channel_id=1, source_target_pairs={{96,0},{97,1},{98,2},{99,3},{100,4},{101,5},{102,6},{103,7},{104,8... | collective-permute-start | bytes 786440 | tf_op jit(solution)/shard_map/ppermute | solution.py:42
  112.4 8.6 %collective-permute-start.24 = (bf16[128,1024]{1,0:T(8,128)(2,1)S(1)}, bf16[128,1024]{1,0:T(8,128)(2,1)S(1)}, u32[]{:S(2)}, u32[]{:S(2)}) collective-permute-start(bf16[128,1024]{1,0:T(8,128)(2,1)S(1)} %get-tuple-element.81), channel_id=1, source_target_pairs={{32,0},{33,1},{34,2},{35,3},{36,4},{37,5},{38,6},{39,7},{40,8},{41... | collective-permute-start | bytes 786440 | tf_op jit(solution)/shard_map/ppermute | solution.py:42
  121.1 2.0 %collective-permute-start.31 = (bf16[256,1024]{1,0:T(8,128)(2,1)S(1)}, bf16[256,1024]{1,0:T(8,128)(2,1)S(1)}, u32[]{:S(2)}, u32[]{:S(2)}) collective-permute-start(bf16[256,1024]{1,0:T(8,128)(2,1)S(1)} %get-tuple-element.92), channel_id=1, source_target_pairs={{1,0},{0,1},{3,2},{2,3},{5,4},{4,5},{7,6},{6,7},{9,8},{8,9},{11,10... | collective-permute-start | bytes 1572872 | tf_op jit(solution)/shard_map/ppermute | solution.py:42
  123.4 20.3 %copy-start.1 = (bf16[128,1024]{1,0:T(8,128)(2,1)S(1)}, bf16[128,1024]{1,0:T(8,128)(2,1)}, u32[]{:S(2)}) copy-start(bf16[128,1024]{1,0:T(8,128)(2,1)} %student.1) | copy-start | bytes 786436
  123.4 9.6 %collective-permute-start.32 = (bf16[128,1024]{1,0:T(8,128)(2,1)S(1)}, bf16[128,1024]{1,0:T(8,128)(2,1)S(1)}, u32[]{:S(2)}, u32[]{:S(2)}) collective-permute-start(bf16[128,1024]{1,0:T(8,128)(2,1)S(1)} %get-tuple-element.97), channel_id=1, source_target_pairs={{96,0},{97,1},{98,2},{99,3},{100,4},{101,5},{102,6},{103,7},{104,8... | collective-permute-start | bytes 786440 | tf_op jit(solution)/shard_map/ppermute | solution.py:42
  123.5 11.1 %collective-permute-start.34 = (bf16[128,1024]{1,0:T(8,128)(2,1)S(1)}, bf16[128,1024]{1,0:T(8,128)(2,1)S(1)}, u32[]{:S(2)}, u32[]{:S(2)}) collective-permute-start(bf16[128,1024]{1,0:T(8,128)(2,1)S(1)} %get-tuple-element.98), channel_id=1, source_target_pairs={{6,0},{7,1},{0,2},{1,3},{2,4},{3,5},{4,6},{5,7},{14,8},{15,9},{8,1... | collective-permute-start | bytes 786440 | tf_op jit(solution)/shard_map/ppermute | solution.py:42
  124.0 12.5 %collective-permute-start.25 = (bf16[128,1024]{1,0:T(8,128)(2,1)S(1)}, bf16[128,1024]{1,0:T(8,128)(2,1)S(1)}, u32[]{:S(2)}, u32[]{:S(2)}) collective-permute-start(bf16[128,1024]{1,0:T(8,128)(2,1)S(1)} %get-tuple-element.84), channel_id=1, source_target_pairs={{48,0},{49,1},{50,2},{51,3},{52,4},{53,5},{54,6},{55,7},{56,8},{57... | collective-permute-start | bytes 786440 | tf_op jit(solution)/shard_map/ppermute | solution.py:42
  128.7 11.0 %collective-permute-start.26 = (bf16[128,1024]{1,0:T(8,128)(2,1)S(1)}, bf16[128,1024]{1,0:T(8,128)(2,1)S(1)}, u32[]{:S(2)}, u32[]{:S(2)}) collective-permute-start(bf16[128,1024]{1,0:T(8,128)(2,1)S(1)} %get-tuple-element.85), channel_id=1, source_target_pairs={{64,0},{65,1},{66,2},{67,3},{68,4},{69,5},{70,6},{71,7},{72,8},{73... | collective-permute-start | bytes 786440 | tf_op jit(solution)/shard_map/ppermute | solution.py:42
  128.9 14.1 %collective-permute-start.27 = (bf16[128,1024]{1,0:T(8,128)(2,1)S(1)}, bf16[128,1024]{1,0:T(8,128)(2,1)S(1)}, u32[]{:S(2)}, u32[]{:S(2)}) collective-permute-start(bf16[128,1024]{1,0:T(8,128)(2,1)S(1)} %get-tuple-element.86), channel_id=1, source_target_pairs={{24,0},{25,1},{26,2},{27,3},{28,4},{29,5},{30,6},{31,7},{16,8},{17... | collective-permute-start | bytes 786440 | tf_op jit(solution)/shard_map/ppermute | solution.py:42
  133.0 10.8 %collective-permute-start.28 = (bf16[128,1024]{1,0:T(8,128)(2,1)S(1)}, bf16[128,1024]{1,0:T(8,128)(2,1)S(1)}, u32[]{:S(2)}, u32[]{:S(2)}) collective-permute-start(bf16[128,1024]{1,0:T(8,128)(2,1)S(1)} %get-tuple-element.87), channel_id=1, source_target_pairs={{2,0},{3,1},{4,2},{5,3},{6,4},{7,5},{0,6},{1,7},{10,8},{11,9},{12,... | collective-permute-start | bytes 786440 | tf_op jit(solution)/shard_map/ppermute | solution.py:42
  134.5 9.3 %collective-permute-start.29 = (bf16[128,1024]{1,0:T(8,128)(2,1)S(1)}, bf16[128,1024]{1,0:T(8,128)(2,1)S(1)}, u32[]{:S(2)}, u32[]{:S(2)}) collective-permute-start(bf16[128,1024]{1,0:T(8,128)(2,1)S(1)} %get-tuple-element.88), channel_id=1, source_target_pairs={{16,0},{17,1},{18,2},{19,3},{20,4},{21,5},{22,6},{23,7},{24,8},{25... | collective-permute-start | bytes 786440 | tf_op jit(solution)/shard_map/ppermute | solution.py:42
  136.6 8.5 %collective-permute-start.30 = (bf16[128,1024]{1,0:T(8,128)(2,1)S(1)}, bf16[128,1024]{1,0:T(8,128)(2,1)S(1)}, u32[]{:S(2)}, u32[]{:S(2)}) collective-permute-start(bf16[128,1024]{1,0:T(8,128)(2,1)S(1)} %get-tuple-element.89), channel_id=1, source_target_pairs={{4,0},{5,1},{6,2},{7,3},{0,4},{1,5},{2,6},{3,7},{12,8},{13,9},{14,... | collective-permute-start | bytes 786440 | tf_op jit(solution)/shard_map/ppermute | solution.py:42
  139.7 9.6 %collective-permute-start.33 = (bf16[128,1024]{1,0:T(8,128)(2,1)S(1)}, bf16[128,1024]{1,0:T(8,128)(2,1)S(1)}, u32[]{:S(2)}, u32[]{:S(2)}) collective-permute-start(bf16[128,1024]{1,0:T(8,128)(2,1)S(1)} %add_convert_fusion.1), channel_id=1, source_target_pairs={{112,0},{113,1},{114,2},{115,3},{116,4},{117,5},{118,6},{119,7},{1... | collective-permute-start | bytes 786440 | tf_op jit(solution)/shard_map/ppermute | solution.py:42
  142.9 10.5 %collective-permute-start.35 = (bf16[128,1024]{1,0:T(8,128)(2,1)S(1)}, bf16[128,1024]{1,0:T(8,128)(2,1)S(1)}, u32[]{:S(2)}, u32[]{:S(2)}) collective-permute-start(bf16[128,1024]{1,0:T(8,128)(2,1)S(1)} %add_convert_fusion), channel_id=1, source_target_pairs={{30,0},{31,1},{24,2},{25,3},{26,4},{27,5},{28,6},{29,7},{22,8},{23... | collective-permute-start | bytes 786440 | tf_op jit(solution)/shard_map/ppermute | solution.py:42
Sparse Core Ops, SparseCore 0:
  10.4 16.4 all-gather.1

commit v3 on v2

--- a/solution.py
+++ b/solution.py
@@ -46,29 +46,33 @@
     return fetch(block, (0, 0, 0), True)
 
 
-def sibling(block):
-    both = lax.all_gather(block, "core", axis=0, tiled=True)
-    return lax.dynamic_slice_in_dim(both, (1 - lax.axis_index("core")) * ROWS, ROWS)
-
-
 def give(block, name):
     return fetch(block, tuple(-t for t in offset(name)), name[3] == "s")
 
 
-def unit_kernel(student, teacher, out):
-    for source, first, width in ((student, 0, DS), (teacher, DS, DT)):
-        wide = source[...].astype(jnp.float32)
+def unit_kernel(student, teacher, out, held_s, held_t, sems):
+    parts = [(student, held_s, 0, i * 32) for i in range(4)] + [(teacher, held_t, DS, i * 32) for i in range(4)]
+    copies = []
+    for i, (source, held, _, row) in enumerate(parts):
+        copies.append(pltpu.make_async_copy(source.at[pl.ds(row, 32), :], held.at[pl.ds(row, 32), :], sems.at[i]))
+        copies[-1].start()
+    for copy, (_, held, first, row) in zip(copies, parts):
+        copy.wait()
+        wide = held[pl.ds(row, 32), :].astype(jnp.float32)
         recip = 1.0 / jnp.sqrt(jnp.sum(wide * wide, axis=1, keepdims=True) + 1e-06)
-        out[:, first : first + width] = (wide * recip).astype(jnp.bfloat16)
+        out[pl.ds(row, 32), first : first + held.shape[1]] = (wide * recip).astype(jnp.bfloat16)
 
 
 def unit_rows(student, teacher):
     return pl.pallas_call(
         unit_kernel,
         out_shape=jax.ShapeDtypeStruct((ROWS, WIDE), jnp.bfloat16),
-        in_specs=[pl.BlockSpec(memory_space=pltpu.VMEM)] * 2,
+        in_specs=[pl.BlockSpec(memory_space=pl.ANY)] * 2,
         out_specs=pl.BlockSpec(memory_space=pltpu.VMEM),
-        compiler_params=pltpu.CompilerParams(vmem_limit_bytes=16 << 20),
+        scratch_shapes=[
+            pltpu.VMEM((ROWS, DS), jnp.bfloat16), pltpu.VMEM((ROWS, DT), jnp.bfloat16), pltpu.SemaphoreType.DMA((8,)),
+        ],
+        compiler_params=pltpu.CompilerParams(vmem_limit_bytes=62 << 20),
         name="unit_rows",
     )(student, teacher)
 
@@ -204,11 +208,12 @@
 def local(student, teacher):
     own = unit_rows(student, teacher)
     f32, bf16 = jnp.float32, jnp.bfloat16
-    got = {"000o": own, "000s": sibling(own)}
-    for name in ("010o", "300o", "030o", "003o", "001o"):
+    got = {"000o": own, "000s": swap(own)}
+    for name in ("010o", "300o", "030o", "003o"):
         got[name] = fetch(own, offset(name))
+    got["001o"] = fetch(after(own, got["000s"]), (0, 0, 1))
     for a in ("010", "300"):
-        got[a + "s"] = swap(after(got[a + "o"], got["001o"], got["000s"]))
+        got[a + "s"] = swap(after(got[a + "o"], got["001o"]))
     got["110o"] = fetch(got["010o"], (1, 0, 0))
     got["200o"] = fetch(got["300o"], (3, 0, 0))
     got["031o"] = fetch(got["030o"], (0, 0, 1))
@@ -236,27 +241,31 @@
         "phase_2", LAYOUT_2, GROUPS_2, rows(LAYOUT_2), [(names_1, sums_1)], None,
         [(names_s, bf16), (names_2, f32), (["000o"], f32)] + [([name], bf16) for name in early],
     )
-    *arrays, siblings, sums_2, home = lax.optimization_barrier((*late.values(), siblings, sums_2, home))
+    *arrays, siblings, sums_2 = lax.optimization_barrier((*late.values(), siblings, sums_2))
     late = dict(zip(late, arrays))
     for (name, first), array in list(late.items()):
         late[name[:3] + "s", first] = swap(array)
-    siblings = swap(siblings)
+    siblings = swap(after(siblings, *late.values()))
     back = [give(value, name) for name, value in zip(early, done)]
 
     near = ["010o", "300o", "030o", "200o"]
-    crossing, sum_032, sum_210, sum_031, sum_110, *done = phase(
+    crossing, *done = phase(
         "phase_3", LAYOUT_3, GROUPS_3, rows(LAYOUT_3) + [(name, first, array) for (name, first), array in late.items()],
-        [(names_2, sums_2)], (["none", "010o", "300o", "110o", "200o"], siblings),
-        [(["032s", "210s"], bf16)] + [([name], f32) for name in ("032o", "210o", "031o", "110o")]
-        + [([name], bf16) for name in near],
+        [(names_2, sums_2)], None,
+        [(["032s", "210s"], bf16)] + [([name], f32) for name in ["032o", "210o", "031o", "110o"] + near],
     )
-    crossing, back[0], back[1] = lax.optimization_barrier((crossing, back[0], back[1]))
+    sums = dict(zip(["032o", "210o", "031o", "110o"] + near, done))
+    crossing, siblings, back[0], back[1] = lax.optimization_barrier((crossing, siblings, back[0], back[1]))
     crossing = swap(crossing).astype(f32)
-    to_031 = fetch((sum_032 + crossing[:ROWS]).astype(bf16), (0, 0, 3))
-    to_110 = fetch((sum_210 + crossing[ROWS:]).astype(bf16), (3, 0, 0))
-    back += [give(value, name) for name, value in zip(near, done)]
-    back.append(give((sum_031 + to_031.astype(f32)).astype(bf16), "031o"))
-    back.append(give((sum_110 + to_110.astype(f32)).astype(bf16), "110o"))
+    for i, name in enumerate(names_s):
+        if name[:3] + "o" in sums:
+            sums[name[:3] + "o"] += siblings[i * ROWS : (i + 1) * ROWS].astype(f32)
+    to_031 = fetch((sums["032o"] + crossing[:ROWS]).astype(bf16), (0, 0, 3))
+    to_110 = fetch((sums["210o"] + crossing[ROWS:]).astype(bf16), (3, 0, 0))
+    send_031 = (sums["031o"] + to_031.astype(f32)).astype(bf16)
+    send_110 = (sums["110o"] + to_110.astype(f32)).astype(bf16)
+    back += [give(send_031, "031o"), give(send_110, "110o"), give(sums["030o"].astype(bf16), "030o")]
+    back += [give(after(sums[name].astype(bf16), send_031, send_110), name) for name in ("010o", "300o", "200o")]
 
     summed = home + siblings[:ROWS].astype(f32)
     for value in back:

time: 163 us -> 153 us (0.939)
  between operations: 13.6 us -> 0.17 us
  waiting for transfers between devices: 69.6 us -> 74.5 us
  Pallas kernels: 33.9 us -> 29.2 us
  starting transfers between devices: 38.9 us -> 42.7 us
  local copies, waits for them, and re-layouts: 3.75 us -> 1.5 us
    ppermute x36 -> x37, waiting for transfers between devices: 61.7 us -> 74.5 us  [fetch(): return lax.ppermute(block, ('chip', 'core'), pairs)]
    all_gather x1 -> x0, waiting for transfers between devices: 7.94 us -> none  [sibling(): both = lax.all_gather(block, 'core', axis=0, tiled=True)]
    pallas_call x3, Pallas kernels: 32.4 us -> 26 us  [phase(): pl.pallas_call(functools.partial(phase_kernel, layout, groups, [(n, f) fo...]
    ppermute x36 -> x37, starting transfers between devices: 38.9 us -> 42.7 us  [fetch(): return lax.ppermute(block, ('chip', 'core'), pairs)]
  transfers between devices with their start and end apart: 37 -> 37, of which waited for: 18 -> 20; matrix products, arithmetic and copies ran while one was open for 1% -> 1% of each run, Pallas kernels for 20% -> 17%
where the time goes in v3:
time: 153 us; the launch traced here: 150 us
  waiting for transfers between devices  74.5 us (49%)
  starting transfers between devices  42.7 us (28%)
  Pallas kernels  29.2 us (19%)
  other arithmetic  2.47 us (2%)
    ppermute x37, waiting for transfers between devices, fetch(): return lax.ppermute(block, ('chip', 'core'), pairs)  74.5 us
    ppermute x37, starting transfers between devices, fetch(): return lax.ppermute(block, ('chip', 'core'), pairs)  42.7 us
    pallas_call x3, Pallas kernels, phase(): pl.pallas_call(functools.partial(phase_kernel, layout, groups, [(n, f) fo...  26 us
    pallas_call x1, Pallas kernels, unit_rows(): pl.pallas_call(unit_kernel, out_shape=jax.ShapeDtypeStruct((ROWS, WIDE),...  3.12 us
  transfers between devices with their start and end apart: 37, of which 20 were waited for; matrix products, arithmetic and copies ran while one was open for 1% of the time, Pallas kernels for 17%

profile of v3, /device:TPU:0, one launch (start us, length us, event | category | flops | bytes accessed | tf_op | source)
XLA Modules:
  0.0 150.5 jit_solution(9008079974857121106)
XLA Ops:
  0.0 3.1 %unit_rows.1.refs_1_ = bf16[128,5120]{1,0:T(8,128)(2,1)} custom-call(bf16[128,1024]{1,0:T(8,128)(2,1)} %student.1, bf16[128,4096]{1,0:T(8,128)(2,1)} %teacher.1), custom_call_target="tpu_custom_call" | custom-call | tf_op jit(solution)/shard_map/unit_rows/pallas_call | solution.py:67
  3.1 0.1 collective-permute-start
  3.2 3.2 %collective-permute-start.3 = (bf16[128,5120]{1,0:T(8,128)(2,1)}, bf16[128,5120]{1,0:T(8,128)(2,1)S(1)}, u32[]{:S(2)}, u32[]{:S(2)}) collective-permute-start(bf16[128,5120]{1,0:T(8,128)(2,1)} %unit_rows.1.refs_1_), channel_id=1, source_target_pairs={{16,0},{17,1},{18,2},{19,3},{20,4},{21,5},{22,6},{23,7},{24,8},{25... | collective-permute-start | bytes 3932168 | tf_op jit(solution)/shard_map/ppermute | solution.py:42
  6.4 0.1 collective-permute-done.refs_0_
  6.5 4.1 %collective-permute-start.1 = (bf16[128,5120]{1,0:T(8,128)(2,1)}, bf16[128,5120]{1,0:T(8,128)(2,1)S(1)}, u32[]{:S(2)}, u32[]{:S(2)}) collective-permute-start(bf16[128,5120]{1,0:T(8,128)(2,1)} %unit_rows.1.refs_1_), channel_id=1, source_target_pairs={{32,0},{33,1},{34,2},{35,3},{36,4},{37,5},{38,6},{39,7},{40,8},{41... | collective-permute-start | bytes 3932168 | tf_op jit(solution)/shard_map/ppermute | solution.py:42
  10.6 1.5 collective-permute-start.5
  12.1 0.0 collective-permute-start.2
  12.1 1.6 %collective-permute-start.8 = (bf16[128,5120]{1,0:T(8,128)(2,1)}, bf16[128,5120]{1,0:T(8,128)(2,1)S(1)}, u32[]{:S(2)}, u32[]{:S(2)}) collective-permute-start(bf16[128,5120]{1,0:T(8,128)(2,1)} %unit_rows.1.refs_1_), channel_id=1, source_target_pairs={{24,0},{25,1},{26,2},{27,3},{28,4},{29,5},{30,6},{31,7},{16,8},{17... | collective-permute-start | bytes 3932168 | tf_op jit(solution)/shard_map/ppermute | solution.py:42
  13.6 21.7 %collective-permute-done.3.refs_7_.refs_2_.refs_0_ = bf16[128,5120]{1,0:T(8,128)(2,1)S(1)} collective-permute-done((bf16[128,5120]{1,0:T(8,128)(2,1)}, bf16[128,5120]{1,0:T(8,128)(2,1)S(1)}, u32[]{:S(2)}, u32[]{:S(2)}) %collective-permute-start.3) | collective-permute-done | bytes 1310752 | tf_op jit(solution)/shard_map/ppermute | solution.py:42
  35.4 3.9 %collective-permute-done.1.refs_2_.refs_10_ = bf16[128,5120]{1,0:T(8,128)(2,1)S(1)} collective-permute-done((bf16[128,5120]{1,0:T(8,128)(2,1)}, bf16[128,5120]{1,0:T(8,128)(2,1)S(1)}, u32[]{:S(2)}, u32[]{:S(2)}) %collective-permute-start.1) | collective-permute-done | bytes 1310752 | tf_op jit(solution)/shard_map/ppermute | solution.py:42
  39.2 3.3 %collective-permute-done.5.refs_5_.refs_4_.refs_1_ = bf16[128,5120]{1,0:T(8,128)(2,1)S(1)} collective-permute-done((bf16[128,5120]{1,0:T(8,128)(2,1)}, bf16[128,5120]{1,0:T(8,128)(2,1)S(1)}, u32[]{:S(2)}, u32[]{:S(2)}) %collective-permute-start.5) | collective-permute-done | bytes 1310752 | tf_op jit(solution)/shard_map/ppermute | solution.py:42
  42.5 1.5 %collective-permute-start.11 = (bf16[128,5120]{1,0:T(8,128)(2,1)S(1)}, bf16[128,5120]{1,0:T(8,128)(2,1)S(1)}, u32[]{:S(2)}, u32[]{:S(2)}) collective-permute-start(bf16[128,5120]{1,0:T(8,128)(2,1)S(1)} %collective-permute-done.3.refs_7_.refs_2_.refs_0_), channel_id=1, source_target_pairs={{2,0},{3,1},{4,2},{5,3},{6,4},{7,5},{0,6},{1,7},{10,8},{11,9},{12,... | collective-permute-start | bytes 3932168 | tf_op jit(solution)/shard_map/ppermute | solution.py:42
  44.1 1.1 collective-permute-start.12
  45.2 1.6 %collective-permute-start.9 = (bf16[128,5120]{1,0:T(8,128)(2,1)S(1)}, bf16[128,5120]{1,0:T(8,128)(2,1)S(1)}, u32[]{:S(2)}, u32[]{:S(2)}) collective-permute-start(bf16[128,5120]{1,0:T(8,128)(2,1)S(1)} %collective-permute-done.8.refs_4_.refs_8_), channel_id=1, source_target_pairs={{32,0},{33,1},{34,2},{35,3},{36,4},{37,5},{38,6},{39,7},{40,8},{41... | collective-permute-start | bytes 3932168 | tf_op jit(solution)/shard_map/ppermute | solution.py:42
  46.8 0.9 collective-permute-start.10
  47.8 1.1 collective-permute-start.7
  48.9 1.3 copy-done
  50.2 8.5 %phase_1.1.refs_16_ = f32[1152,1024]{1,0:T(8,128)S(1)} custom-call(bf16[128,5120]{1,0:T(8,128)(2,1)S(1)} %collective-permute-done.refs_0_, bf16[128,5120]{1,0:T(8,128)(2,1)S(1)} %copy-done, bf16[128,5120]{1,0:T(8,128)(2,1)S(1)} %collective-permute-done.1.refs_2_.refs_10_, bf16[128,5120]{1,0:T(8,128)(2,1)S(1)} %collective-permute-done.2.refs_3_.refs_9_, ...), custom_call_target="tpu_custom_call" | custom-call | flops 10334765056 | bytes 11796480 | tf_op jit(solution)/shard_map/phase_1/pallas_call | solution.py:183
  58.7 15.1 %collective-permute-done.11.refs_14_.refs_2_ = bf16[128,5120]{1,0:T(8,128)(2,1)S(1)} collective-permute-done((bf16[128,5120]{1,0:T(8,128)(2,1)S(1)}, bf16[128,5120]{1,0:T(8,128)(2,1)S(1)}, u32[]{:S(2)}, u32[]{:S(2)}) %collective-permute-start.11) | collective-permute-done | bytes 1310752 | tf_op jit(solution)/shard_map/ppermute | solution.py:42
  73.7 2.5 %collective-permute-done.12.refs_6_.refs_3_ = bf16[128,5120]{1,0:T(8,128)(2,1)S(1)} collective-permute-done((bf16[128,5120]{1,0:T(8,128)(2,1)S(1)}, bf16[128,5120]{1,0:T(8,128)(2,1)S(1)}, u32[]{:S(2)}, u32[]{:S(2)}) %collective-permute-start.12) | collective-permute-done | bytes 1310752 | tf_op jit(solution)/shard_map/ppermute | solution.py:42
  76.2 1.4 collective-permute-done.10.refs_13_
  77.7 1.2 collective-permute-done.7.refs_11_
  78.9 0.5 collective-permute-start.14
  79.5 3.0 %collective-permute-start.15 = (bf16[128,2560]{1,0:T(8,128)(2,1)S(1)}, bf16[128,2560]{1,0:T(8,128)(2,1)S(1)}, u32[]{:S(2)}, u32[]{:S(2)}) collective-permute-start(bf16[128,2560]{1,0:T(8,128)(2,1)S(1)} %slice.33), channel_id=1, source_target_pairs={{2,0},{3,1},{4,2},{5,3},{6,4},{7,5},{0,6},{1,7},{10,8},{11,9},{12,... | collective-permute-start | bytes 1966088 | tf_op jit(solution)/shard_map/ppermute | solution.py:42
  82.6 1.8 %collective-permute-start.16 = (bf16[128,2560]{1,0:T(8,128)(2,1)S(1)}, bf16[128,2560]{1,0:T(8,128)(2,1)S(1)}, u32[]{:S(2)}, u32[]{:S(2)}) collective-permute-start(bf16[128,2560]{1,0:T(8,128)(2,1)S(1)} %slice.34), channel_id=1, source_target_pairs={{16,0},{17,1},{18,2},{19,3},{20,4},{21,5},{22,6},{23,7},{24,8},{25... | collective-permute-start | bytes 1966088 | tf_op jit(solution)/shard_map/ppermute | solution.py:42
  84.4 0.9 collective-permute-start.17
  85.4 1.3 collective-permute-start.18
  86.6 12.6 %phase_2.1 = (bf16[640,1024]{1,0:T(8,128)(2,1)S(1)}, f32[768,1024]{1,0:T(8,128)S(1)}, f32[128,1024]{1,0:T(8,128)S(1)}, bf16[128,1024]{1,0:T(8,128)(2,1)S(1)}, bf...) custom-call(bf16[128,5120]{1,0:T(8,128)(2,1)S(1)} %collective-permute-done.refs_0_, ...), custom_call_target="tpu_custom_call" | custom-call | flops 16911433728 | bytes 25690112 | tf_op jit(solution)/shard_map/phase_2/pallas_call | solution.py:183
  99.2 1.3 collective-permute-done.17.refs_8_
  100.6 1.9 %collective-permute-done.18.refs_9_ = bf16[128,2560]{1,0:T(8,128)(2,1)S(1)} collective-permute-done((bf16[128,2560]{1,0:T(8,128)(2,1)S(1)}, bf16[128,2560]{1,0:T(8,128)(2,1)S(1)}, u32[]{:S(2)}, u32[]{:S(2)}) %collective-permute-start.18) | collective-permute-done | bytes 655392 | tf_op jit(solution)/shard_map/ppermute | solution.py:42
  102.4 0.5 collective-permute-start.20
  103.0 0.0 collective-permute-start.21
  103.0 0.5 collective-permute-start.22
  103.5 1.1 collective-permute-done.19.refs_10_
  104.5 0.9 collective-permute-done.20.refs_11_
  105.5 0.9 collective-permute-done.21.refs_12_
  106.4 0.9 collective-permute-done.22.refs_13_
  107.4 0.1 collective-permute-start.23
  107.5 0.0 collective-permute-start.24
  107.5 3.2 %collective-permute-start.25 = (bf16[128,1024]{1,0:T(8,128)(2,1)S(1)}, bf16[128,1024]{1,0:T(8,128)(2,1)S(1)}, u32[]{:S(2)}, u32[]{:S(2)}) collective-permute-start(bf16[128,1024]{1,0:T(8,128)(2,1)S(1)} %get-tuple-element.87), channel_id=1, source_target_pairs={{32,0},{33,1},{34,2},{35,3},{36,4},{37,5},{38,6},{39,7},{40,8},{41... | collective-permute-start | bytes 786440 | tf_op jit(solution)/shard_map/ppermute | solution.py:42
  110.7 5.0 %phase_3.1 = (bf16[256,1024]{1,0:T(8,128)(2,1)S(1)}, f32[128,1024]{1,0:T(8,128)S(1)}, f32[128,1024]{1,0:T(8,128)S(1)}, f32[128,1024]{1,0:T(8,128)S(1)}, f32[128,...) custom-call(bf16[128,5120]{1,0:T(8,128)(2,1)S(1)} %collective-permut, ...), custom_call_target="tpu_custom_call" | custom-call | flops 6576668672 | bytes 16252928 | tf_op jit(solution)/shard_map/phase_3/pallas_call | solution.py:183
  115.7 1.5 %collective-permute-done.24 = bf16[128,1024]{1,0:T(8,128)(2,1)S(1)} collective-permute-done((bf16[128,1024]{1,0:T(8,128)(2,1)S(1)}, bf16[128,1024]{1,0:T(8,128)(2,1)S(1)}, u32[]{:S(2)}, u32[]{:S(2)}) %collective-permute-start.24) | collective-permute-done | bytes 262176 | tf_op jit(solution)/shard_map/ppermute | solution.py:42
  117.3 1.9 %collective-permute-done.28 = bf16[256,1024]{1,0:T(8,128)(2,1)S(1)} collective-permute-done((bf16[256,1024]{1,0:T(8,128)(2,1)S(1)}, bf16[256,1024]{1,0:T(8,128)(2,1)S(1)}, u32[]{:S(2)}, u32[]{:S(2)}) %collective-permute-start.28) | collective-permute-done | bytes 524320 | tf_op jit(solution)/shard_map/ppermute | solution.py:42
  119.2 0.1 convert_element_type.87
  119.3 0.2 fusion.6
  119.5 0.1 collective-permute-start.29
  119.6 0.2 collective-permute-start.31
  119.8 4.3 %collective-permute-start.26 = (bf16[128,1024]{1,0:T(8,128)(2,1)S(1)}, bf16[128,1024]{1,0:T(8,128)(2,1)S(1)}, u32[]{:S(2)}, u32[]{:S(2)}) collective-permute-start(bf16[128,1024]{1,0:T(8,128)(2,1)S(1)} %get-tuple-element.91), channel_id=1, source_target_pairs={{48,0},{49,1},{50,2},{51,3},{52,4},{53,5},{54,6},{55,7},{56,8},{57... | collective-permute-start | bytes 786440 | tf_op jit(solution)/shard_map/ppermute | solution.py:42
  124.1 0.3 collective-permute-start.27
  124.4 1.8 %collective-permute-start.33 = (bf16[128,1024]{1,0:T(8,128)(2,1)S(1)}, bf16[128,1024]{1,0:T(8,128)(2,1)S(1)}, u32[]{:S(2)}, u32[]{:S(2)}) collective-permute-start(bf16[128,1024]{1,0:T(8,128)(2,1)S(1)} %convert_element_type.97), channel_id=1, source_target_pairs={{16,0},{17,1},{18,2},{19,3},{20,4},{21,5},{22,6},{23,7},{24,8},{25... | collective-permute-start | bytes 786440 | tf_op jit(solution)/shard_map/ppermute | solution.py:42
  126.2 2.9 %collective-permute-done.29 = bf16[128,1024]{1,0:T(8,128)(2,1)S(1)} collective-permute-done((bf16[128,1024]{1,0:T(8,128)(2,1)S(1)}, bf16[128,1024]{1,0:T(8,128)(2,1)S(1)}, u32[]{:S(2)}, u32[]{:S(2)}) %collective-permute-start.29) | collective-permute-done | bytes 262176 | tf_op jit(solution)/shard_map/ppermute | solution.py:42
  129.1 0.1 add_convert_fusion.4
  129.2 0.8 collective-permute-start.30
  130.0 0.4 add_convert_fusion.2
  130.4 1.2 collective-permute-start.32
  131.6 0.7 collective-permute-start.34
  132.2 3.9 %collective-permute-done.27 = bf16[128,1024]{1,0:T(8,128)(2,1)S(1)} collective-permute-done((bf16[128,1024]{1,0:T(8,128)(2,1)S(1)}, bf16[128,1024]{1,0:T(8,128)(2,1)S(1)}, u32[]{:S(2)}, u32[]{:S(2)}) %collective-permute-start.27) | collective-permute-done | bytes 262176 | tf_op jit(solution)/shard_map/ppermute | solution.py:42
  136.1 2.1 %collective-permute-start.35 = (bf16[128,1024]{1,0:T(8,128)(2,1)S(1)}, bf16[128,1024]{1,0:T(8,128)(2,1)S(1)}, u32[]{:S(2)}, u32[]{:S(2)}) collective-permute-start(bf16[128,1024]{1,0:T(8,128)(2,1)S(1)} %get-tuple-element.102), channel_id=1, source_target_pairs={{2,0},{3,1},{4,2},{5,3},{6,4},{7,5},{0,6},{1,7},{10,8},{11,9},{12,... | collective-permute-start | bytes 786440 | tf_op jit(solution)/shard_map/ppermute | solution.py:42
  138.2 2.7 %collective-permute-start.36 = (bf16[128,1024]{1,0:T(8,128)(2,1)S(1)}, bf16[128,1024]{1,0:T(8,128)(2,1)S(1)}, u32[]{:S(2)}, u32[]{:S(2)}) collective-permute-start(bf16[128,1024]{1,0:T(8,128)(2,1)S(1)} %get-tuple-element.104), channel_id=1, source_target_pairs={{4,0},{5,1},{6,2},{7,3},{0,4},{1,5},{2,6},{3,7},{12,8},{13,9},{14,... | collective-permute-start | bytes 786440 | tf_op jit(solution)/shard_map/ppermute | solution.py:42
  140.9 0.1 fusion.5
  141.0 4.0 %collective-permute-done.34 = bf16[128,1024]{1,0:T(8,128)(2,1)S(1)} collective-permute-done((bf16[128,1024]{1,0:T(8,128)(2,1)S(1)}, bf16[128,1024]{1,0:T(8,128)(2,1)S(1)}, u32[]{:S(2)}, u32[]{:S(2)}) %collective-permute-start.34) | collective-permute-done | bytes 262176 | tf_op jit(solution)/shard_map/ppermute | solution.py:42
  145.0 3.9 %collective-permute-done.35 = bf16[128,1024]{1,0:T(8,128)(2,1)S(1)} collective-permute-done((bf16[128,1024]{1,0:T(8,128)(2,1)S(1)}, bf16[128,1024]{1,0:T(8,128)(2,1)S(1)}, u32[]{:S(2)}, u32[]{:S(2)}) %collective-permute-start.35) | collective-permute-done | bytes 262176 | tf_op jit(solution)/shard_map/ppermute | solution.py:42
  148.9 0.6 fusion.2
  149.4 1.0 fusion.4
  (33 shorter events, 0.3 us)
Async XLA Ops:
  3.1 3.3 %collective-permute-start = (bf16[128,5120]{1,0:T(8,128)(2,1)}, bf16[128,5120]{1,0:T(8,128)(2,1)S(1)}, u32[]{:S(2)}, u32[]{:S(2)}) collective-permute-start(bf16[128,5120]{1,0:T(8,128)(2,1)} %unit_rows.1.refs_1_), channel_id=1, source_target_pairs={{1,0},{0,1},{3,2},{2,3},{5,4},{4,5},{7,6},{6,7},{9,8},{8,9},{11,10... | collective-permute-start | bytes 3932168 | tf_op jit(solution)/shard_map/ppermute | solution.py:42
  3.2 32.1 %collective-permute-start.3 = (bf16[128,5120]{1,0:T(8,128)(2,1)}, bf16[128,5120]{1,0:T(8,128)(2,1)S(1)}, u32[]{:S(2)}, u32[]{:S(2)}) collective-permute-start(bf16[128,5120]{1,0:T(8,128)(2,1)} %unit_rows.1.refs_1_), channel_id=1, source_target_pairs={{16,0},{17,1},{18,2},{19,3},{20,4},{21,5},{22,6},{23,7},{24,8},{25... | collective-permute-start | bytes 3932168 | tf_op jit(solution)/shard_map/ppermute | solution.py:42
  6.5 32.8 %collective-permute-start.1 = (bf16[128,5120]{1,0:T(8,128)(2,1)}, bf16[128,5120]{1,0:T(8,128)(2,1)S(1)}, u32[]{:S(2)}, u32[]{:S(2)}) collective-permute-start(bf16[128,5120]{1,0:T(8,128)(2,1)} %unit_rows.1.refs_1_), channel_id=1, source_target_pairs={{32,0},{33,1},{34,2},{35,3},{36,4},{37,5},{38,6},{39,7},{40,8},{41... | collective-permute-start | bytes 3932168 | tf_op jit(solution)/shard_map/ppermute | solution.py:42
  10.6 32.0 %collective-permute-start.5 = (bf16[128,5120]{1,0:T(8,128)(2,1)}, bf16[128,5120]{1,0:T(8,128)(2,1)S(1)}, u32[]{:S(2)}, u32[]{:S(2)}) collective-permute-start(bf16[128,5120]{1,0:T(8,128)(2,1)} %unit_rows.1.refs_1_), channel_id=1, source_target_pairs={{6,0},{7,1},{0,2},{1,3},{2,4},{3,5},{4,6},{5,7},{14,8},{15,9},{8,1... | collective-permute-start | bytes 3932168 | tf_op jit(solution)/shard_map/ppermute | solution.py:42
  12.1 32.0 %collective-permute-start.2 = (bf16[128,5120]{1,0:T(8,128)(2,1)}, bf16[128,5120]{1,0:T(8,128)(2,1)S(1)}, u32[]{:S(2)}, u32[]{:S(2)}) collective-permute-start(bf16[128,5120]{1,0:T(8,128)(2,1)} %unit_rows.1.refs_1_), channel_id=1, source_target_pairs={{96,0},{97,1},{98,2},{99,3},{100,4},{101,5},{102,6},{103,7},{104,8... | collective-permute-start | bytes 3932168 | tf_op jit(solution)/shard_map/ppermute | solution.py:42
  12.1 33.2 %collective-permute-start.8 = (bf16[128,5120]{1,0:T(8,128)(2,1)}, bf16[128,5120]{1,0:T(8,128)(2,1)S(1)}, u32[]{:S(2)}, u32[]{:S(2)}) collective-permute-start(bf16[128,5120]{1,0:T(8,128)(2,1)} %unit_rows.1.refs_1_), channel_id=1, source_target_pairs={{24,0},{25,1},{26,2},{27,3},{28,4},{29,5},{30,6},{31,7},{16,8},{17... | collective-permute-start | bytes 3932168 | tf_op jit(solution)/shard_map/ppermute | solution.py:42
  39.2 7.6 %collective-permute-start.4 = (bf16[128,5120]{1,0:T(8,128)(2,1)S(1)}, bf16[128,5120]{1,0:T(8,128)(2,1)S(1)}, u32[]{:S(2)}, u32[]{:S(2)}) collective-permute-start(bf16[128,5120]{1,0:T(8,128)(2,1)S(1)} %collective-permute-done.3.refs_7_.refs_2_.refs_0_), channel_id=1, source_target_pairs={{1,0},{0,1},{3,2},{2,3},{5,4},{4,5},{7,6},{6,7},{9,8},{8,9},{11,10... | collective-permute-start | bytes 3932168 | tf_op jit(solution)/shard_map/ppermute | solution.py:42
  42.5 4.3 %collective-permute-start.6 = (bf16[128,5120]{1,0:T(8,128)(2,1)S(1)}, bf16[128,5120]{1,0:T(8,128)(2,1)S(1)}, u32[]{:S(2)}, u32[]{:S(2)}) collective-permute-start(bf16[128,5120]{1,0:T(8,128)(2,1)S(1)} %collective-permute-done.5.refs_5_.refs_4_.refs_1_), channel_id=1, source_target_pairs={{1,0},{0,1},{3,2},{2,3},{5,4},{4,5},{7,6},{6,7},{9,8},{8,9},{11,10... | collective-permute-start | bytes 3932168 | tf_op jit(solution)/shard_map/ppermute | solution.py:42
  42.5 31.2 %collective-permute-start.11 = (bf16[128,5120]{1,0:T(8,128)(2,1)S(1)}, bf16[128,5120]{1,0:T(8,128)(2,1)S(1)}, u32[]{:S(2)}, u32[]{:S(2)}) collective-permute-start(bf16[128,5120]{1,0:T(8,128)(2,1)S(1)} %collective-permute-done.3.refs_7_.refs_2_.refs_0_), channel_id=1, source_target_pairs={{2,0},{3,1},{4,2},{5,3},{6,4},{7,5},{0,6},{1,7},{10,8},{11,9},{12,... | collective-permute-start | bytes 3932168 | tf_op jit(solution)/shard_map/ppermute | solution.py:42
  44.1 32.1 %collective-permute-start.12 = (bf16[128,5120]{1,0:T(8,128)(2,1)S(1)}, bf16[128,5120]{1,0:T(8,128)(2,1)S(1)}, u32[]{:S(2)}, u32[]{:S(2)}) collective-permute-start(bf16[128,5120]{1,0:T(8,128)(2,1)S(1)} %collective-permute-done.5.refs_5_.refs_4_.refs_1_), channel_id=1, source_target_pairs={{6,0},{7,1},{0,2},{1,3},{2,4},{3,5},{4,6},{5,7},{14,8},{15,9},{8,1... | collective-permute-start | bytes 3932168 | tf_op jit(solution)/shard_map/ppermute | solution.py:42
  45.2 31.0 %collective-permute-start.9 = (bf16[128,5120]{1,0:T(8,128)(2,1)S(1)}, bf16[128,5120]{1,0:T(8,128)(2,1)S(1)}, u32[]{:S(2)}, u32[]{:S(2)}) collective-permute-start(bf16[128,5120]{1,0:T(8,128)(2,1)S(1)} %collective-permute-done.8.refs_4_.refs_8_), channel_id=1, source_target_pairs={{32,0},{33,1},{34,2},{35,3},{36,4},{37,5},{38,6},{39,7},{40,8},{41... | collective-permute-start | bytes 3932168 | tf_op jit(solution)/shard_map/ppermute | solution.py:42
  46.8 30.9 %collective-permute-start.10 = (bf16[128,5120]{1,0:T(8,128)(2,1)S(1)}, bf16[128,5120]{1,0:T(8,128)(2,1)S(1)}, u32[]{:S(2)}, u32[]{:S(2)}) collective-permute-start(bf16[128,5120]{1,0:T(8,128)(2,1)S(1)} %collective-permute-done.2.refs_3_.refs_9_), channel_id=1, source_target_pairs={{24,0},{25,1},{26,2},{27,3},{28,4},{29,5},{30,6},{31,7},{16,8},{17... | collective-permute-start | bytes 3932168 | tf_op jit(solution)/shard_map/ppermute | solution.py:42
  47.8 31.1 %collective-permute-start.7 = (bf16[128,5120]{1,0:T(8,128)(2,1)S(1)}, bf16[128,5120]{1,0:T(8,128)(2,1)S(1)}, u32[]{:S(2)}, u32[]{:S(2)}) collective-permute-start(bf16[128,5120]{1,0:T(8,128)(2,1)S(1)} %collective-permute-done.2.refs_3_.refs_9_), channel_id=1, source_target_pairs={{96,0},{97,1},{98,2},{99,3},{100,4},{101,5},{102,6},{103,7},{104,8... | collective-permute-start | bytes 3932168 | tf_op jit(solution)/shard_map/ppermute | solution.py:42
  48.9 1.3 copy-start
  78.9 6.4 %collective-permute-start.13 = (bf16[128,5120]{1,0:T(8,128)(2,1)S(1)}, bf16[128,5120]{1,0:T(8,128)(2,1)S(1)}, u32[]{:S(2)}, u32[]{:S(2)}) collective-permute-start(bf16[128,5120]{1,0:T(8,128)(2,1)S(1)} %collective-permute-done.12.refs_6_.refs_3_), channel_id=1, source_target_pairs={{1,0},{0,1},{3,2},{2,3},{5,4},{4,5},{7,6},{6,7},{9,8},{8,9},{11,10... | collective-permute-start | bytes 3932168 | tf_op jit(solution)/shard_map/ppermute | solution.py:42
  78.9 6.4 %collective-permute-start.14 = (bf16[128,5120]{1,0:T(8,128)(2,1)S(1)}, bf16[128,5120]{1,0:T(8,128)(2,1)S(1)}, u32[]{:S(2)}, u32[]{:S(2)}) collective-permute-start(bf16[128,5120]{1,0:T(8,128)(2,1)S(1)} %collective-permute-done.11.refs_14_.refs_2_), channel_id=1, source_target_pairs={{1,0},{0,1},{3,2},{2,3},{5,4},{4,5},{7,6},{6,7},{9,8},{8,9},{11,10... | collective-permute-start | bytes 3932168 | tf_op jit(solution)/shard_map/ppermute | solution.py:42
  79.5 7.1 %copy-start.1 = (bf16[128,5120]{1,0:T(8,128)(2,1)S(1)}, bf16[128,5120]{1,0:T(8,128)(2,1)}, u32[]{:S(2)}) copy-start(bf16[128,5120]{1,0:T(8,128)(2,1)} %unit_rows.1.refs_1_) | copy-start | bytes 3932164
  79.5 19.7 %collective-permute-start.15 = (bf16[128,2560]{1,0:T(8,128)(2,1)S(1)}, bf16[128,2560]{1,0:T(8,128)(2,1)S(1)}, u32[]{:S(2)}, u32[]{:S(2)}) collective-permute-start(bf16[128,2560]{1,0:T(8,128)(2,1)S(1)} %slice.33), channel_id=1, source_target_pairs={{2,0},{3,1},{4,2},{5,3},{6,4},{7,5},{0,6},{1,7},{10,8},{11,9},{12,... | collective-permute-start | bytes 1966088 | tf_op jit(solution)/shard_map/ppermute | solution.py:42
  82.6 16.6 %collective-permute-start.16 = (bf16[128,2560]{1,0:T(8,128)(2,1)S(1)}, bf16[128,2560]{1,0:T(8,128)(2,1)S(1)}, u32[]{:S(2)}, u32[]{:S(2)}) collective-permute-start(bf16[128,2560]{1,0:T(8,128)(2,1)S(1)} %slice.34), channel_id=1, source_target_pairs={{16,0},{17,1},{18,2},{19,3},{20,4},{21,5},{22,6},{23,7},{24,8},{25... | collective-permute-start | bytes 1966088 | tf_op jit(solution)/shard_map/ppermute | solution.py:42
  84.4 16.2 %collective-permute-start.17 = (bf16[128,2560]{1,0:T(8,128)(2,1)S(1)}, bf16[128,2560]{1,0:T(8,128)(2,1)S(1)}, u32[]{:S(2)}, u32[]{:S(2)}) collective-permute-start(bf16[128,2560]{1,0:T(8,128)(2,1)S(1)} %slice.35), channel_id=1, source_target_pairs={{32,0},{33,1},{34,2},{35,3},{36,4},{37,5},{38,6},{39,7},{40,8},{41... | collective-permute-start | bytes 1966088 | tf_op jit(solution)/shard_map/ppermute | solution.py:42
  85.4 17.1 %collective-permute-start.18 = (bf16[128,2560]{1,0:T(8,128)(2,1)S(1)}, bf16[128,2560]{1,0:T(8,128)(2,1)S(1)}, u32[]{:S(2)}, u32[]{:S(2)}) collective-permute-start(bf16[128,2560]{1,0:T(8,128)(2,1)S(1)} %slice.36), channel_id=1, source_target_pairs={{96,0},{97,1},{98,2},{99,3},{100,4},{101,5},{102,6},{103,7},{104,8... | collective-permute-start | bytes 1966088 | tf_op jit(solution)/shard_map/ppermute | solution.py:42
  102.4 2.1 %collective-permute-start.19 = (bf16[128,2560]{1,0:T(8,128)(2,1)S(1)}, bf16[128,2560]{1,0:T(8,128)(2,1)S(1)}, u32[]{:S(2)}, u32[]{:S(2)}) collective-permute-start(bf16[128,2560]{1,0:T(8,128)(2,1)S(1)} %collective-permute-done.15.refs_6_), channel_id=1, source_target_pairs={{1,0},{0,1},{3,2},{2,3},{5,4},{4,5},{7,6},{6,7},{9,8},{8,9},{11,10... | collective-permute-start | bytes 1966088 | tf_op jit(solution)/shard_map/ppermute | solution.py:42
  102.4 3.0 %collective-permute-start.20 = (bf16[128,2560]{1,0:T(8,128)(2,1)S(1)}, bf16[128,2560]{1,0:T(8,128)(2,1)S(1)}, u32[]{:S(2)}, u32[]{:S(2)}) collective-permute-start(bf16[128,2560]{1,0:T(8,128)(2,1)S(1)} %collective-permute-done.16.refs_7_), channel_id=1, source_target_pairs={{1,0},{0,1},{3,2},{2,3},{5,4},{4,5},{7,6},{6,7},{9,8},{8,9},{11,10... | collective-permute-start | bytes 1966088 | tf_op jit(solution)/shard_map/ppermute | solution.py:42
  103.0 3.5 %collective-permute-start.21 = (bf16[128,2560]{1,0:T(8,128)(2,1)S(1)}, bf16[128,2560]{1,0:T(8,128)(2,1)S(1)}, u32[]{:S(2)}, u32[]{:S(2)}) collective-permute-start(bf16[128,2560]{1,0:T(8,128)(2,1)S(1)} %collective-permute-done.17.refs_8_), channel_id=1, source_target_pairs={{1,0},{0,1},{3,2},{2,3},{5,4},{4,5},{7,6},{6,7},{9,8},{8,9},{11,10... | collective-permute-start | bytes 1966088 | tf_op jit(solution)/shard_map/ppermute | solution.py:42
  103.0 4.4 %collective-permute-start.22 = (bf16[128,2560]{1,0:T(8,128)(2,1)S(1)}, bf16[128,2560]{1,0:T(8,128)(2,1)S(1)}, u32[]{:S(2)}, u32[]{:S(2)}) collective-permute-start(bf16[128,2560]{1,0:T(8,128)(2,1)S(1)} %collective-permute-done.18.refs_9_), channel_id=1, source_target_pairs={{1,0},{0,1},{3,2},{2,3},{5,4},{4,5},{7,6},{6,7},{9,8},{8,9},{11,10... | collective-permute-start | bytes 1966088 | tf_op jit(solution)/shard_map/ppermute | solution.py:42
  107.4 9.9 %collective-permute-start.23 = (bf16[640,1024]{1,0:T(8,128)(2,1)S(1)}, bf16[640,1024]{1,0:T(8,128)(2,1)S(1)}, u32[]{:S(2)}, u32[]{:S(2)}) collective-permute-start(bf16[640,1024]{1,0:T(8,128)(2,1)S(1)} %get-tuple-element.85), channel_id=1, source_target_pairs={{1,0},{0,1},{3,2},{2,3},{5,4},{4,5},{7,6},{6,7},{9,8},{8,9},{11,10... | collective-permute-start | bytes 3932168 | tf_op jit(solution)/shard_map/ppermute | solution.py:42
  107.5 9.8 %collective-permute-start.24 = (bf16[128,1024]{1,0:T(8,128)(2,1)S(1)}, bf16[128,1024]{1,0:T(8,128)(2,1)S(1)}, u32[]{:S(2)}, u32[]{:S(2)}) collective-permute-start(bf16[128,1024]{1,0:T(8,128)(2,1)S(1)} %get-tuple-element.86), channel_id=1, source_target_pairs={{96,0},{97,1},{98,2},{99,3},{100,4},{101,5},{102,6},{103,7},{104,8... | collective-permute-start | bytes 786440 | tf_op jit(solution)/shard_map/ppermute | solution.py:42
  107.5 9.8 %collective-permute-start.25 = (bf16[128,1024]{1,0:T(8,128)(2,1)S(1)}, bf16[128,1024]{1,0:T(8,128)(2,1)S(1)}, u32[]{:S(2)}, u32[]{:S(2)}) collective-permute-start(bf16[128,1024]{1,0:T(8,128)(2,1)S(1)} %get-tuple-element.87), channel_id=1, source_target_pairs={{32,0},{33,1},{34,2},{35,3},{36,4},{37,5},{38,6},{39,7},{40,8},{41... | collective-permute-start | bytes 786440 | tf_op jit(solution)/shard_map/ppermute | solution.py:42
  117.3 1.9 %collective-permute-start.28 = (bf16[256,1024]{1,0:T(8,128)(2,1)S(1)}, bf16[256,1024]{1,0:T(8,128)(2,1)S(1)}, u32[]{:S(2)}, u32[]{:S(2)}) collective-permute-start(bf16[256,1024]{1,0:T(8,128)(2,1)S(1)} %get-tuple-element.95), channel_id=1, source_target_pairs={{1,0},{0,1},{3,2},{2,3},{5,4},{4,5},{7,6},{6,7},{9,8},{8,9},{11,10... | collective-permute-start | bytes 1572872 | tf_op jit(solution)/shard_map/ppermute | solution.py:42
  119.5 9.6 %collective-permute-start.29 = (bf16[128,1024]{1,0:T(8,128)(2,1)S(1)}, bf16[128,1024]{1,0:T(8,128)(2,1)S(1)}, u32[]{:S(2)}, u32[]{:S(2)}) collective-permute-start(bf16[128,1024]{1,0:T(8,128)(2,1)S(1)} %get-tuple-element.112), channel_id=1, source_target_pairs={{96,0},{97,1},{98,2},{99,3},{100,4},{101,5},{102,6},{103,7},{104,8... | collective-permute-start | bytes 786440 | tf_op jit(solution)/shard_map/ppermute | solution.py:42
  119.6 10.4 %collective-permute-start.31 = (bf16[128,1024]{1,0:T(8,128)(2,1)S(1)}, bf16[128,1024]{1,0:T(8,128)(2,1)S(1)}, u32[]{:S(2)}, u32[]{:S(2)}) collective-permute-start(bf16[128,1024]{1,0:T(8,128)(2,1)S(1)} %get-tuple-element.111), channel_id=1, source_target_pairs={{6,0},{7,1},{0,2},{1,3},{2,4},{3,5},{4,6},{5,7},{14,8},{15,9},{8,1... | collective-permute-start | bytes 786440 | tf_op jit(solution)/shard_map/ppermute | solution.py:42
  119.8 11.8 %collective-permute-start.26 = (bf16[128,1024]{1,0:T(8,128)(2,1)S(1)}, bf16[128,1024]{1,0:T(8,128)(2,1)S(1)}, u32[]{:S(2)}, u32[]{:S(2)}) collective-permute-start(bf16[128,1024]{1,0:T(8,128)(2,1)S(1)} %get-tuple-element.91), channel_id=1, source_target_pairs={{48,0},{49,1},{50,2},{51,3},{52,4},{53,5},{54,6},{55,7},{56,8},{57... | collective-permute-start | bytes 786440 | tf_op jit(solution)/shard_map/ppermute | solution.py:42
  124.1 12.0 %collective-permute-start.27 = (bf16[128,1024]{1,0:T(8,128)(2,1)S(1)}, bf16[128,1024]{1,0:T(8,128)(2,1)S(1)}, u32[]{:S(2)}, u32[]{:S(2)}) collective-permute-start(bf16[128,1024]{1,0:T(8,128)(2,1)S(1)} %get-tuple-element.92), channel_id=1, source_target_pairs={{64,0},{65,1},{66,2},{67,3},{68,4},{69,5},{70,6},{71,7},{72,8},{73... | collective-permute-start | bytes 786440 | tf_op jit(solution)/shard_map/ppermute | solution.py:42
  124.4 13.8 %collective-permute-start.33 = (bf16[128,1024]{1,0:T(8,128)(2,1)S(1)}, bf16[128,1024]{1,0:T(8,128)(2,1)S(1)}, u32[]{:S(2)}, u32[]{:S(2)}) collective-permute-start(bf16[128,1024]{1,0:T(8,128)(2,1)S(1)} %convert_element_type.97), channel_id=1, source_target_pairs={{16,0},{17,1},{18,2},{19,3},{20,4},{21,5},{22,6},{23,7},{24,8},{25... | collective-permute-start | bytes 786440 | tf_op jit(solution)/shard_map/ppermute | solution.py:42
  129.2 19.7 %collective-permute-start.30 = (bf16[128,1024]{1,0:T(8,128)(2,1)S(1)}, bf16[128,1024]{1,0:T(8,128)(2,1)S(1)}, u32[]{:S(2)}, u32[]{:S(2)}) collective-permute-start(bf16[128,1024]{1,0:T(8,128)(2,1)S(1)} %add_convert_fusion.4), channel_id=1, source_target_pairs={{112,0},{113,1},{114,2},{115,3},{116,4},{117,5},{118,6},{119,7},{1... | collective-permute-start | bytes 786440 | tf_op jit(solution)/shard_map/ppermute | solution.py:42
  130.0 10.9 %copy-start.2 = (bf16[128,1024]{1,0:T(8,128)(2,1)S(1)}, bf16[128,1024]{1,0:T(8,128)(2,1)}, u32[]{:S(2)}) copy-start(bf16[128,1024]{1,0:T(8,128)(2,1)} %student.1) | copy-start | bytes 786436
  130.4 18.5 %collective-permute-start.32 = (bf16[128,1024]{1,0:T(8,128)(2,1)S(1)}, bf16[128,1024]{1,0:T(8,128)(2,1)S(1)}, u32[]{:S(2)}, u32[]{:S(2)}) collective-permute-start(bf16[128,1024]{1,0:T(8,128)(2,1)S(1)} %get-tuple-element.110), channel_id=1, source_target_pairs={{30,0},{31,1},{24,2},{25,3},{26,4},{27,5},{28,6},{29,7},{22,8},{23... | collective-permute-start | bytes 786440 | tf_op jit(solution)/shard_map/ppermute | solution.py:42
  131.6 13.4 %collective-permute-start.34 = (bf16[128,1024]{1,0:T(8,128)(2,1)S(1)}, bf16[128,1024]{1,0:T(8,128)(2,1)S(1)}, u32[]{:S(2)}, u32[]{:S(2)}) collective-permute-start(bf16[128,1024]{1,0:T(8,128)(2,1)S(1)} %get-tuple-element.100), channel_id=1, source_target_pairs={{24,0},{25,1},{26,2},{27,3},{28,4},{29,5},{30,6},{31,7},{16,8},{17... | collective-permute-start | bytes 786440 | tf_op jit(solution)/shard_map/ppermute | solution.py:42
  136.1 12.8 %collective-permute-start.35 = (bf16[128,1024]{1,0:T(8,128)(2,1)S(1)}, bf16[128,1024]{1,0:T(8,128)(2,1)S(1)}, u32[]{:S(2)}, u32[]{:S(2)}) collective-permute-start(bf16[128,1024]{1,0:T(8,128)(2,1)S(1)} %get-tuple-element.102), channel_id=1, source_target_pairs={{2,0},{3,1},{4,2},{5,3},{6,4},{7,5},{0,6},{1,7},{10,8},{11,9},{12,... | collective-permute-start | bytes 786440 | tf_op jit(solution)/shard_map/ppermute | solution.py:42
  138.2 10.7 %collective-permute-start.36 = (bf16[128,1024]{1,0:T(8,128)(2,1)S(1)}, bf16[128,1024]{1,0:T(8,128)(2,1)S(1)}, u32[]{:S(2)}, u32[]{:S(2)}) collective-permute-start(bf16[128,1024]{1,0:T(8,128)(2,1)S(1)} %get-tuple-element.104), channel_id=1, source_target_pairs={{4,0},{5,1},{6,2},{7,3},{0,4},{1,5},{2,6},{3,7},{12,8},{13,9},{14,... | collective-permute-start | bytes 786440 | tf_op jit(solution)/shard_map/ppermute | solution.py:42

commit v4 on v3

--- a/solution.py
+++ b/solution.py
@@ -246,7 +246,8 @@
     for (name, first), array in list(late.items()):
         late[name[:3] + "s", first] = swap(array)
     siblings = swap(after(siblings, *late.values()))
-    back = [give(value, name) for name, value in zip(early, done)]
+    sum_001, outer = done[0], done[2:]
+    back = [give(done[1], "003o")]
 
     near = ["010o", "300o", "030o", "200o"]
     crossing, *done = phase(
@@ -255,17 +256,24 @@
         [(["032s", "210s"], bf16)] + [([name], f32) for name in ["032o", "210o", "031o", "110o"] + near],
     )
     sums = dict(zip(["032o", "210o", "031o", "110o"] + near, done))
-    crossing, siblings, back[0], back[1] = lax.optimization_barrier((crossing, siblings, back[0], back[1]))
+    crossing, siblings = lax.optimization_barrier((crossing, siblings))
     crossing = swap(crossing).astype(f32)
     for i, name in enumerate(names_s):
         if name[:3] + "o" in sums:
             sums[name[:3] + "o"] += siblings[i * ROWS : (i + 1) * ROWS].astype(f32)
-    to_031 = fetch((sums["032o"] + crossing[:ROWS]).astype(bf16), (0, 0, 3))
-    to_110 = fetch((sums["210o"] + crossing[ROWS:]).astype(bf16), (3, 0, 0))
-    send_031 = (sums["031o"] + to_031.astype(f32)).astype(bf16)
-    send_110 = (sums["110o"] + to_110.astype(f32)).astype(bf16)
-    back += [give(send_031, "031o"), give(send_110, "110o"), give(sums["030o"].astype(bf16), "030o")]
-    back += [give(after(sums[name].astype(bf16), send_031, send_110), name) for name in ("010o", "300o", "200o")]
+    back[0], far_032, far_210, last_110, *aside = lax.optimization_barrier((
+        back[0],
+        sums["032o"] + crossing[:ROWS], sums["210o"] + crossing[ROWS:],
+        sums["110o"].astype(bf16), sums["300o"].astype(bf16), sums["030o"].astype(bf16),
+    ))
+    up = fetch(jnp.concatenate([far_032.astype(bf16), sum_001]), (0, 0, 3))
+    along = fetch(jnp.concatenate([far_210, sums["010o"]]).astype(bf16), (0, 3, 0))
+    back += [up[ROWS:], along[ROWS:]]
+    send_031 = (sums["031o"] + up[:ROWS].astype(f32)).astype(bf16)
+    send_200 = (sums["200o"] + along[:ROWS].astype(f32)).astype(bf16)
+    back += [give(send_031, "031o"), give(send_200, "200o")]
+    back += [give(value, name) for name, value in zip(("300o", "030o"), aside)]
+    back += [give(after(value, send_031, send_200), name) for name, value in zip(["110o"] + early[2:], [last_110] + outer)]
 
     summed = home + siblings[:ROWS].astype(f32)
     for value in back:

time: 153 us -> 155 us (1.013)
  waiting for transfers between devices: 74.5 us -> 82.6 us
  starting transfers between devices: 42.7 us -> 37.6 us
    ppermute x37 -> x35, waiting for transfers between devices: 74.5 us -> 82.6 us  [fetch(): return lax.ppermute(block, ('chip', 'core'), pairs)]
    ppermute x37 -> x35, starting transfers between devices: 42.7 us -> 37.6 us  [fetch(): return lax.ppermute(block, ('chip', 'core'), pairs)]
  transfers between devices with their start and end apart: 37 -> 35, of which waited for: 20 -> 18; matrix products, arithmetic and copies ran while one was open for 1% -> 1% of each run, Pallas kernels for 17% -> 17%
where the time goes in v4:
time: 155 us; the launch traced here: 154 us
  waiting for transfers between devices  82.6 us (53%)
  starting transfers between devices  37.6 us (24%)
  Pallas kernels  29.2 us (19%)
  other arithmetic  2.49 us (2%)
    ppermute x35, waiting for transfers between devices, fetch(): return lax.ppermute(block, ('chip', 'core'), pairs)  82.6 us
    ppermute x35, starting transfers between devices, fetch(): return lax.ppermute(block, ('chip', 'core'), pairs)  37.6 us
    pallas_call x3, Pallas kernels, phase(): pl.pallas_call(functools.partial(phase_kernel, layout, groups, [(n, f) fo...  26 us
    pallas_call x1, Pallas kernels, unit_rows(): pl.pallas_call(unit_kernel, out_shape=jax.ShapeDtypeStruct((ROWS, WIDE),...  3.11 us
  transfers between devices with their start and end apart: 35, of which 18 were waited for; matrix products, arithmetic and copies ran while one was open for 1% of the time, Pallas kernels for 17%

profile of v4, /device:TPU:0, one launch (start us, length us, event | category | flops | bytes accessed | tf_op | source)
XLA Modules:
  0.0 153.5 jit_solution(11637785074196707371)
XLA Ops:
  0.0 3.1 %unit_rows.1.refs_1_ = bf16[128,5120]{1,0:T(8,128)(2,1)} custom-call(bf16[128,1024]{1,0:T(8,128)(2,1)} %student.1, bf16[128,4096]{1,0:T(8,128)(2,1)} %teacher.1), custom_call_target="tpu_custom_call" | custom-call | tf_op jit(solution)/shard_map/unit_rows/pallas_call | solution.py:67
  3.1 0.1 collective-permute-start
  3.2 3.2 %collective-permute-start.3 = (bf16[128,5120]{1,0:T(8,128)(2,1)}, bf16[128,5120]{1,0:T(8,128)(2,1)S(1)}, u32[]{:S(2)}, u32[]{:S(2)}) collective-permute-start(bf16[128,5120]{1,0:T(8,128)(2,1)} %unit_rows.1.refs_1_), channel_id=1, source_target_pairs={{16,0},{17,1},{18,2},{19,3},{20,4},{21,5},{22,6},{23,7},{24,8},{25... | collective-permute-start | bytes 3932168 | tf_op jit(solution)/shard_map/ppermute | solution.py:42
  6.4 0.1 collective-permute-done.refs_0_
  6.4 4.1 %collective-permute-start.1 = (bf16[128,5120]{1,0:T(8,128)(2,1)}, bf16[128,5120]{1,0:T(8,128)(2,1)S(1)}, u32[]{:S(2)}, u32[]{:S(2)}) collective-permute-start(bf16[128,5120]{1,0:T(8,128)(2,1)} %unit_rows.1.refs_1_), channel_id=1, source_target_pairs={{32,0},{33,1},{34,2},{35,3},{36,4},{37,5},{38,6},{39,7},{40,8},{41... | collective-permute-start | bytes 3932168 | tf_op jit(solution)/shard_map/ppermute | solution.py:42
  10.6 1.5 collective-permute-start.5
  12.1 1.6 %collective-permute-start.8 = (bf16[128,5120]{1,0:T(8,128)(2,1)}, bf16[128,5120]{1,0:T(8,128)(2,1)S(1)}, u32[]{:S(2)}, u32[]{:S(2)}) collective-permute-start(bf16[128,5120]{1,0:T(8,128)(2,1)} %unit_rows.1.refs_1_), channel_id=1, source_target_pairs={{24,0},{25,1},{26,2},{27,3},{28,4},{29,5},{30,6},{31,7},{16,8},{17... | collective-permute-start | bytes 3932168 | tf_op jit(solution)/shard_map/ppermute | solution.py:42
  13.6 21.7 %collective-permute-done.3.refs_7_.refs_2_.refs_0_ = bf16[128,5120]{1,0:T(8,128)(2,1)S(1)} collective-permute-done((bf16[128,5120]{1,0:T(8,128)(2,1)}, bf16[128,5120]{1,0:T(8,128)(2,1)S(1)}, u32[]{:S(2)}, u32[]{:S(2)}) %collective-permute-start.3) | collective-permute-done | bytes 1310752 | tf_op jit(solution)/shard_map/ppermute | solution.py:42
  35.3 3.9 %collective-permute-done.1.refs_2_.refs_10_ = bf16[128,5120]{1,0:T(8,128)(2,1)S(1)} collective-permute-done((bf16[128,5120]{1,0:T(8,128)(2,1)}, bf16[128,5120]{1,0:T(8,128)(2,1)S(1)}, u32[]{:S(2)}, u32[]{:S(2)}) %collective-permute-start.1) | collective-permute-done | bytes 1310752 | tf_op jit(solution)/shard_map/ppermute | solution.py:42
  39.2 0.0 collective-permute-start.4
  39.2 3.3 %collective-permute-done.5.refs_5_.refs_4_.refs_1_ = bf16[128,5120]{1,0:T(8,128)(2,1)S(1)} collective-permute-done((bf16[128,5120]{1,0:T(8,128)(2,1)}, bf16[128,5120]{1,0:T(8,128)(2,1)S(1)}, u32[]{:S(2)}, u32[]{:S(2)}) %collective-permute-start.5) | collective-permute-done | bytes 1310752 | tf_op jit(solution)/shard_map/ppermute | solution.py:42
  42.5 1.5 %collective-permute-start.11 = (bf16[128,5120]{1,0:T(8,128)(2,1)S(1)}, bf16[128,5120]{1,0:T(8,128)(2,1)S(1)}, u32[]{:S(2)}, u32[]{:S(2)}) collective-permute-start(bf16[128,5120]{1,0:T(8,128)(2,1)S(1)} %collective-permute-done.3.refs_7_.refs_2_.refs_0_), channel_id=1, source_target_pairs={{2,0},{3,1},{4,2},{5,3},{6,4},{7,5},{0,6},{1,7},{10,8},{11,9},{12,... | collective-permute-start | bytes 3932168 | tf_op jit(solution)/shard_map/ppermute | solution.py:42
  44.1 1.1 collective-permute-start.12
  45.2 1.6 %collective-permute-start.9 = (bf16[128,5120]{1,0:T(8,128)(2,1)S(1)}, bf16[128,5120]{1,0:T(8,128)(2,1)S(1)}, u32[]{:S(2)}, u32[]{:S(2)}) collective-permute-start(bf16[128,5120]{1,0:T(8,128)(2,1)S(1)} %collective-permute-done.8.refs_4_.refs_8_), channel_id=1, source_target_pairs={{32,0},{33,1},{34,2},{35,3},{36,4},{37,5},{38,6},{39,7},{40,8},{41... | collective-permute-start | bytes 3932168 | tf_op jit(solution)/shard_map/ppermute | solution.py:42
  46.8 0.5 collective-permute-start.7
  47.3 1.6 %collective-permute-start.10 = (bf16[128,5120]{1,0:T(8,128)(2,1)S(1)}, bf16[128,5120]{1,0:T(8,128)(2,1)S(1)}, u32[]{:S(2)}, u32[]{:S(2)}) collective-permute-start(bf16[128,5120]{1,0:T(8,128)(2,1)S(1)} %collective-permute-done.2.refs_3_.refs_9_), channel_id=1, source_target_pairs={{24,0},{25,1},{26,2},{27,3},{28,4},{29,5},{30,6},{31,7},{16,8},{17... | collective-permute-start | bytes 3932168 | tf_op jit(solution)/shard_map/ppermute | solution.py:42
  48.9 1.3 copy-done
  50.2 8.5 %phase_1.1.refs_16_ = f32[1152,1024]{1,0:T(8,128)S(1)} custom-call(bf16[128,5120]{1,0:T(8,128)(2,1)S(1)} %collective-permute-done.refs_0_, bf16[128,5120]{1,0:T(8,128)(2,1)S(1)} %copy-done, bf16[128,5120]{1,0:T(8,128)(2,1)S(1)} %collective-permute-done.1.refs_2_.refs_10_, bf16[128,5120]{1,0:T(8,128)(2,1)S(1)} %collective-permute-done.2.refs_3_.refs_9_, ...), custom_call_target="tpu_custom_call" | custom-call | flops 10334765056 | bytes 11796480 | tf_op jit(solution)/shard_map/phase_1/pallas_call | solution.py:183
  58.6 16.5 %collective-permute-done.9.refs_12_.refs_5_ = bf16[128,5120]{1,0:T(8,128)(2,1)S(1)} collective-permute-done((bf16[128,5120]{1,0:T(8,128)(2,1)S(1)}, bf16[128,5120]{1,0:T(8,128)(2,1)S(1)}, u32[]{:S(2)}, u32[]{:S(2)}) %collective-permute-start.9) | collective-permute-done | bytes 1310752 | tf_op jit(solution)/shard_map/ppermute | solution.py:42
  75.2 1.0 collective-permute-done.12.refs_6_.refs_3_
  76.2 1.4 collective-permute-done.7.refs_11_
  77.6 0.3 collective-permute-done.10.refs_13_
  77.9 0.5 collective-permute-start.14
  78.6 3.0 %collective-permute-start.15 = (bf16[128,2560]{1,0:T(8,128)(2,1)S(1)}, bf16[128,2560]{1,0:T(8,128)(2,1)S(1)}, u32[]{:S(2)}, u32[]{:S(2)}) collective-permute-start(bf16[128,2560]{1,0:T(8,128)(2,1)S(1)} %slice.45), channel_id=1, source_target_pairs={{2,0},{3,1},{4,2},{5,3},{6,4},{7,5},{0,6},{1,7},{10,8},{11,9},{12,... | collective-permute-start | bytes 1966088 | tf_op jit(solution)/shard_map/ppermute | solution.py:42
  81.6 2.7 %collective-permute-start.16 = (bf16[128,2560]{1,0:T(8,128)(2,1)S(1)}, bf16[128,2560]{1,0:T(8,128)(2,1)S(1)}, u32[]{:S(2)}, u32[]{:S(2)}) collective-permute-start(bf16[128,2560]{1,0:T(8,128)(2,1)S(1)} %slice.46), channel_id=1, source_target_pairs={{16,0},{17,1},{18,2},{19,3},{20,4},{21,5},{22,6},{23,7},{24,8},{25... | collective-permute-start | bytes 1966088 | tf_op jit(solution)/shard_map/ppermute | solution.py:42
  84.3 1.8 %collective-permute-start.17 = (bf16[128,2560]{1,0:T(8,128)(2,1)S(1)}, bf16[128,2560]{1,0:T(8,128)(2,1)S(1)}, u32[]{:S(2)}, u32[]{:S(2)}) collective-permute-start(bf16[128,2560]{1,0:T(8,128)(2,1)S(1)} %slice.47), channel_id=1, source_target_pairs={{32,0},{33,1},{34,2},{35,3},{36,4},{37,5},{38,6},{39,7},{40,8},{41... | collective-permute-start | bytes 1966088 | tf_op jit(solution)/shard_map/ppermute | solution.py:42
  86.2 0.4 collective-permute-start.18
  86.5 12.6 %phase_2.1 = (bf16[640,1024]{1,0:T(8,128)(2,1)S(1)}, f32[768,1024]{1,0:T(8,128)S(1)}, f32[128,1024]{1,0:T(8,128)S(1)}, bf16[128,1024]{1,0:T(8,128)(2,1)S(1)}, bf...) custom-call(bf16[128,5120]{1,0:T(8,128)(2,1)S(1)} %collective-permute-done.refs_0_, ...), custom_call_target="tpu_custom_call" | custom-call | flops 16911433728 | bytes 25690112 | tf_op jit(solution)/shard_map/phase_2/pallas_call | solution.py:183
  99.1 1.3 collective-permute-done.17.refs_8_
  100.5 2.8 %collective-permute-done.18.refs_9_ = bf16[128,2560]{1,0:T(8,128)(2,1)S(1)} collective-permute-done((bf16[128,2560]{1,0:T(8,128)(2,1)S(1)}, bf16[128,2560]{1,0:T(8,128)(2,1)S(1)}, u32[]{:S(2)}, u32[]{:S(2)}) %collective-permute-start.18) | collective-permute-done | bytes 655392 | tf_op jit(solution)/shard_map/ppermute | solution.py:42
  103.3 0.5 collective-permute-start.20
  103.8 0.0 collective-permute-start.21
  103.8 0.5 collective-permute-start.22
  104.3 1.1 collective-permute-done.19.refs_10_
  105.4 0.9 collective-permute-done.20.refs_11_
  106.3 0.9 collective-permute-done.21.refs_12_
  107.2 0.9 collective-permute-done.22.refs_13_
  108.2 0.1 collective-permute-start.23
  108.3 5.0 %phase_3.1 = (bf16[256,1024]{1,0:T(8,128)(2,1)S(1)}, f32[128,1024]{1,0:T(8,128)S(1)}, f32[128,1024]{1,0:T(8,128)S(1)}, f32[128,1024]{1,0:T(8,128)S(1)}, f32[128,...) custom-call(bf16[128,5120]{1,0:T(8,128)(2,1)S(1)} %collective-permut, ...), custom_call_target="tpu_custom_call" | custom-call | flops 6576668672 | bytes 16252928 | tf_op jit(solution)/shard_map/phase_3/pallas_call | solution.py:183
  113.3 0.5 collective-permute-start.25
  113.8 0.2 collective-permute-start.24
  114.0 0.3 add_convert_fusion.2
  114.2 1.1 collective-permute-done.25
  115.3 0.1 convert_element_type.78
  115.4 0.2 slice_add_fusion
  115.6 6.5 %collective-permute-done.24 = bf16[128,1024]{1,0:T(8,128)(2,1)S(1)} collective-permute-done((bf16[128,1024]{1,0:T(8,128)(2,1)S(1)}, bf16[128,1024]{1,0:T(8,128)(2,1)S(1)}, u32[]{:S(2)}, u32[]{:S(2)}) %collective-permute-start.24) | collective-permute-done | bytes 262176 | tf_op jit(solution)/shard_map/ppermute | solution.py:42
  122.2 0.3 collective-permute-start.27
  122.6 0.0 copy-start.2
  122.6 0.1 collective-permute-start.26
  122.7 3.0 %collective-permute-start.31 = (bf16[128,1024]{1,0:T(8,128)(2,1)S(1)}, bf16[128,1024]{1,0:T(8,128)(2,1)S(1)}, u32[]{:S(2)}, u32[]{:S(2)}) collective-permute-start(bf16[128,1024]{1,0:T(8,128)(2,1)S(1)} %convert_element_type.83), channel_id=1, source_target_pairs={{16,0},{17,1},{18,2},{19,3},{20,4},{21,5},{22,6},{23,7},{24,8},{25... | collective-permute-start | bytes 786440 | tf_op jit(solution)/shard_map/ppermute | solution.py:42
  125.7 0.4 collective-permute-start.30
  126.1 10.5 %collective-permute-done.27 = bf16[256,1024]{1,0:T(8,128)(2,1)S(1)} collective-permute-done((bf16[256,1024]{1,0:T(8,128)(2,1)S(1)}, bf16[256,1024]{1,0:T(8,128)(2,1)S(1)}, u32[]{:S(2)}, u32[]{:S(2)}) %collective-permute-start.27) | collective-permute-done | bytes 524320 | tf_op jit(solution)/shard_map/ppermute | solution.py:42
  136.6 0.1 add_convert_fusion
  136.7 0.1 collective-permute-start.29
  136.8 0.1 add_convert_fusion.1
  136.9 1.4 collective-permute-start.28
  138.3 2.8 %collective-permute-start.34 = (bf16[128,1024]{1,0:T(8,128)(2,1)S(1)}, bf16[128,1024]{1,0:T(8,128)(2,1)S(1)}, u32[]{:S(2)}, u32[]{:S(2)}) collective-permute-start(bf16[128,1024]{1,0:T(8,128)(2,1)S(1)} %get-tuple-element.112), channel_id=1, source_target_pairs={{64,0},{65,1},{66,2},{67,3},{68,4},{69,5},{70,6},{71,7},{72,8},{73... | collective-permute-start | bytes 786440 | tf_op jit(solution)/shard_map/ppermute | solution.py:42
  141.1 1.1 collective-permute-start.33
  142.2 1.3 collective-permute-start.32
  143.5 0.1 fusion.5
  143.7 8.2 %collective-permute-done.34 = bf16[128,1024]{1,0:T(8,128)(2,1)S(1)} collective-permute-done((bf16[128,1024]{1,0:T(8,128)(2,1)S(1)}, bf16[128,1024]{1,0:T(8,128)(2,1)S(1)}, u32[]{:S(2)}, u32[]{:S(2)}) %collective-permute-start.34) | collective-permute-done | bytes 262176 | tf_op jit(solution)/shard_map/ppermute | solution.py:42
  151.9 0.0 collective-permute-done.32
  151.9 0.6 fusion.2
  152.5 1.0 fusion.4
  (32 shorter events, 0.3 us)
Async XLA Ops:
  3.1 3.3 %collective-permute-start = (bf16[128,5120]{1,0:T(8,128)(2,1)}, bf16[128,5120]{1,0:T(8,128)(2,1)S(1)}, u32[]{:S(2)}, u32[]{:S(2)}) collective-permute-start(bf16[128,5120]{1,0:T(8,128)(2,1)} %unit_rows.1.refs_1_), channel_id=1, source_target_pairs={{1,0},{0,1},{3,2},{2,3},{5,4},{4,5},{7,6},{6,7},{9,8},{8,9},{11,10... | collective-permute-start | bytes 3932168 | tf_op jit(solution)/shard_map/ppermute | solution.py:42
  3.2 32.1 %collective-permute-start.3 = (bf16[128,5120]{1,0:T(8,128)(2,1)}, bf16[128,5120]{1,0:T(8,128)(2,1)S(1)}, u32[]{:S(2)}, u32[]{:S(2)}) collective-permute-start(bf16[128,5120]{1,0:T(8,128)(2,1)} %unit_rows.1.refs_1_), channel_id=1, source_target_pairs={{16,0},{17,1},{18,2},{19,3},{20,4},{21,5},{22,6},{23,7},{24,8},{25... | collective-permute-start | bytes 3932168 | tf_op jit(solution)/shard_map/ppermute | solution.py:42
  6.4 32.8 %collective-permute-start.1 = (bf16[128,5120]{1,0:T(8,128)(2,1)}, bf16[128,5120]{1,0:T(8,128)(2,1)S(1)}, u32[]{:S(2)}, u32[]{:S(2)}) collective-permute-start(bf16[128,5120]{1,0:T(8,128)(2,1)} %unit_rows.1.refs_1_), channel_id=1, source_target_pairs={{32,0},{33,1},{34,2},{35,3},{36,4},{37,5},{38,6},{39,7},{40,8},{41... | collective-permute-start | bytes 3932168 | tf_op jit(solution)/shard_map/ppermute | solution.py:42
  10.6 32.0 %collective-permute-start.5 = (bf16[128,5120]{1,0:T(8,128)(2,1)}, bf16[128,5120]{1,0:T(8,128)(2,1)S(1)}, u32[]{:S(2)}, u32[]{:S(2)}) collective-permute-start(bf16[128,5120]{1,0:T(8,128)(2,1)} %unit_rows.1.refs_1_), channel_id=1, source_target_pairs={{6,0},{7,1},{0,2},{1,3},{2,4},{3,5},{4,6},{5,7},{14,8},{15,9},{8,1... | collective-permute-start | bytes 3932168 | tf_op jit(solution)/shard_map/ppermute | solution.py:42
  12.1 32.0 %collective-permute-start.2 = (bf16[128,5120]{1,0:T(8,128)(2,1)}, bf16[128,5120]{1,0:T(8,128)(2,1)S(1)}, u32[]{:S(2)}, u32[]{:S(2)}) collective-permute-start(bf16[128,5120]{1,0:T(8,128)(2,1)} %unit_rows.1.refs_1_), channel_id=1, source_target_pairs={{96,0},{97,1},{98,2},{99,3},{100,4},{101,5},{102,6},{103,7},{104,8... | collective-permute-start | bytes 3932168 | tf_op jit(solution)/shard_map/ppermute | solution.py:42
  12.1 33.2 %collective-permute-start.8 = (bf16[128,5120]{1,0:T(8,128)(2,1)}, bf16[128,5120]{1,0:T(8,128)(2,1)S(1)}, u32[]{:S(2)}, u32[]{:S(2)}) collective-permute-start(bf16[128,5120]{1,0:T(8,128)(2,1)} %unit_rows.1.refs_1_), channel_id=1, source_target_pairs={{24,0},{25,1},{26,2},{27,3},{28,4},{29,5},{30,6},{31,7},{16,8},{17... | collective-permute-start | bytes 3932168 | tf_op jit(solution)/shard_map/ppermute | solution.py:42
  39.2 7.6 %collective-permute-start.4 = (bf16[128,5120]{1,0:T(8,128)(2,1)S(1)}, bf16[128,5120]{1,0:T(8,128)(2,1)S(1)}, u32[]{:S(2)}, u32[]{:S(2)}) collective-permute-start(bf16[128,5120]{1,0:T(8,128)(2,1)S(1)} %collective-permute-done.3.refs_7_.refs_2_.refs_0_), channel_id=1, source_target_pairs={{1,0},{0,1},{3,2},{2,3},{5,4},{4,5},{7,6},{6,7},{9,8},{8,9},{11,10... | collective-permute-start | bytes 3932168 | tf_op jit(solution)/shard_map/ppermute | solution.py:42
  42.5 4.3 %collective-permute-start.6 = (bf16[128,5120]{1,0:T(8,128)(2,1)S(1)}, bf16[128,5120]{1,0:T(8,128)(2,1)S(1)}, u32[]{:S(2)}, u32[]{:S(2)}) collective-permute-start(bf16[128,5120]{1,0:T(8,128)(2,1)S(1)} %collective-permute-done.5.refs_5_.refs_4_.refs_1_), channel_id=1, source_target_pairs={{1,0},{0,1},{3,2},{2,3},{5,4},{4,5},{7,6},{6,7},{9,8},{8,9},{11,10... | collective-permute-start | bytes 3932168 | tf_op jit(solution)/shard_map/ppermute | solution.py:42
  42.5 32.7 %collective-permute-start.11 = (bf16[128,5120]{1,0:T(8,128)(2,1)S(1)}, bf16[128,5120]{1,0:T(8,128)(2,1)S(1)}, u32[]{:S(2)}, u32[]{:S(2)}) collective-permute-start(bf16[128,5120]{1,0:T(8,128)(2,1)S(1)} %collective-permute-done.3.refs_7_.refs_2_.refs_0_), channel_id=1, source_target_pairs={{2,0},{3,1},{4,2},{5,3},{6,4},{7,5},{0,6},{1,7},{10,8},{11,9},{12,... | collective-permute-start | bytes 3932168 | tf_op jit(solution)/shard_map/ppermute | solution.py:42
  44.1 32.1 %collective-permute-start.12 = (bf16[128,5120]{1,0:T(8,128)(2,1)S(1)}, bf16[128,5120]{1,0:T(8,128)(2,1)S(1)}, u32[]{:S(2)}, u32[]{:S(2)}) collective-permute-start(bf16[128,5120]{1,0:T(8,128)(2,1)S(1)} %collective-permute-done.5.refs_5_.refs_4_.refs_1_), channel_id=1, source_target_pairs={{6,0},{7,1},{0,2},{1,3},{2,4},{3,5},{4,6},{5,7},{14,8},{15,9},{8,1... | collective-permute-start | bytes 3932168 | tf_op jit(solution)/shard_map/ppermute | solution.py:42
  45.2 30.0 %collective-permute-start.9 = (bf16[128,5120]{1,0:T(8,128)(2,1)S(1)}, bf16[128,5120]{1,0:T(8,128)(2,1)S(1)}, u32[]{:S(2)}, u32[]{:S(2)}) collective-permute-start(bf16[128,5120]{1,0:T(8,128)(2,1)S(1)} %collective-permute-done.8.refs_4_.refs_8_), channel_id=1, source_target_pairs={{32,0},{33,1},{34,2},{35,3},{36,4},{37,5},{38,6},{39,7},{40,8},{41... | collective-permute-start | bytes 3932168 | tf_op jit(solution)/shard_map/ppermute | solution.py:42
  46.8 30.8 %collective-permute-start.7 = (bf16[128,5120]{1,0:T(8,128)(2,1)S(1)}, bf16[128,5120]{1,0:T(8,128)(2,1)S(1)}, u32[]{:S(2)}, u32[]{:S(2)}) collective-permute-start(bf16[128,5120]{1,0:T(8,128)(2,1)S(1)} %collective-permute-done.2.refs_3_.refs_9_), channel_id=1, source_target_pairs={{96,0},{97,1},{98,2},{99,3},{100,4},{101,5},{102,6},{103,7},{104,8... | collective-permute-start | bytes 3932168 | tf_op jit(solution)/shard_map/ppermute | solution.py:42
  47.3 30.7 %collective-permute-start.10 = (bf16[128,5120]{1,0:T(8,128)(2,1)S(1)}, bf16[128,5120]{1,0:T(8,128)(2,1)S(1)}, u32[]{:S(2)}, u32[]{:S(2)}) collective-permute-start(bf16[128,5120]{1,0:T(8,128)(2,1)S(1)} %collective-permute-done.2.refs_3_.refs_9_), channel_id=1, source_target_pairs={{24,0},{25,1},{26,2},{27,3},{28,4},{29,5},{30,6},{31,7},{16,8},{17... | collective-permute-start | bytes 3932168 | tf_op jit(solution)/shard_map/ppermute | solution.py:42
  48.8 1.3 copy-start
  77.9 8.2 %collective-permute-start.13 = (bf16[128,5120]{1,0:T(8,128)(2,1)S(1)}, bf16[128,5120]{1,0:T(8,128)(2,1)S(1)}, u32[]{:S(2)}, u32[]{:S(2)}) collective-permute-start(bf16[128,5120]{1,0:T(8,128)(2,1)S(1)} %collective-permute-done.12.refs_6_.refs_3_), channel_id=1, source_target_pairs={{1,0},{0,1},{3,2},{2,3},{5,4},{4,5},{7,6},{6,7},{9,8},{8,9},{11,10... | collective-permute-start | bytes 3932168 | tf_op jit(solution)/shard_map/ppermute | solution.py:42
  77.9 8.2 %collective-permute-start.14 = (bf16[128,5120]{1,0:T(8,128)(2,1)S(1)}, bf16[128,5120]{1,0:T(8,128)(2,1)S(1)}, u32[]{:S(2)}, u32[]{:S(2)}) collective-permute-start(bf16[128,5120]{1,0:T(8,128)(2,1)S(1)} %collective-permute-done.11.refs_14_.refs_2_), channel_id=1, source_target_pairs={{1,0},{0,1},{3,2},{2,3},{5,4},{4,5},{7,6},{6,7},{9,8},{8,9},{11,10... | collective-permute-start | bytes 3932168 | tf_op jit(solution)/shard_map/ppermute | solution.py:42
  78.6 8.0 %copy-start.1 = (bf16[128,5120]{1,0:T(8,128)(2,1)S(1)}, bf16[128,5120]{1,0:T(8,128)(2,1)}, u32[]{:S(2)}) copy-start(bf16[128,5120]{1,0:T(8,128)(2,1)} %unit_rows.1.refs_1_) | copy-start | bytes 3932164
  78.6 20.6 %collective-permute-start.15 = (bf16[128,2560]{1,0:T(8,128)(2,1)S(1)}, bf16[128,2560]{1,0:T(8,128)(2,1)S(1)}, u32[]{:S(2)}, u32[]{:S(2)}) collective-permute-start(bf16[128,2560]{1,0:T(8,128)(2,1)S(1)} %slice.45), channel_id=1, source_target_pairs={{2,0},{3,1},{4,2},{5,3},{6,4},{7,5},{0,6},{1,7},{10,8},{11,9},{12,... | collective-permute-start | bytes 1966088 | tf_op jit(solution)/shard_map/ppermute | solution.py:42
  81.6 17.6 %collective-permute-start.16 = (bf16[128,2560]{1,0:T(8,128)(2,1)S(1)}, bf16[128,2560]{1,0:T(8,128)(2,1)S(1)}, u32[]{:S(2)}, u32[]{:S(2)}) collective-permute-start(bf16[128,2560]{1,0:T(8,128)(2,1)S(1)} %slice.46), channel_id=1, source_target_pairs={{16,0},{17,1},{18,2},{19,3},{20,4},{21,5},{22,6},{23,7},{24,8},{25... | collective-permute-start | bytes 1966088 | tf_op jit(solution)/shard_map/ppermute | solution.py:42
  84.3 16.2 %collective-permute-start.17 = (bf16[128,2560]{1,0:T(8,128)(2,1)S(1)}, bf16[128,2560]{1,0:T(8,128)(2,1)S(1)}, u32[]{:S(2)}, u32[]{:S(2)}) collective-permute-start(bf16[128,2560]{1,0:T(8,128)(2,1)S(1)} %slice.47), channel_id=1, source_target_pairs={{32,0},{33,1},{34,2},{35,3},{36,4},{37,5},{38,6},{39,7},{40,8},{41... | collective-permute-start | bytes 1966088 | tf_op jit(solution)/shard_map/ppermute | solution.py:42
  86.2 17.1 %collective-permute-start.18 = (bf16[128,2560]{1,0:T(8,128)(2,1)S(1)}, bf16[128,2560]{1,0:T(8,128)(2,1)S(1)}, u32[]{:S(2)}, u32[]{:S(2)}) collective-permute-start(bf16[128,2560]{1,0:T(8,128)(2,1)S(1)} %slice.48), channel_id=1, source_target_pairs={{96,0},{97,1},{98,2},{99,3},{100,4},{101,5},{102,6},{103,7},{104,8... | collective-permute-start | bytes 1966088 | tf_op jit(solution)/shard_map/ppermute | solution.py:42
  103.3 2.1 %collective-permute-start.19 = (bf16[128,2560]{1,0:T(8,128)(2,1)S(1)}, bf16[128,2560]{1,0:T(8,128)(2,1)S(1)}, u32[]{:S(2)}, u32[]{:S(2)}) collective-permute-start(bf16[128,2560]{1,0:T(8,128)(2,1)S(1)} %collective-permute-done.15.refs_6_), channel_id=1, source_target_pairs={{1,0},{0,1},{3,2},{2,3},{5,4},{4,5},{7,6},{6,7},{9,8},{8,9},{11,10... | collective-permute-start | bytes 1966088 | tf_op jit(solution)/shard_map/ppermute | solution.py:42
  103.3 3.0 %collective-permute-start.20 = (bf16[128,2560]{1,0:T(8,128)(2,1)S(1)}, bf16[128,2560]{1,0:T(8,128)(2,1)S(1)}, u32[]{:S(2)}, u32[]{:S(2)}) collective-permute-start(bf16[128,2560]{1,0:T(8,128)(2,1)S(1)} %collective-permute-done.16.refs_7_), channel_id=1, source_target_pairs={{1,0},{0,1},{3,2},{2,3},{5,4},{4,5},{7,6},{6,7},{9,8},{8,9},{11,10... | collective-permute-start | bytes 1966088 | tf_op jit(solution)/shard_map/ppermute | solution.py:42
  103.8 3.5 %collective-permute-start.21 = (bf16[128,2560]{1,0:T(8,128)(2,1)S(1)}, bf16[128,2560]{1,0:T(8,128)(2,1)S(1)}, u32[]{:S(2)}, u32[]{:S(2)}) collective-permute-start(bf16[128,2560]{1,0:T(8,128)(2,1)S(1)} %collective-permute-done.17.refs_8_), channel_id=1, source_target_pairs={{1,0},{0,1},{3,2},{2,3},{5,4},{4,5},{7,6},{6,7},{9,8},{8,9},{11,10... | collective-permute-start | bytes 1966088 | tf_op jit(solution)/shard_map/ppermute | solution.py:42
  103.8 4.4 %collective-permute-start.22 = (bf16[128,2560]{1,0:T(8,128)(2,1)S(1)}, bf16[128,2560]{1,0:T(8,128)(2,1)S(1)}, u32[]{:S(2)}, u32[]{:S(2)}) collective-permute-start(bf16[128,2560]{1,0:T(8,128)(2,1)S(1)} %collective-permute-done.18.refs_9_), channel_id=1, source_target_pairs={{1,0},{0,1},{3,2},{2,3},{5,4},{4,5},{7,6},{6,7},{9,8},{8,9},{11,10... | collective-permute-start | bytes 1966088 | tf_op jit(solution)/shard_map/ppermute | solution.py:42
  108.2 5.1 %collective-permute-start.23 = (bf16[640,1024]{1,0:T(8,128)(2,1)S(1)}, bf16[640,1024]{1,0:T(8,128)(2,1)S(1)}, u32[]{:S(2)}, u32[]{:S(2)}) collective-permute-start(bf16[640,1024]{1,0:T(8,128)(2,1)S(1)} %get-tuple-element.89), channel_id=1, source_target_pairs={{1,0},{0,1},{3,2},{2,3},{5,4},{4,5},{7,6},{6,7},{9,8},{8,9},{11,10... | collective-permute-start | bytes 3932168 | tf_op jit(solution)/shard_map/ppermute | solution.py:42
  113.3 2.0 %collective-permute-start.25 = (bf16[256,1024]{1,0:T(8,128)(2,1)S(1)}, bf16[256,1024]{1,0:T(8,128)(2,1)S(1)}, u32[]{:S(2)}, u32[]{:S(2)}) collective-permute-start(bf16[256,1024]{1,0:T(8,128)(2,1)S(1)} %get-tuple-element.93), channel_id=1, source_target_pairs={{1,0},{0,1},{3,2},{2,3},{5,4},{4,5},{7,6},{6,7},{9,8},{8,9},{11,10... | collective-permute-start | bytes 1572872 | tf_op jit(solution)/shard_map/ppermute | solution.py:42
  113.8 8.3 %collective-permute-start.24 = (bf16[128,1024]{1,0:T(8,128)(2,1)S(1)}, bf16[128,1024]{1,0:T(8,128)(2,1)S(1)}, u32[]{:S(2)}, u32[]{:S(2)}) collective-permute-start(bf16[128,1024]{1,0:T(8,128)(2,1)S(1)} %get-tuple-element.91), channel_id=1, source_target_pairs={{32,0},{33,1},{34,2},{35,3},{36,4},{37,5},{38,6},{39,7},{40,8},{41... | collective-permute-start | bytes 786440 | tf_op jit(solution)/shard_map/ppermute | solution.py:42
  122.2 14.4 %collective-permute-start.27 = (bf16[256,1024]{1,0:T(8,128)(2,1)S(1)}, bf16[256,1024]{1,0:T(8,128)(2,1)S(1)}, u32[]{:S(2)}, u32[]{:S(2)}) collective-permute-start(bf16[256,1024]{1,0:T(8,128)(2,1)S(1)} %pad_maximum_fusion.1), channel_id=1, source_target_pairs={{24,0},{25,1},{26,2},{27,3},{28,4},{29,5},{30,6},{31,7},{16,8},{17... | collective-permute-start | bytes 1572872 | tf_op jit(solution)/shard_map/ppermute | solution.py:42
  122.6 21.0 %copy-start.2 = (bf16[128,1024]{1,0:T(8,128)(2,1)S(1)}, bf16[128,1024]{1,0:T(8,128)(2,1)}, u32[]{:S(2)}) copy-start(bf16[128,1024]{1,0:T(8,128)(2,1)} %student.1) | copy-start | bytes 786436
  122.6 14.2 %collective-permute-start.26 = (bf16[256,1024]{1,0:T(8,128)(2,1)S(1)}, bf16[256,1024]{1,0:T(8,128)(2,1)S(1)}, u32[]{:S(2)}, u32[]{:S(2)}) collective-permute-start(bf16[256,1024]{1,0:T(8,128)(2,1)S(1)} %pad_maximum_fusion), channel_id=1, source_target_pairs={{96,0},{97,1},{98,2},{99,3},{100,4},{101,5},{102,6},{103,7},{104,8... | collective-permute-start | bytes 1572872 | tf_op jit(solution)/shard_map/ppermute | solution.py:42
  122.7 18.5 %collective-permute-start.31 = (bf16[128,1024]{1,0:T(8,128)(2,1)S(1)}, bf16[128,1024]{1,0:T(8,128)(2,1)S(1)}, u32[]{:S(2)}, u32[]{:S(2)}) collective-permute-start(bf16[128,1024]{1,0:T(8,128)(2,1)S(1)} %convert_element_type.83), channel_id=1, source_target_pairs={{16,0},{17,1},{18,2},{19,3},{20,4},{21,5},{22,6},{23,7},{24,8},{25... | collective-permute-start | bytes 786440 | tf_op jit(solution)/shard_map/ppermute | solution.py:42
  125.7 16.6 %collective-permute-start.30 = (bf16[128,1024]{1,0:T(8,128)(2,1)S(1)}, bf16[128,1024]{1,0:T(8,128)(2,1)S(1)}, u32[]{:S(2)}, u32[]{:S(2)}) collective-permute-start(bf16[128,1024]{1,0:T(8,128)(2,1)S(1)} %get-tuple-element.105), channel_id=1, source_target_pairs={{2,0},{3,1},{4,2},{5,3},{6,4},{7,5},{0,6},{1,7},{10,8},{11,9},{12,... | collective-permute-start | bytes 786440 | tf_op jit(solution)/shard_map/ppermute | solution.py:42
  136.7 15.2 %collective-permute-start.29 = (bf16[128,1024]{1,0:T(8,128)(2,1)S(1)}, bf16[128,1024]{1,0:T(8,128)(2,1)S(1)}, u32[]{:S(2)}, u32[]{:S(2)}) collective-permute-start(bf16[128,1024]{1,0:T(8,128)(2,1)S(1)} %add_convert_fusion), channel_id=1, source_target_pairs={{4,0},{5,1},{6,2},{7,3},{0,4},{1,5},{2,6},{3,7},{12,8},{13,9},{14,... | collective-permute-start | bytes 786440 | tf_op jit(solution)/shard_map/ppermute | solution.py:42
  136.9 15.1 %collective-permute-start.28 = (bf16[128,1024]{1,0:T(8,128)(2,1)S(1)}, bf16[128,1024]{1,0:T(8,128)(2,1)S(1)}, u32[]{:S(2)}, u32[]{:S(2)}) collective-permute-start(bf16[128,1024]{1,0:T(8,128)(2,1)S(1)} %add_convert_fusion.1), channel_id=1, source_target_pairs={{112,0},{113,1},{114,2},{115,3},{116,4},{117,5},{118,6},{119,7},{1... | collective-permute-start | bytes 786440 | tf_op jit(solution)/shard_map/ppermute | solution.py:42
  138.3 13.6 %collective-permute-start.34 = (bf16[128,1024]{1,0:T(8,128)(2,1)S(1)}, bf16[128,1024]{1,0:T(8,128)(2,1)S(1)}, u32[]{:S(2)}, u32[]{:S(2)}) collective-permute-start(bf16[128,1024]{1,0:T(8,128)(2,1)S(1)} %get-tuple-element.112), channel_id=1, source_target_pairs={{64,0},{65,1},{66,2},{67,3},{68,4},{69,5},{70,6},{71,7},{72,8},{73... | collective-permute-start | bytes 786440 | tf_op jit(solution)/shard_map/ppermute | solution.py:42
  141.1 10.8 %collective-permute-start.33 = (bf16[128,1024]{1,0:T(8,128)(2,1)S(1)}, bf16[128,1024]{1,0:T(8,128)(2,1)S(1)}, u32[]{:S(2)}, u32[]{:S(2)}) collective-permute-start(bf16[128,1024]{1,0:T(8,128)(2,1)S(1)} %get-tuple-element.110), channel_id=1, source_target_pairs={{48,0},{49,1},{50,2},{51,3},{52,4},{53,5},{54,6},{55,7},{56,8},{57... | collective-permute-start | bytes 786440 | tf_op jit(solution)/shard_map/ppermute | solution.py:42
  142.2 9.7 %collective-permute-start.32 = (bf16[128,1024]{1,0:T(8,128)(2,1)S(1)}, bf16[128,1024]{1,0:T(8,128)(2,1)S(1)}, u32[]{:S(2)}, u32[]{:S(2)}) collective-permute-start(bf16[128,1024]{1,0:T(8,128)(2,1)S(1)} %get-tuple-element.108), channel_id=1, source_target_pairs={{30,0},{31,1},{24,2},{25,3},{26,4},{27,5},{28,6},{29,7},{22,8},{23... | collective-permute-start | bytes 786440 | tf_op jit(solution)/shard_map/ppermute | solution.py:42
